TPU v7x, 512 devices: a whole 4x4x16 slice. The times are simulated.
512 devices in a mesh: row: 16 (over y, x_lo, core), col: 32 (over x_hi, z).
Axes of the slice: x: 4 (x_hi: 2, x_lo: 2; x = x_hi * 2 + x_lo), y: 4, z: 16, core: 2. Of those that a mesh axis runs over, the one named last changes fastest.
Arguments:
- left_panel: bfloat16 [16384, 16384], P('row', 'col'), may hold values from -0.125 to 0.125
- right_panel: bfloat16 [16384, 16384], P('row', 'col'), may hold values from -6 to 6
- earlier_terms: bfloat16 [16384, 16384], P('row', 'col'), may hold values from 0 to 1
- density: bfloat16 [16384, 16384], P('row', 'col'), may hold values from -3 to 3
- left_occupied: int32 [32, 32], P('row', 'col'), may hold values from 0 to 1, as said below
- right_occupied: int32 [32, 32], P('row', 'col'), may hold values from 0 to 1, as said below
- kept_tiles: int32 [32, 32], P('row', 'col'), may hold values from 0 to 1, as said below
- branch: int32 [32], P('row'), may hold values from 0 to 1, as said below
Outputs:
- new_density: bfloat16 [16384, 16384], P('row', 'col')
- occupation: float32 [1], replicated
Inputs may be any that keep to these rules, and one draw needn't show every extreme that they name: `left_occupied`: 1 marks an occupied tile, 0 an empty one; of the 2 x 1 tiles of one device's block at most 1 are occupied, and some device's block holds exactly 1. `right_occupied`: 1 marks an occupied tile, 0 an empty one; of the 2 x 1 tiles of one device's block at most 1 are occupied, and some device's block holds exactly 1. `kept_tiles`: 1 marks a tile kept in the new matrix. `branch`: for each tile row, 1 selects X squared, 0 selects 2 X minus X squared; both values occur.
All inputs are finite; a program needn't handle non-finite values.
Results may differ from a plain program's by a relative error of at most 0.001.
Values may be sent and summed in bfloat16 or wider, within the bound.
No kernel may reach another device: no remote copies, remote signals or barrier semaphores. Data moves between devices by JAX's collectives and lax.ppermute only.
A program may use at most 64 MiB of HBM per device.

v0:
```python
import jax
import jax.numpy as jnp
from jax import lax
from jax.sharding import PartitionSpec as P

STEPS = 4


def from_behind(value, axis, steps):
    count = lax.axis_size(axis)
    pairs = [(source, (source + steps) % count) for source in range(count)]
    return lax.ppermute(value, axis, pairs)


def spread(occupied, tile_size):
    row_count, col_count = occupied.shape
    widened = jnp.broadcast_to(
        occupied[:, None, :, None], (row_count, tile_size, col_count, tile_size)
    )
    return widened.reshape(row_count * tile_size, col_count * tile_size)


def local(
    left_panel,
    right_panel,
    earlier_terms,
    density,
    left_occupied,
    right_occupied,
    kept_tiles,
    branch,
):
    block_rows, block_cols = left_panel.shape
    tile_size = block_cols // left_occupied.shape[1]
    left_tiles = left_panel * spread(left_occupied, tile_size).astype(jnp.bfloat16)
    right_tiles = right_panel * spread(right_occupied, tile_size).astype(jnp.bfloat16)
    right_next = from_behind(right_tiles, "row", -1)
    accumulated = earlier_terms.astype(jnp.float32)
    current = left_tiles
    for turn_index in range(STEPS):
        following = from_behind(current, "col", -1) if turn_index + 1 < STEPS else current
        held_block = left_tiles if turn_index == 0 else current
        source = right_tiles if turn_index < 2 else right_next
        first_row = turn_index % 2 * block_cols
        accumulated = accumulated + jnp.dot(
            held_block,
            source[first_row : first_row + block_cols],
            preferred_element_type=jnp.float32,
        )
        current = following
    retained = spread(kept_tiles, tile_size) == 1
    row_flags = (jnp.repeat(branch, tile_size) == 1)[:, None]
    chosen = jnp.where(row_flags, accumulated, 2.0 * density.astype(jnp.float32) - accumulated)
    combined = jnp.where(retained, chosen, jnp.zeros_like(chosen))
    new_density = combined.astype(jnp.bfloat16)
    row_offset = lax.axis_index("row") * block_rows
    col_offset = lax.axis_index("col") * block_cols
    row_numbers = lax.broadcasted_iota(jnp.int32, (block_rows, block_cols), 0) + row_offset
    col_numbers = lax.broadcasted_iota(jnp.int32, (block_rows, block_cols), 1) + col_offset
    on_diagonal = row_numbers == col_numbers
    diagonal_part = jnp.sum(jnp.where(on_diagonal, combined, jnp.zeros_like(combined)))
    matrix_order = lax.axis_size("row") * block_rows
    occupation = lax.psum(diagonal_part, ("row", "col")) / matrix_order
    return (new_density, occupation.reshape(1))


def solution(mesh):
    in_specs = (
        P("row", "col"),
        P("row", "col"),
        P("row", "col"),
        P("row", "col"),
        P("row", "col"),
        P("row", "col"),
        P("row", "col"),
        P("row"),
    )
    out_specs = (P("row", "col"), P())
    return jax.shard_map(local, mesh=mesh, in_specs=in_specs, out_specs=out_specs, check_vma=False)
```

profile of v0, /device:TPU:1, one launch (start us, length us, event | category | flops | bytes accessed | tf_op | source)
XLA Modules:
  0.0 214.2 jit_solution(2194858351292249211)
XLA Ops:
  0.6 0.0 copy-start.3
  0.6 0.0 copy-start.2
  0.7 0.7 convert_bitcast_fusion.1
  1.4 0.1 broadcast_bitcast_fusion.1
  1.5 0.0 copy-start.4
  1.5 0.0 copy-start.5
  1.5 1.5 broadcast_multiply_fusion.1
  2.9 14.4 %collective-permute-start = (bf16[1024,512]{1,0:T(8,128)(2,1)S(1)}, bf16[1024,512]{1,0:T(8,128)(2,1)S(1)}, u32[]{:S(2)}, u32[]{:S(2)}) collective-permute-start(bf16[1024,512]{1,0:T(8,128)(2,1)S(1)} %broadcast_multiply_fusion.1), channel_id=1, source_target_pairs={{0,31},{1,0},{2,1},{3,2},{4,3},{5,4},{6,5},{7,6},{8,7},{9,8},{10,9... | collective-permute-start | bytes 3145736 | tf_op jit(solution)/shard_map/ppermute | solution.py:12
  17.4 0.0 copy-done.3
  17.4 21.8 %collective-permute-done = bf16[1024,512]{1,0:T(8,128)(2,1)S(1)} collective-permute-done((bf16[1024,512]{1,0:T(8,128)(2,1)S(1)}, bf16[1024,512]{1,0:T(8,128)(2,1)S(1)}, u32[]{:S(2)}, u32[]{:S(2)}) %collective-permute-start) | collective-permute-done | bytes 1048608 | tf_op jit(solution)/shard_map/ppermute | solution.py:12
  39.2 7.7 %collective-permute-start.1 = (bf16[1024,512]{1,0:T(8,128)(2,1)S(1)}, bf16[1024,512]{1,0:T(8,128)(2,1)}, u32[]{:S(2)}, u32[]{:S(2)}) collective-permute-start(bf16[1024,512]{1,0:T(8,128)(2,1)S(1)} %collective-permute-done), channel_id=1, source_target_pairs={{0,31},{1,0},{2,1},{3,2},{4,3},{5,4},{6,5},{7,6},{8,7},{9,8},{10,9... | collective-permute-start | bytes 3145736 | tf_op jit(solution)/shard_map/ppermute | solution.py:12
  46.9 0.1 broadcast_bitcast_fusion
  47.0 0.0 copy-done.2
  47.0 0.2 broadcast_multiply_fusion
  47.2 3.7 %collective-permute-start.2 = (bf16[1024,512]{1,0:T(8,128)(2,1)S(1)}, bf16[1024,512]{1,0:T(8,128)(2,1)}, u32[]{:S(2)}, u32[]{:S(2)}) collective-permute-start(bf16[1024,512]{1,0:T(8,128)(2,1)S(1)} %broadcast_multiply_fusion), channel_id=1, source_target_pairs={{0,480},{32,0},{64,32},{96,64},{128,96},{160,128},{192,160},{224,1... | collective-permute-start | bytes 3145736 | tf_op jit(solution)/shard_map/ppermute | solution.py:12
  50.9 0.0 copy-done.4
  51.0 0.1 broadcast_in_dim.36
  51.1 0.0 copy-done.5
  51.1 0.1 broadcast_in_dim.38
  51.2 16.7 %collective-permute-done.1 = bf16[1024,512]{1,0:T(8,128)(2,1)} collective-permute-done((bf16[1024,512]{1,0:T(8,128)(2,1)S(1)}, bf16[1024,512]{1,0:T(8,128)(2,1)}, u32[]{:S(2)}, u32[]{:S(2)}) %collective-permute-start.1) | collective-permute-done | bytes 1048608 | tf_op jit(solution)/shard_map/ppermute | solution.py:12
  67.8 7.8 %collective-permute-start.3 = (bf16[1024,512]{1,0:T(8,128)(2,1)}, bf16[1024,512]{1,0:T(8,128)(2,1)S(1)}, u32[]{:S(2)}, u32[]{:S(2)}) collective-permute-start(bf16[1024,512]{1,0:T(8,128)(2,1)} %collective-permute-done.1), channel_id=1, source_target_pairs={{0,31},{1,0},{2,1},{3,2},{4,3},{5,4},{6,5},{7,6},{8,7},{9,8},{10,9... | collective-permute-start | bytes 3145736 | tf_op jit(solution)/shard_map/ppermute | solution.py:12
  75.7 0.7 fusion.6
  76.4 0.7 fusion.4
  77.1 0.0 copy-start
  77.1 0.0 copy-start.1
  77.1 0.0 collective-permute-done.2
  77.1 2.2 %fusion.2 = f32[1024,512]{1,0:T(8,128)S(1)} fusion(bf16[1024,512]{1,0:T(8,128)(2,1)} %collective-permute-done.1, bf16[1024,512]{1,0:T(8,128)(2,1)} %collective-permute-done.2), kind=kOutput, calls=%fused_computation.4 | convolution fusion | flops 536870912 | bytes 3670016 | tf_op jit(solution)/shard_map/dot_general | solution.py:45
  79.3 16.6 %collective-permute-done.3 = bf16[1024,512]{1,0:T(8,128)(2,1)S(1)} collective-permute-done((bf16[1024,512]{1,0:T(8,128)(2,1)}, bf16[1024,512]{1,0:T(8,128)(2,1)S(1)}, u32[]{:S(2)}, u32[]{:S(2)}) %collective-permute-start.3) | collective-permute-done | bytes 1048608 | tf_op jit(solution)/shard_map/ppermute | solution.py:12
  95.9 0.0 copy-done
  95.9 0.0 copy-done.1
  95.9 4.2 %select_reduce_fusion = (f32[]{:T(128)}, bf16[1024,512]{1,0:T(8,128)(2,1)}) fusion(s32[512]{0:T(512)S(1)} %iota_add_fusion.1, s32[1024]{0:T(1024)S(1)} %iota_add_fusion, bf16[1024,512]{1,0:T(8,128)(2,1)S(1)} %copy-done, bf16[1024,512]{1,0:T(8,128)(2,1)S(1)} %collective-permute-done.3, bf16[1024,512]{1,0:T(8,128)(2,1)} %collective-permute-done.2, ...), kind=kOutput, calls=%fused_computation.2 | convolution fusion | flops 544210944 | bytes 11018244 | tf_op jit(solution)/shard_map/dot_general | solution.py:45
  100.1 112.3 %psum.7 = f32[]{:T(128)} all-reduce(f32[]{:T(128)} %get-tuple-element.2), channel_id=1, replica_groups=mesh['row'=16,'col'=32] {'row','col'}, use_global_device_ids=true, to_apply=%region_1.2 | all-reduce | flops 1 | bytes 8 | tf_op jit(solution)/shard_map/psum | solution.py:63
  (9 shorter events, 0.1 us)
Async XLA Ops:
  0.6 16.7 %copy-start.3 = (s32[2,1]{0,1:T(1,128)S(1)}, s32[2,1]{0,1:T(1,128)}, u32[]{:S(2)}) copy-start(s32[2,1]{0,1:T(1,128)} %param.13) | copy-start | bytes 28
  0.6 46.3 %copy-start.2 = (bf16[1024,512]{1,0:T(8,128)(2,1)S(1)}, bf16[1024,512]{1,0:T(8,128)(2,1)}, u32[]{:S(2)}) copy-start(bf16[1024,512]{1,0:T(8,128)(2,1)} %param.9) | copy-start | bytes 3145732
  1.5 49.5 %copy-start.4 = (s32[2,1]{0,1:T(1,128)S(1)}, s32[2,1]{0,1:T(1,128)}, u32[]{:S(2)}) copy-start(s32[2,1]{0,1:T(1,128)} %param.14) | copy-start | bytes 28
  1.5 49.6 %copy-start.5 = (s32[2]{0:T(128)S(1)}, s32[2]{0:T(128)}, u32[]{:S(2)}) copy-start(s32[2]{0:T(128)} %param.15) | copy-start | bytes 28
  2.9 36.2 %collective-permute-start = (bf16[1024,512]{1,0:T(8,128)(2,1)S(1)}, bf16[1024,512]{1,0:T(8,128)(2,1)S(1)}, u32[]{:S(2)}, u32[]{:S(2)}) collective-permute-start(bf16[1024,512]{1,0:T(8,128)(2,1)S(1)} %broadcast_multiply_fusion.1), channel_id=1, source_target_pairs={{0,31},{1,0},{2,1},{3,2},{4,3},{5,4},{6,5},{7,6},{8,7},{9,8},{10,9... | collective-permute-start | bytes 3145736 | tf_op jit(solution)/shard_map/ppermute | solution.py:12
  39.2 28.6 %collective-permute-start.1 = (bf16[1024,512]{1,0:T(8,128)(2,1)S(1)}, bf16[1024,512]{1,0:T(8,128)(2,1)}, u32[]{:S(2)}, u32[]{:S(2)}) collective-permute-start(bf16[1024,512]{1,0:T(8,128)(2,1)S(1)} %collective-permute-done), channel_id=1, source_target_pairs={{0,31},{1,0},{2,1},{3,2},{4,3},{5,4},{6,5},{7,6},{8,7},{9,8},{10,9... | collective-permute-start | bytes 3145736 | tf_op jit(solution)/shard_map/ppermute | solution.py:12
  47.2 29.9 %collective-permute-start.2 = (bf16[1024,512]{1,0:T(8,128)(2,1)S(1)}, bf16[1024,512]{1,0:T(8,128)(2,1)}, u32[]{:S(2)}, u32[]{:S(2)}) collective-permute-start(bf16[1024,512]{1,0:T(8,128)(2,1)S(1)} %broadcast_multiply_fusion), channel_id=1, source_target_pairs={{0,480},{32,0},{64,32},{96,64},{128,96},{160,128},{192,160},{224,1... | collective-permute-start | bytes 3145736 | tf_op jit(solution)/shard_map/ppermute | solution.py:12
  67.8 28.1 %collective-permute-start.3 = (bf16[1024,512]{1,0:T(8,128)(2,1)}, bf16[1024,512]{1,0:T(8,128)(2,1)S(1)}, u32[]{:S(2)}, u32[]{:S(2)}) collective-permute-start(bf16[1024,512]{1,0:T(8,128)(2,1)} %collective-permute-done.1), channel_id=1, source_target_pairs={{0,31},{1,0},{2,1},{3,2},{4,3},{5,4},{6,5},{7,6},{8,7},{9,8},{10,9... | collective-permute-start | bytes 3145736 | tf_op jit(solution)/shard_map/ppermute | solution.py:12
  77.1 18.9 %copy-start = (bf16[1024,512]{1,0:T(8,128)(2,1)S(1)}, bf16[1024,512]{1,0:T(8,128)(2,1)}, u32[]{:S(2)}) copy-start(bf16[1024,512]{1,0:T(8,128)(2,1)} %param.11) | copy-start | bytes 3145732
  77.1 18.9 %copy-start.1 = (bf16[1024,512]{1,0:T(8,128)(2,1)S(1)}, bf16[1024,512]{1,0:T(8,128)(2,1)}, u32[]{:S(2)}) copy-start(bf16[1024,512]{1,0:T(8,128)(2,1)} %param.10) | copy-start | bytes 3145732
where the time goes:
time: 215 us; the launch traced here: 214 us
  blocking collectives  112 us (52%)
  waiting for transfers between devices  55.1 us (26%)
  starting transfers between devices  33.7 us (16%)
  matrix products  7.81 us (4%)
  between operations  2.56 us (1%)
  other arithmetic  2.43 us (1%)
    psum x1, blocking collectives, local(): occupation = lax.psum(diagonal_part, ('row', 'col')) / matrix_order  112 us
    ppermute x4, waiting for transfers between devices, from_behind(): return lax.ppermute(value, axis, pairs)  55.1 us
    ppermute x4, starting transfers between devices, from_behind(): return lax.ppermute(value, axis, pairs)  33.7 us
    dot_general x4, matrix products, local(): jnp.dot(held_block, source[first_row:first_row + block_cols], preferred_e...  7.81 us
  transfers between devices with their start and end apart: 4, of which 3 were waited for; matrix products, arithmetic and copies ran while one was open for 2% of the time, Pallas kernels for 0%

commit v1 on v0

v1 whole, which is shorter than its diff:
```python
import jax
import jax.numpy as jnp
from jax import lax
from jax.experimental import pallas as pl
from jax.experimental.pallas import tpu as pltpu
from jax.sharding import PartitionSpec as P

FLAG_ROWS = 16
LANES = 128

VMEM = pl.BlockSpec(memory_space=pltpu.VMEM)
SMEM = pl.BlockSpec(memory_space=pltpu.SMEM)
ANY = pl.BlockSpec(memory_space=pl.ANY)


def shift(value, axis, steps):
    count = lax.axis_size(axis)
    return lax.ppermute(value, axis, [(src, (src + steps) % count) for src in range(count)])


def pack(panel, occupied):
    tile_size = panel.shape[1]
    flags = occupied[:, 0].astype(jnp.bfloat16)
    tile = lax.dynamic_slice_in_dim(panel, occupied[1, 0] * tile_size, tile_size, 0)
    lanes = lax.broadcasted_iota(jnp.int32, (FLAG_ROWS, tile_size), 1)
    tail = jnp.where(lanes < tile_size // 2, flags[0], flags[1])
    return jnp.concatenate([tile, tail], axis=0)


def flag_pair(payload):
    size = payload.shape[1]
    tail = payload[size:, :].astype(jnp.float32)
    return tail[0:1, 0:1], tail[0:1, size // 2 : size // 2 + 1]


def dot(a, b):
    return jnp.dot(a, b, preferred_element_type=jnp.float32)


def diagonal(block):
    rows = lax.broadcasted_iota(jnp.int32, block.shape, 0)
    cols = lax.broadcasted_iota(jnp.int32, block.shape, 1)
    return jnp.sum(jnp.where(rows == cols, block, 0.0), axis=(0, 1), keepdims=True)


def product_trace(left, right, size):
    total = jnp.zeros((1, 1), jnp.float32)
    for start in range(0, size, LANES):
        part = pl.ds(start, LANES)
        total = total + diagonal(dot(left(part), right[:size, part]))
    return total


def trace_kernel(
    place, right_occupied, kept, branch, own, one, chosen, right_own, right_trace, earlier, density,
    parts, earlier_tile, density_tile, sems,
):
    size = own.shape[1]
    half = lax.rem(place[1], 2)
    near_mine = lax.div(place[1], 2) == place[0]
    far_mine = lax.div(place[2], 2) == place[0]
    lanes = lax.broadcasted_iota(jnp.int32, parts.shape, 1)
    parts[...] = jnp.zeros_like(parts)

    @pl.when(near_mine)
    def _near():
        rows = pl.ds(pl.multiple_of(half * size, size), size)
        copies = [
            pltpu.make_async_copy(earlier.at[rows], earlier_tile, sems.at[0]),
            pltpu.make_async_copy(density.at[rows], density_tile, sems.at[1]),
        ]
        for copy in copies:
            copy.start()
        second = right_occupied[1, 0] == 1
        value = product_trace(lambda part: jnp.where(second, one[part, :], own[part, :]), right_own, size)
        flags = [jnp.where(second, a, b) for a, b in zip(flag_pair(one), flag_pair(own))]
        occupied = (right_occupied[0, 0] + right_occupied[1, 0]).astype(jnp.float32)
        value = value * jnp.where(half == 1, flags[1], flags[0]) * occupied
        for copy in copies:
            copy.wait()
        base = jnp.zeros((1, 1), jnp.float32)
        twice = jnp.zeros((1, 1), jnp.float32)
        for start in range(0, size, LANES):
            part = pl.ds(start, LANES)
            base = base + diagonal(earlier_tile[part, part].astype(jnp.float32))
            twice = twice + diagonal(2.0 * density_tile[part, part].astype(jnp.float32))
        squared = branch[half] == 1
        value = jnp.where(squared, base + value, twice - base - value)
        keep = (kept[half, 0] == 1).astype(jnp.float32)
        weight = jnp.where(squared, keep, -keep)
        parts[...] += jnp.where(lanes == 0, value * keep, 0.0) + jnp.where(lanes == 2, weight, 0.0)

    @pl.when(far_mine)
    def _far():
        value = product_trace(lambda part: chosen[part, :], right_trace, size)
        flags, right_flags = flag_pair(chosen), flag_pair(right_trace)
        value = value * jnp.where(half == 1, flags[1], flags[0]) * (right_flags[0] + right_flags[1])
        parts[...] += jnp.where(lanes == 1, value, 0.0)


def middle_kernel(parts, spread):
    spread[...] = jnp.broadcast_to(jnp.sum(parts[...], axis=0, keepdims=True), spread.shape)


def total_kernel(parts, total):
    values = parts[...]
    lanes = lax.broadcasted_iota(jnp.int32, values.shape, 1)
    moved = jnp.concatenate([values[-2:], values[:-2]], axis=0)
    weights = jnp.sum(jnp.where(lanes == 2, moved, 0.0), axis=1, keepdims=True)
    far = jnp.sum(jnp.where(lanes == 1, values, 0.0), axis=1, keepdims=True)
    near = jnp.sum(jnp.where(lanes == 0, values, 0.0), axis=1, keepdims=True)
    total[...] = jnp.broadcast_to(jnp.sum(near + weights * far, axis=0, keepdims=True), total.shape)


def last_kernel(
    right_occupied, kept, branch, own, one, right_own, two, right_next, earlier, density, after, out,
):
    size = own.shape[1]
    second = right_occupied[1, 0] == 1
    occupied = (right_occupied[0, 0] + right_occupied[1, 0]).astype(jnp.float32)
    first_flags = [jnp.where(second, a, b) * occupied for a, b in zip(flag_pair(one), flag_pair(own))]
    right_flags = flag_pair(right_next)
    last_flags = [flag * (right_flags[0] + right_flags[1]) for flag in flag_pair(two)]
    step = size // 4
    for start in range(0, size, step):
        part = pl.ds(start, step)
        first = dot(jnp.where(second, one[part, :], own[part, :]), right_own[:size, :])
        last = dot(two[part, :], right_next[:size, :])
        for half in range(2):
            rows = pl.ds(half * size + start, step)
            product = earlier[rows, :].astype(jnp.float32) + first_flags[half] * first + last_flags[half] * last
            other = 2.0 * density[rows, :].astype(jnp.float32) - product
            value = jnp.where(branch[half] == 1, product, other)
            value = jnp.where(kept[half, 0] == 1, value, 0.0)
            out[rows, :] = value.astype(out.dtype)


def spread_over(rows, axis):
    return lax.all_to_all(rows, axis, 0, 0, tiled=True)


def local(left_panel, right_panel, earlier, density, left_occupied, right_occupied, kept_tiles, branch):
    block_rows, size = left_panel.shape
    row_count, col_count = lax.axis_size("row"), lax.axis_size("col")
    me_row, me_col = lax.axis_index("row"), lax.axis_index("col")
    both = ("row", "col")

    left_own = pack(left_panel, left_occupied)
    left_one = shift(left_own, "col", -1)

    right_own = pack(right_panel, right_occupied)
    to_trace = [
        (((j // 2 + 1) % row_count) * col_count + j, (j // 2) * col_count + (j + 2) % col_count)
        for j in range(col_count)
    ]
    right_trace = lax.ppermute(right_own, both, to_trace)

    to_wanted = [
        (((i + 1) % row_count) * col_count + j, i * col_count + (j + 2) % col_count)
        for i in range(row_count)
        for j in range(col_count)
    ]
    wanted = lax.ppermute(jnp.broadcast_to(right_occupied[1, 0], (8, LANES)), both, to_wanted)
    right_next = shift(right_own, "row", -1)

    chosen = jnp.where(wanted[0, 0] == 1, left_one, left_own)
    left_two = shift(chosen, "col", -2)

    place = jnp.stack([me_row, me_col, (me_col + col_count - 2) % col_count])
    parts = pl.pallas_call(
        trace_kernel,
        out_shape=jax.ShapeDtypeStruct((row_count, LANES), jnp.float32),
        in_specs=[SMEM] * 4 + [VMEM] * 5 + [ANY] * 2,
        out_specs=VMEM,
        scratch_shapes=[
            pltpu.VMEM((size, size), earlier.dtype),
            pltpu.VMEM((size, size), density.dtype),
            pltpu.SemaphoreType.DMA((2,)),
        ],
        compiler_params=pltpu.CompilerParams(vmem_limit_bytes=16 * 2**20),
        name="trace",
    )(place, right_occupied, kept_tiles, branch, left_own, left_one, chosen, right_own, right_trace, earlier, density)
    parts = spread_over(parts, "row")
    parts = pl.pallas_call(
        middle_kernel,
        out_shape=jax.ShapeDtypeStruct((col_count, LANES), jnp.float32),
        in_specs=[VMEM],
        out_specs=VMEM,
        name="middle",
    )(parts)
    parts = spread_over(parts, "col")
    total = pl.pallas_call(
        total_kernel,
        out_shape=jax.ShapeDtypeStruct((8, LANES), jnp.float32),
        in_specs=[VMEM],
        out_specs=VMEM,
        name="total",
    )(parts)
    occupation = total[0, :1] / (row_count * block_rows)

    new_density = pl.pallas_call(
        last_kernel,
        out_shape=jax.ShapeDtypeStruct((block_rows, size), jnp.bfloat16),
        in_specs=[SMEM] * 3 + [VMEM] * 7 + [ANY],
        out_specs=VMEM,
        compiler_params=pltpu.CompilerParams(vmem_limit_bytes=16 * 2**20),
        name="last",
    )(right_occupied, kept_tiles, branch, left_own, left_one, right_own, left_two, right_next, earlier, density, total)
    return new_density, occupation


def solution(mesh):
    whole = P("row", "col")
    in_specs = (whole,) * 7 + (P("row"),)
    return jax.shard_map(local, mesh=mesh, in_specs=in_specs, out_specs=(whole, P()), check_vma=False)
```

time: 215 us -> 96.1 us (0.45)
  blocking collectives: 112 us -> 37.4 us
  waiting for transfers between devices: 55.1 us -> 0.01 us
  local copies, waits for them, and re-layouts: 0.38 us -> 11.5 us
  matrix products: 7.81 us -> 0 us
  Pallas kernels: 0 us -> 7.04 us
  starting transfers between devices: 33.7 us -> 31 us
    psum x1 -> x0, blocking collectives: 112 us -> none  [local(): occupation = lax.psum(diagonal_part, ('row', 'col')) / matrix_order]
    ppermute x4 -> x5, waiting for transfers between devices: 55.1 us -> 0.01 us  [the longest x3 0.01 us: shift(): lax.ppermute(value, axis, [(src, (src + steps) % count) for src in range(...]
    all_to_all x0 -> x2, blocking collectives: none -> 37.4 us  [spread_over(): return lax.all_to_all(rows, axis, 0, 0, tiled=True)]
    dot_general x4 -> x0, matrix products: 7.81 us -> none  [local(): jnp.dot(held_block, source[first_row:first_row + block_cols], preferred_e...]
    pallas_call x0 -> x4, Pallas kernels: none -> 7.04 us  [the longest x1 3.23 us: local(): pl.pallas_call(last_kernel, out_shape=jax.ShapeDtypeStruct((block_rows, s...]
    unnamed x16 -> x26, local copies, waits for them, and re-layouts: 0.19 us -> 5.81 us
    slice x0 -> x6, local copies, waits for them, and re-layouts: none -> 4.94 us  [the longest x2 1.91 us: pack(): occupied[1, 0] * tile_size]
    select_n x0 -> x3, other arithmetic: none -> 2.95 us  [the longest x2 2.81 us: pack(): tail = jnp.where(lanes < tile_size // 2, flags[0], flags[1])]
  transfers between devices with their start and end apart: 4 -> 5, of which waited for: 3 -> 0; matrix products, arithmetic and copies ran while one was open for 2% -> 6% of each run, Pallas kernels for 0% -> 4%
where the time goes in v1:
time: 96.1 us; the launch traced here: 95.3 us
  blocking collectives  37.4 us (39%)
  starting transfers between devices  31 us (32%)
  local copies, waits for them, and re-layouts  11.5 us (12%)
  Pallas kernels  7.04 us (7%)
  between operations  4.63 us (5%)
  other arithmetic  3.76 us (4%)
    all_to_all x2, blocking collectives, spread_over(): return lax.all_to_all(rows, axis, 0, 0, tiled=True)  37.4 us
    ppermute x3, starting transfers between devices, shift(): lax.ppermute(value, axis, [(src, (src + steps) % count) for src in range(...  26.8 us
    unnamed x26, local copies, waits for them, and re-layouts  5.81 us
    pallas_call x1, Pallas kernels, local(): pl.pallas_call(last_kernel, out_shape=jax.ShapeDtypeStruct((block_rows, s...  3.23 us
    select_n x2, other arithmetic, pack(): tail = jnp.where(lanes < tile_size // 2, flags[0], flags[1])  2.81 us
    ppermute x1, starting transfers between devices, local(): right_trace = lax.ppermute(right_own, both, to_trace)  2.24 us
  transfers between devices with their start and end apart: 5, of which 0 were waited for; matrix products, arithmetic and copies ran while one was open for 6% of the time, Pallas kernels for 4%

profile of v1, /device:TPU:1, one launch (start us, length us, event | category | flops | bytes accessed | tf_op | source)
XLA Modules:
  0.0 95.3 jit_solution(17776893064208539074)
XLA Ops:
  0.6 0.0 copy-start
  0.6 1.3 %slice.29 = s32[1,1]{0,1:T(1,128)} slice(s32[2,1]{0,1:T(1,128)} %param.12), slice={[1:2], [0:1]} | slice | bytes 8 | tf_op jit(solution)/shard_map/slice | solution.py:24
  2.0 0.7 convert_element_type.8
  3.3 0.7 fusion.3
  3.9 0.0 copy-done
  3.9 0.0 copy-start.10
  3.9 0.0 copy-start.9
  4.0 0.0 copy-start.7
  4.0 1.5 %fusion.1 = bf16[512]{0:T(512)(128)(2,1)S(1)} fusion(bf16[]{:T(256)} %bitcast.2, bf16[]{:T(256)} %bitcast.1), kind=kLoop, calls=%fused_computation.5 | loop fusion | flops 1024 | bytes 1028 | tf_op jit(solution)/shard_map/jit(_where)/select_n | solution.py:26
  5.5 0.0 copy-done.7
  5.5 14.4 %collective-permute-start = (bf16[528,512]{1,0:T(8,128)(2,1)S(1)}, bf16[528,512]{1,0:T(8,128)(2,1)S(1)}, u32[]{:S(2)}, u32[]{:S(2)}) collective-permute-start(bf16[528,512]{1,0:T(8,128)(2,1)S(1)} %pad_maximum_fusion.own), channel_id=1, source_target_pairs={{0,31},{1,0},{2,1},{3,2},{4,3},{5,4},{6,5},{7,6},{8,7},{9,8},{10,9... | collective-permute-start | bytes 1622024 | tf_op jit(solution)/shard_map/ppermute | solution.py:18
  20.0 0.0 copy-done.10
  20.0 0.6 slice.32
  20.6 0.6 broadcast_in_dim.21
  21.2 1.9 %collective-permute-start.1 = (s32[8,128]{1,0:T(8,128)S(1)}, s32[8,128]{1,0:T(8,128)S(1)}, u32[]{:S(2)}, u32[]{:S(2)}) collective-permute-start(s32[8,128]{1,0:T(8,128)S(1)} %broadcast_in_dim.21), channel_id=1, source_target_pairs={{32,2},{33,3},{34,4},{35,5},{36,6},{37,7},{38,8},{39,9},{40,10},{4... | collective-permute-start | bytes 12296 | tf_op jit(solution)/shard_map/ppermute | solution.py:163
  23.8 0.7 fusion.2
  24.5 1.3 %fusion = bf16[512]{0:T(512)(128)(2,1)S(1)} fusion(bf16[]{:T(256)} %bitcast.5, bf16[]{:T(256)} %bitcast.4), kind=kLoop, calls=%fused_computation.4 | loop fusion | flops 1024 | bytes 1028 | tf_op jit(solution)/shard_map/jit(_where)/select_n | solution.py:26
  25.8 0.0 copy-done.9
  25.8 0.0 copy-start.8
  25.9 0.0 copy-start.11
  26.0 0.0 copy-start.6
  26.0 2.2 %collective-permute-start.4 = (bf16[528,512]{1,0:T(8,128)(2,1)S(1)}, bf16[528,512]{1,0:T(8,128)(2,1)}, u32[]{:S(2)}, u32[]{:S(2)}) collective-permute-start(bf16[528,512]{1,0:T(8,128)(2,1)S(1)} %pad_maximum_fusion.1.right_own), channel_id=1, source_target_pairs={{32,2},{33,3},{66,36},{67,37},{100,70},{101,71},{134,104},{135,105... | collective-permute-start | bytes 1622024 | tf_op jit(solution)/shard_map/ppermute | solution.py:156
  28.2 2.2 %collective-permute-start.3 = (bf16[528,512]{1,0:T(8,128)(2,1)S(1)}, bf16[528,512]{1,0:T(8,128)(2,1)}, u32[]{:S(2)}, u32[]{:S(2)}) collective-permute-start(bf16[528,512]{1,0:T(8,128)(2,1)S(1)} %pad_maximum_fusion.1.right_own), channel_id=1, source_target_pairs={{0,480},{32,0},{64,32},{96,64},{128,96},{160,128},{192,160},{224,1... | collective-permute-start | bytes 1622024 | tf_op jit(solution)/shard_map/ppermute | solution.py:18
  30.4 0.0 collective-permute-done.1
  30.5 0.5 slice.35
  31.6 0.0 collective-permute-done.one
  31.6 0.0 copy-done.8
  31.6 0.1 broadcast_select_fusion.chosen
  31.8 10.2 %collective-permute-start.2 = (bf16[528,512]{1,0:T(8,128)(2,1)S(1)}, bf16[528,512]{1,0:T(8,128)(2,1)}, u32[]{:S(2)}, u32[]{:S(2)}) collective-permute-start(bf16[528,512]{1,0:T(8,128)(2,1)S(1)} %broadcast_select_fusion.chosen), channel_id=1, source_target_pairs={{0,30},{1,31},{2,0},{3,1},{4,2},{5,3},{6,4},{7,5},{8,6},{9,7},{10,... | collective-permute-start | bytes 1622024 | tf_op jit(solution)/shard_map/ppermute | solution.py:18
  42.0 0.1 copy.18.right_occupied
  42.1 0.0 copy-done.11
  42.1 0.1 copy.19.kept
  42.1 0.1 pad_add_fusion.place
  42.2 0.0 collective-permute-done.4.right_trace
  42.2 0.0 copy-done.6
  42.2 0.0 copy-start.1
  42.2 1.2 %copy-done.1 = bf16[1024,512]{1,0:T(8,128)(2,1)S(1)} copy-done((bf16[1024,512]{1,0:T(8,128)(2,1)S(1)}, bf16[1024,512]{1,0:T(8,128)(2,1)}, u32[]{:S(2)}) %copy-start.1) | copy-done | bytes 1048600
  43.5 0.0 copy-start.3
  43.5 1.2 %copy-done.3 = bf16[1024,512]{1,0:T(8,128)(2,1)S(1)} copy-done((bf16[1024,512]{1,0:T(8,128)(2,1)S(1)}, bf16[1024,512]{1,0:T(8,128)(2,1)}, u32[]{:S(2)}) %copy-start.3) | copy-done | bytes 1048600
  44.7 1.1 %trace.1 = f32[16,128]{1,0:T(8,128)S(1)} custom-call(s32[3]{0:T(128)S(1)} %pad_add_fusion.place, s32[2,1]{1,0:T(2,128)S(1)} %copy.18.right_occupied, s32[2,1]{1,0:T(2,128)S(1)} %copy.19.kept, s32[2]{0:T(128)S(1)} %copy-done.6, bf16[528,512]{1,0:T(8,128)(2,1)S(1)} %pad_maximum_fusion.own, bf16[528,512]{1,0:T(8,128)(2,1)S(1)} %collective-permute-done.one, ...), custom_call_target="tpu_custom_call" | custom-call | tf_op jit(solution)/shard_map/trace/pallas_call | solution.py:170
  45.8 14.1 %all_to_all.22 = f32[16,1,128]{2,1,0:T(1,128)} all-to-all(f32[16,1,128]{2,1,0:T(1,128)S(1)} %bitcast.19), channel_id=1, replica_groups=mesh['row'=16,'col'=32] {'row'}, dimensions={0} | all-to-all | bytes 16384 | tf_op jit(solution)/shard_map/all_to_all | solution.py:139
  59.9 1.3 %middle.1 = f32[32,128]{1,0:T(8,128)} custom-call(f32[16,128]{1,0:T(8,128)} %bitcast.22), custom_call_target="tpu_custom_call" | custom-call | tf_op jit(solution)/shard_map/middle/pallas_call | solution.py:184
  61.2 23.3 %all_to_all.23 = f32[32,1,128]{2,1,0:T(1,128)} all-to-all(f32[32,1,128]{2,1,0:T(1,128)} %bitcast.21), channel_id=1, replica_groups=mesh['row'=16,'col'=32] {'col'}, dimensions={0} | all-to-all | bytes 32768 | tf_op jit(solution)/shard_map/all_to_all | solution.py:139
  84.5 1.4 %total.1.after = f32[8,128]{1,0:T(8,128)} custom-call(f32[32,128]{1,0:T(8,128)} %bitcast.20), custom_call_target="tpu_custom_call" | custom-call | tf_op jit(solution)/shard_map/total/pallas_call | solution.py:192
  85.9 1.2 %slice.36 = f32[1,1]{1,0:T(1,128)} slice(f32[8,128]{1,0:T(8,128)} %total.1.after), slice={[0:1], [0:1]} | slice | bytes 8 | tf_op jit(solution)/shard_map/slice | solution.py:199
  87.8 0.0 collective-permute-done.3.right_next
  87.8 0.0 collective-permute-done.2.two
  87.8 0.0 copy-start.2
  87.8 1.2 %copy-done.2 = bf16[1024,512]{1,0:T(8,128)(2,1)S(1)} copy-done((bf16[1024,512]{1,0:T(8,128)(2,1)S(1)}, bf16[1024,512]{1,0:T(8,128)(2,1)}, u32[]{:S(2)}) %copy-start.2) | copy-done | bytes 1048600
  89.0 0.0 copy-start.4
  89.0 1.2 %copy-done.4 = bf16[1024,512]{1,0:T(8,128)(2,1)S(1)} copy-done((bf16[1024,512]{1,0:T(8,128)(2,1)S(1)}, bf16[1024,512]{1,0:T(8,128)(2,1)}, u32[]{:S(2)}) %copy-start.4) | copy-done | bytes 1048600
  90.2 0.0 copy-start.5
  90.2 0.7 copy-done.5
  90.9 3.2 %last.1 = bf16[1024,512]{1,0:T(8,128)(2,1)} custom-call(s32[2,1]{1,0:T(2,128)S(1)} %copy.18.right_occupied, s32[2,1]{1,0:T(2,128)S(1)} %copy.19.kept, s32[2]{0:T(128)S(1)} %copy-done.6, bf16[528,512]{1,0:T(8,128)(2,1)S(1)} %pad_maximum_fusion.own, bf16[528,512]{1,0:T(8,128)(2,1)S(1)} %collective-permute-done.one, ...), custom_call_target="tpu_custom_call" | custom-call | tf_op jit(solution)/shard_map/last/pallas_call | solution.py:201
  (7 shorter events, 0.2 us)
Async XLA Ops:
  0.6 3.3 %copy-start = (bf16[1024,512]{1,0:T(8,128)(2,1)S(1)}, bf16[1024,512]{1,0:T(8,128)(2,1)}, u32[]{:S(2)}) copy-start(bf16[1024,512]{1,0:T(8,128)(2,1)} %param.8) | copy-start | bytes 3145732
  3.9 16.0 %copy-start.10 = (s32[2,1]{0,1:T(1,128)S(1)}, s32[2,1]{0,1:T(1,128)}, u32[]{:S(2)}) copy-start(s32[2,1]{0,1:T(1,128)} %param.13) | copy-start | bytes 28
  3.9 21.9 %copy-start.9 = (bf16[1024,512]{1,0:T(8,128)(2,1)S(1)}, bf16[1024,512]{1,0:T(8,128)(2,1)}, u32[]{:S(2)}) copy-start(bf16[1024,512]{1,0:T(8,128)(2,1)} %param.9) | copy-start | bytes 3145732
  4.0 1.5 %copy-start.7 = (bf16[512,512]{1,0:T(8,128)(2,1)}, bf16[512,512]{1,0:T(8,128)(2,1)S(1)}, u32[]{:S(2)}) copy-start(bf16[512,512]{1,0:T(8,128)(2,1)S(1)} %constant_dynamic-slice_fusion.1) | copy-start | bytes 1572868
  5.5 26.1 %collective-permute-start = (bf16[528,512]{1,0:T(8,128)(2,1)S(1)}, bf16[528,512]{1,0:T(8,128)(2,1)S(1)}, u32[]{:S(2)}, u32[]{:S(2)}) collective-permute-start(bf16[528,512]{1,0:T(8,128)(2,1)S(1)} %pad_maximum_fusion.own), channel_id=1, source_target_pairs={{0,31},{1,0},{2,1},{3,2},{4,3},{5,4},{6,5},{7,6},{8,7},{9,8},{10,9... | collective-permute-start | bytes 1622024 | tf_op jit(solution)/shard_map/ppermute | solution.py:18
  21.2 9.2 %collective-permute-start.1 = (s32[8,128]{1,0:T(8,128)S(1)}, s32[8,128]{1,0:T(8,128)S(1)}, u32[]{:S(2)}, u32[]{:S(2)}) collective-permute-start(s32[8,128]{1,0:T(8,128)S(1)} %broadcast_in_dim.21), channel_id=1, source_target_pairs={{32,2},{33,3},{34,4},{35,5},{36,6},{37,7},{38,8},{39,9},{40,10},{4... | collective-permute-start | bytes 12296 | tf_op jit(solution)/shard_map/ppermute | solution.py:163
  25.8 5.8 %copy-start.8 = (bf16[512,512]{1,0:T(8,128)(2,1)S(1)}, bf16[512,512]{1,0:T(8,128)(2,1)}, u32[]{:S(2)}) copy-start(bf16[512,512]{1,0:T(8,128)(2,1)} %copy-done.7) | copy-start | bytes 1572868
  25.9 16.1 %copy-start.11 = (s32[2,1]{0,1:T(1,128)S(1)}, s32[2,1]{0,1:T(1,128)}, u32[]{:S(2)}) copy-start(s32[2,1]{0,1:T(1,128)} %param.14) | copy-start | bytes 28
  26.0 16.3 %copy-start.6 = (s32[2]{0:T(128)S(1)}, s32[2]{0:T(128)}, u32[]{:S(2)}) copy-start(s32[2]{0:T(128)} %branch.3) | copy-start | bytes 28
  26.0 16.3 %collective-permute-start.4 = (bf16[528,512]{1,0:T(8,128)(2,1)S(1)}, bf16[528,512]{1,0:T(8,128)(2,1)}, u32[]{:S(2)}, u32[]{:S(2)}) collective-permute-start(bf16[528,512]{1,0:T(8,128)(2,1)S(1)} %pad_maximum_fusion.1.right_own), channel_id=1, source_target_pairs={{32,2},{33,3},{66,36},{67,37},{100,70},{101,71},{134,104},{135,105... | collective-permute-start | bytes 1622024 | tf_op jit(solution)/shard_map/ppermute | solution.py:156
  28.2 59.6 %collective-permute-start.3 = (bf16[528,512]{1,0:T(8,128)(2,1)S(1)}, bf16[528,512]{1,0:T(8,128)(2,1)}, u32[]{:S(2)}, u32[]{:S(2)}) collective-permute-start(bf16[528,512]{1,0:T(8,128)(2,1)S(1)} %pad_maximum_fusion.1.right_own), channel_id=1, source_target_pairs={{0,480},{32,0},{64,32},{96,64},{128,96},{160,128},{192,160},{224,1... | collective-permute-start | bytes 1622024 | tf_op jit(solution)/shard_map/ppermute | solution.py:18
  31.8 56.0 %collective-permute-start.2 = (bf16[528,512]{1,0:T(8,128)(2,1)S(1)}, bf16[528,512]{1,0:T(8,128)(2,1)}, u32[]{:S(2)}, u32[]{:S(2)}) collective-permute-start(bf16[528,512]{1,0:T(8,128)(2,1)S(1)} %broadcast_select_fusion.chosen), channel_id=1, source_target_pairs={{0,30},{1,31},{2,0},{3,1},{4,2},{5,3},{6,4},{7,5},{8,6},{9,7},{10,... | collective-permute-start | bytes 1622024 | tf_op jit(solution)/shard_map/ppermute | solution.py:18
  42.2 1.2 %copy-start.1 = (bf16[1024,512]{1,0:T(8,128)(2,1)S(1)}, bf16[1024,512]{1,0:T(8,128)(2,1)}, u32[]{:S(2)}) copy-start(bf16[1024,512]{1,0:T(8,128)(2,1)} %earlier.3) | copy-start | bytes 3145732
  43.5 1.2 %copy-start.3 = (bf16[1024,512]{1,0:T(8,128)(2,1)S(1)}, bf16[1024,512]{1,0:T(8,128)(2,1)}, u32[]{:S(2)}) copy-start(bf16[1024,512]{1,0:T(8,128)(2,1)} %density.3) | copy-start | bytes 3145732
  87.8 1.2 %copy-start.2 = (bf16[1024,512]{1,0:T(8,128)(2,1)S(1)}, bf16[1024,512]{1,0:T(8,128)(2,1)}, u32[]{:S(2)}) copy-start(bf16[1024,512]{1,0:T(8,128)(2,1)} %earlier.3) | copy-start | bytes 3145732
  89.0 1.2 %copy-start.4 = (bf16[1024,512]{1,0:T(8,128)(2,1)S(1)}, bf16[1024,512]{1,0:T(8,128)(2,1)}, u32[]{:S(2)}) copy-start(bf16[1024,512]{1,0:T(8,128)(2,1)} %density.3) | copy-start | bytes 3145732
  90.2 0.7 copy-start.5

commit v2 on v1

v2 whole, which is shorter than its diff:
```python
import functools

import jax
import jax.numpy as jnp
from jax import lax
from jax.experimental import pallas as pl
from jax.experimental.pallas import tpu as pltpu
from jax.sharding import PartitionSpec as P

FLAG_ROWS = 16
LANES = 128
LEFT_LIMIT = 62 * 2**20

VMEM = pl.BlockSpec(memory_space=pltpu.VMEM)
SMEM = pl.BlockSpec(memory_space=pltpu.SMEM)
HBM = pl.BlockSpec(memory_space=pltpu.HBM)


def call(kernel, name, ins, outs, out_specs, scratch=(), limit=12 * 2**20):
    return pl.pallas_call(
        kernel,
        out_shape=outs,
        in_specs=[spec for _, spec in ins],
        out_specs=out_specs,
        scratch_shapes=list(scratch),
        compiler_params=pltpu.CompilerParams(vmem_limit_bytes=limit),
        name=name,
    )(*[array for array, _ in ins])


def shift(value, axis, steps):
    count = lax.axis_size(axis)
    return lax.ppermute(value, axis, [(src, (src + steps) % count) for src in range(count)])


def pack_tile(occupied, panel, packed, tail, sems):
    size = panel.shape[1]
    rows = pl.ds(pl.multiple_of(occupied[1] * size, size), size)
    tile = pltpu.make_async_copy(panel.at[rows], packed.at[:size], sems.at[0])
    tile.start()
    lanes = lax.broadcasted_iota(jnp.int32, tail.shape, 1)
    flags = [occupied[k].astype(jnp.float32) for k in range(2)]
    tail[...] = jnp.where(lanes < size // 2, flags[0], flags[1]).astype(tail.dtype)
    below = pltpu.make_async_copy(tail, packed.at[size:], sems.at[1])
    below.start()
    tile.wait()
    below.wait()


def left_kernel(occupied, right_occupied, panel, packed, wanted, tail, sems):
    wanted[...] = jnp.full(wanted.shape, right_occupied[1], wanted.dtype)
    pack_tile(occupied, panel, packed, tail, sems)


def right_kernel(occupied, panel, packed, tail, sems):
    pack_tile(occupied, panel, packed, tail, sems)


def base_kernel(kept, branch, earlier, density, base, earlier_tile, density_tile, sems):
    size = earlier_tile.shape[0]
    row, col = lax.axis_index("row"), lax.axis_index("col")
    half = lax.rem(col, 2)
    base[...] = jnp.zeros_like(base)

    @pl.when(lax.div(col, 2) == row)
    def _mine():
        rows = pl.ds(pl.multiple_of(half * size, size), size)
        copies = [
            pltpu.make_async_copy(earlier.at[rows], earlier_tile, sems.at[0]),
            pltpu.make_async_copy(density.at[rows], density_tile, sems.at[1]),
        ]
        for copy in copies:
            copy.start()
        for copy in copies:
            copy.wait()
        once = jnp.zeros((1, 1), jnp.float32)
        twice = jnp.zeros((1, 1), jnp.float32)
        for start in range(0, size, LANES):
            part = pl.ds(start, LANES)
            once = once + diagonal(earlier_tile[part, part].astype(jnp.float32))
            twice = twice + diagonal(2.0 * density_tile[part, part].astype(jnp.float32))
        squared = branch[half] == 1
        keep = (kept[half] == 1).astype(jnp.float32)
        lanes = lax.broadcasted_iota(jnp.int32, base.shape, 1)
        value = keep * jnp.where(squared, once, twice - once)
        weight = jnp.where(squared, keep, -keep)
        base[...] = jnp.where(lanes == 0, value, 0.0) + jnp.where(lanes == 2, weight, 0.0)


def flag_pair(payload):
    size = payload.shape[1]
    tail = payload[size:, :].astype(jnp.float32)
    return tail[0:1, 0:1], tail[0:1, size // 2 : size // 2 + 1]


def dot(a, b):
    return jnp.dot(a, b, preferred_element_type=jnp.float32)


def diagonal(block):
    rows = lax.broadcasted_iota(jnp.int32, block.shape, 0)
    cols = lax.broadcasted_iota(jnp.int32, block.shape, 1)
    return jnp.sum(jnp.where(rows == cols, block, 0.0), axis=(0, 1), keepdims=True)


def product_trace(left, right, size):
    total = jnp.zeros((1, 1), jnp.float32)
    for start in range(0, size, LANES):
        part = pl.ds(start, LANES)
        total = total + diagonal(dot(left(part), right[:size, part]))
    return total


def trace_kernel(right_occupied, own, one, chosen, right_own, right_trace, base, parts):
    size = own.shape[1]
    row, col = lax.axis_index("row"), lax.axis_index("col")
    count = lax.axis_size("col")
    half = lax.rem(col, 2)
    lanes = lax.broadcasted_iota(jnp.int32, (1, LANES), 1)
    parts[...] = jnp.zeros_like(parts)

    @pl.when(lax.div(col, 2) == row)
    def _near():
        second = right_occupied[1] == 1
        value = product_trace(lambda part: jnp.where(second, one[part, :], own[part, :]), right_own, size)
        flags = [jnp.where(second, a, b) for a, b in zip(flag_pair(one), flag_pair(own))]
        occupied = (right_occupied[0] + right_occupied[1]).astype(jnp.float32)
        value = value * jnp.where(half == 1, flags[1], flags[0]) * occupied
        known = base[0:1, :]
        weight = jnp.sum(jnp.where(lanes == 2, known, 0.0), axis=1, keepdims=True)
        parts[...] += known + jnp.where(lanes == 0, value * weight, 0.0)

    @pl.when(lax.div(lax.rem(col + count - 2, count), 2) == row)
    def _far():
        value = product_trace(lambda part: chosen[part, :], right_trace, size)
        flags, right_flags = flag_pair(chosen), flag_pair(right_trace)
        value = value * jnp.where(half == 1, flags[1], flags[0]) * (right_flags[0] + right_flags[1])
        parts[...] += jnp.where(lanes == 1, value, 0.0)


def middle_kernel(parts, spread):
    spread[...] = jnp.broadcast_to(jnp.sum(parts[...], axis=0, keepdims=True), spread.shape)


def total_kernel(order, parts, occupation):
    values = parts[...]
    lanes = lax.broadcasted_iota(jnp.int32, values.shape, 1)
    moved = jnp.concatenate([values[-2:], values[:-2]], axis=0)
    weights = jnp.sum(jnp.where(lanes == 2, moved, 0.0), axis=1, keepdims=True)
    far = jnp.sum(jnp.where(lanes == 1, values, 0.0), axis=1, keepdims=True)
    near = jnp.sum(jnp.where(lanes == 0, values, 0.0), axis=1, keepdims=True)
    occupation[0] = jnp.sum(near + weights * far) / order


def last_kernel(
    right_occupied, kept, branch, own, one, right_own, two, right_next, earlier, density, out,
    earlier_all, density_all, result, in_sems, out_sems,
):
    size = own.shape[1]
    step = size // 4
    pieces = [(start, half) for start in range(0, size, step) for half in range(2)]
    loads = []
    for k, (start, half) in enumerate(pieces):
        rows = pl.ds(half * size + start, step)
        pair = [
            pltpu.make_async_copy(earlier.at[rows], earlier_all.at[rows], in_sems.at[2 * k]),
            pltpu.make_async_copy(density.at[rows], density_all.at[rows], in_sems.at[2 * k + 1]),
        ]
        for copy in pair:
            copy.start()
        loads.append(pair)
    second = right_occupied[1] == 1
    occupied = (right_occupied[0] + right_occupied[1]).astype(jnp.float32)
    first_flags = [jnp.where(second, a, b) * occupied for a, b in zip(flag_pair(one), flag_pair(own))]
    right_flags = flag_pair(right_next)
    last_flags = [flag * (right_flags[0] + right_flags[1]) for flag in flag_pair(two)]
    stores = []
    for k, (start, half) in enumerate(pieces):
        if half == 0:
            part = pl.ds(start, step)
            first = dot(jnp.where(second, one[part, :], own[part, :]), right_own[:size, :])
            last = dot(two[part, :], right_next[:size, :])
        rows = pl.ds(half * size + start, step)
        for copy in loads[k]:
            copy.wait()
        product = earlier_all[rows, :].astype(jnp.float32) + first_flags[half] * first + last_flags[half] * last
        other = 2.0 * density_all[rows, :].astype(jnp.float32) - product
        value = jnp.where(branch[half] == 1, product, other)
        value = jnp.where(kept[half] == 1, value, 0.0)
        result[rows, :] = value.astype(result.dtype)
        store = pltpu.make_async_copy(result.at[rows], out.at[rows], out_sems.at[k])
        store.start()
        stores.append(store)
    for store in stores:
        store.wait()


def spread_over(rows, axis):
    return lax.all_to_all(rows, axis, 0, 0, tiled=True)


def local(left_panel, right_panel, earlier, density, left_occupied, right_occupied, kept_tiles, branch):
    block_rows, size = left_panel.shape
    row_count, col_count = lax.axis_size("row"), lax.axis_size("col")
    both = ("row", "col")
    left_occupied, right_occupied, kept_tiles = (a.reshape(2) for a in (left_occupied, right_occupied, kept_tiles))
    kind = left_panel.dtype
    payload = jax.ShapeDtypeStruct((size + FLAG_ROWS, size), kind)
    tail = [pltpu.VMEM((FLAG_ROWS, size), kind), pltpu.SemaphoreType.DMA((2,))]

    left_own, wanted = call(
        left_kernel,
        "left",
        [(left_occupied, SMEM), (right_occupied, SMEM), (left_panel, HBM)],
        [payload, jax.ShapeDtypeStruct((8, LANES), jnp.int32)],
        [HBM, VMEM],
        tail,
        LEFT_LIMIT,
    )
    left_one = shift(left_own, "col", -1)

    right_own = call(
        right_kernel, "right", [(right_occupied, SMEM), (right_panel, HBM)], payload, HBM, tail
    )
    to_trace = [
        (((j // 2 + 1) % row_count) * col_count + j, (j // 2) * col_count + (j + 2) % col_count)
        for j in range(col_count)
    ]
    right_trace = lax.ppermute(right_own, both, to_trace)

    to_wanted = [
        (((i + 1) % row_count) * col_count + j, i * col_count + (j + 2) % col_count)
        for i in range(row_count)
        for j in range(col_count)
    ]
    wanted = lax.ppermute(wanted, both, to_wanted)
    right_next = shift(right_own, "row", -1)
    base = call(
        base_kernel,
        "base",
        [(kept_tiles, SMEM), (branch, SMEM), (earlier, HBM), (density, HBM)],
        jax.ShapeDtypeStruct((8, LANES), jnp.float32),
        VMEM,
        [pltpu.VMEM((size, size), kind), pltpu.VMEM((size, size), kind), pltpu.SemaphoreType.DMA((2,))],
    )

    wanted, base = lax.optimization_barrier((wanted, base))

    chosen = jnp.where(wanted[0, 0] == 1, left_one, left_own)
    left_two = shift(chosen, "col", -2)

    parts = call(
        trace_kernel,
        "trace",
        [(right_occupied, SMEM)] + [(a, VMEM) for a in (left_own, left_one, chosen, right_own, right_trace, base)],
        jax.ShapeDtypeStruct((row_count, LANES), jnp.float32),
        VMEM,
    )
    parts = spread_over(parts, "row")
    parts = call(
        middle_kernel, "middle", [(parts, VMEM)], jax.ShapeDtypeStruct((col_count, LANES), jnp.float32), VMEM
    )
    parts = spread_over(parts, "col")
    occupation = call(
        functools.partial(total_kernel, row_count * block_rows),
        "total",
        [(parts, VMEM)],
        jax.ShapeDtypeStruct((1,), jnp.float32),
        SMEM,
    )

    new_density = call(
        last_kernel,
        "last",
        [(right_occupied, SMEM), (kept_tiles, SMEM), (branch, SMEM)]
        + [(a, VMEM) for a in (left_own, left_one, right_own, left_two, right_next)]
        + [(earlier, HBM), (density, HBM)],
        jax.ShapeDtypeStruct((block_rows, size), jnp.bfloat16),
        HBM,
        [pltpu.VMEM((block_rows, size), kind)] * 3
        + [pltpu.SemaphoreType.DMA((16,)), pltpu.SemaphoreType.DMA((8,))],
    )
    return new_density, occupation


def solution(mesh):
    whole = P("row", "col")
    in_specs = (whole,) * 7 + (P("row"),)
    return jax.shard_map(local, mesh=mesh, in_specs=in_specs, out_specs=(whole, P()), check_vma=False)
```

time: 96.1 us -> 98.4 us (1.024)
  Pallas kernels: 7.04 us -> 27.1 us
  local copies, waits for them, and re-layouts: 11.5 us -> 1.77 us
  other arithmetic: 3.76 us -> 0.06 us
  between operations: 4.63 us -> 1.49 us
  starting transfers between devices: 31 us -> 28.1 us
  waiting for transfers between devices: 0.01 us -> 2.12 us
    pallas_call x4 -> x7, Pallas kernels: 7.04 us -> 27.1 us  [call(): pl.pallas_call(kernel, out_shape=outs, in_specs=[spec for _, spec in ins]...]
    unnamed x26 -> x14, local copies, waits for them, and re-layouts: 5.81 us -> 1.25 us
    slice x5 -> x0, local copies, waits for them, and re-layouts: 4.42 us -> none  [the longest x2 1.91 us: pack(): occupied[1, 0] * tile_size]
    select_n x2 -> x0, other arithmetic: 2.81 us -> none  [pack(): tail = jnp.where(lanes < tile_size // 2, flags[0], flags[1])]
    ppermute x3, starting transfers between devices: 26.8 us -> 24.8 us  [shift(): lax.ppermute(value, axis, [(src, (src + steps) % count) for src in range(...]
    ppermute x1, waiting for transfers between devices: 0.01 us -> 1.32 us  [local(): wanted = lax.ppermute(wanted, both, to_wanted)]
  transfers between devices with their start and end apart: 5 -> 5, of which waited for: 0 -> 2; matrix products, arithmetic and copies ran while one was open for 6% -> 1% of each run, Pallas kernels for 4% -> 3%
where the time goes in v2:
time: 98.4 us; the launch traced here: 98.1 us
  blocking collectives  37.5 us (38%)
  starting transfers between devices  28.1 us (29%)
  Pallas kernels  27.1 us (28%)
  waiting for transfers between devices  2.12 us (2%)
  local copies, waits for them, and re-layouts  1.77 us (2%)
  between operations  1.49 us (2%)
    all_to_all x2, blocking collectives, spread_over(): return lax.all_to_all(rows, axis, 0, 0, tiled=True)  37.5 us
    pallas_call x7, Pallas kernels, call(): pl.pallas_call(kernel, out_shape=outs, in_specs=[spec for _, spec in ins]...  27.1 us
    ppermute x3, starting transfers between devices, shift(): lax.ppermute(value, axis, [(src, (src + steps) % count) for src in range(...  24.8 us
  transfers between devices with their start and end apart: 5, of which 2 were waited for; matrix products, arithmetic and copies ran while one was open for 1% of the time, Pallas kernels for 3%

profile of v2, /device:TPU:1, one launch (start us, length us, event | category | flops | bytes accessed | tf_op | source)
XLA Modules:
  0.0 98.1 jit_solution(6425466845199381225)
XLA Ops:
  0.6 0.0 copy-start.4
  0.6 0.0 copy-start.2
  0.7 18.4 %left.1 = (bf16[528,512]{1,0:T(8,128)(2,1)}, s32[8,128]{1,0:T(8,128)}) custom-call(s32[2]{0:T(128)} %bitcast.22, s32[2]{0:T(128)} %bitcast.16, bf16[1024,512]{1,0:T(8,128)(2,1)} %panel.2), custom_call_target="tpu_custom_call" | custom-call | tf_op jit(solution)/shard_map/left/pallas_call | solution.py:20
  19.1 0.0 copy-start.1
  19.1 14.5 %collective-permute-start = (bf16[528,512]{1,0:T(8,128)(2,1)}, bf16[528,512]{1,0:T(8,128)(2,1)S(1)}, u32[]{:S(2)}, u32[]{:S(2)}) collective-permute-start(bf16[528,512]{1,0:T(8,128)(2,1)} %get-tuple-element.6.own), channel_id=1, source_target_pairs={{0,31},{1,0},{2,1},{3,2},{4,3},{5,4},{6,5},{7,6},{8,7},{9,8},{10,9... | collective-permute-start | bytes 1622024 | tf_op jit(solution)/shard_map/ppermute | solution.py:33
  33.6 1.9 %collective-permute-start.1 = (s32[8,128]{1,0:T(8,128)}, s32[8,128]{1,0:T(8,128)S(1)}, u32[]{:S(2)}, u32[]{:S(2)}) collective-permute-start(s32[8,128]{1,0:T(8,128)} %get-tuple-element.7), channel_id=1, source_target_pairs={{32,2},{33,3},{34,4},{35,5},{36,6},{37,7},{38,8},{39,9},{40,10},{4... | collective-permute-start | bytes 12296 | tf_op jit(solution)/shard_map/ppermute | solution.py:236
  35.5 0.0 copy-done.4
  35.6 0.0 copy-start.3
  35.6 1.2 %copy-done.3 = bf16[1024,512]{1,0:T(8,128)(2,1)S(1)} copy-done((bf16[1024,512]{1,0:T(8,128)(2,1)S(1)}, bf16[1024,512]{1,0:T(8,128)(2,1)}, u32[]{:S(2)}) %copy-start.3) | copy-done | bytes 1048600
  36.8 0.6 right.1.right_own
  37.4 0.0 copy-start.5
  37.4 0.0 copy-start.6
  37.4 1.3 %collective-permute-start.4 = (bf16[528,512]{1,0:T(8,128)(2,1)S(1)}, bf16[528,512]{1,0:T(8,128)(2,1)S(1)}, u32[]{:S(2)}, u32[]{:S(2)}) collective-permute-start(bf16[528,512]{1,0:T(8,128)(2,1)S(1)} %right.1.right_own), channel_id=1, source_target_pairs={{32,2},{33,3},{66,36},{67,37},{100,70},{101,71},{134,104},{135,105... | collective-permute-start | bytes 1622024 | tf_op jit(solution)/shard_map/ppermute | solution.py:229
  38.8 2.2 %collective-permute-start.3 = (bf16[528,512]{1,0:T(8,128)(2,1)S(1)}, bf16[528,512]{1,0:T(8,128)(2,1)S(1)}, u32[]{:S(2)}, u32[]{:S(2)}) collective-permute-start(bf16[528,512]{1,0:T(8,128)(2,1)S(1)} %right.1.right_own), channel_id=1, source_target_pairs={{0,480},{32,0},{64,32},{96,64},{128,96},{160,128},{192,160},{224,1... | collective-permute-start | bytes 1622024 | tf_op jit(solution)/shard_map/ppermute | solution.py:33
  41.0 0.0 copy-done.2
  41.0 0.0 copy-done.1
  41.0 0.0 copy-done.5
  41.0 0.0 copy-done.6
  41.1 0.0 copy-start
  41.1 0.6 base.1
  41.7 1.3 %collective-permute-done.1 = s32[8,128]{1,0:T(8,128)S(1)} collective-permute-done((s32[8,128]{1,0:T(8,128)}, s32[8,128]{1,0:T(8,128)S(1)}, u32[]{:S(2)}, u32[]{:S(2)}) %collective-permute-start.1) | collective-permute-done | bytes 4128 | tf_op jit(solution)/shard_map/ppermute | solution.py:236
  43.0 0.5 slice.3
  44.1 0.8 collective-permute-done.one
  44.9 0.0 copy-done
  44.9 0.1 broadcast_select_fusion.chosen
  45.0 8.1 %collective-permute-start.2 = (bf16[528,512]{1,0:T(8,128)(2,1)S(1)}, bf16[528,512]{1,0:T(8,128)(2,1)S(1)}, u32[]{:S(2)}, u32[]{:S(2)}) collective-permute-start(bf16[528,512]{1,0:T(8,128)(2,1)S(1)} %broadcast_select_fusion.chosen), channel_id=1, source_target_pairs={{0,30},{1,31},{2,0},{3,1},{4,2},{5,3},{6,4},{7,5},{8,6},{9,7},{10,... | collective-permute-start | bytes 1622024 | tf_op jit(solution)/shard_map/ppermute | solution.py:33
  53.1 0.0 collective-permute-done.4.right_trace
  53.1 0.6 trace.1
  53.7 14.4 %all_to_all.22 = f32[16,1,128]{2,1,0:T(1,128)S(1)} all-to-all(f32[16,1,128]{2,1,0:T(1,128)S(1)} %bitcast.14), channel_id=1, replica_groups=mesh['row'=16,'col'=32] {'row'}, dimensions={0} | all-to-all | bytes 16384 | tf_op jit(solution)/shard_map/all_to_all | solution.py:199
  68.1 23.1 %all_to_all.23 = f32[32,1,128]{2,1,0:T(1,128)S(1)} all-to-all(f32[32,1,128]{2,1,0:T(1,128)S(1)} %bitcast.12), channel_id=1, replica_groups=mesh['row'=16,'col'=32] {'col'}, dimensions={0} | all-to-all | bytes 32768 | tf_op jit(solution)/shard_map/all_to_all | solution.py:199
  91.2 0.7 total.1
  91.9 0.0 collective-permute-done.3.right_next
  91.9 0.0 collective-permute-done.2.two
  91.9 6.1 %last.1 = bf16[1024,512]{1,0:T(8,128)(2,1)} custom-call(s32[2]{0:T(128)S(1)} %bitcast.19, s32[2]{0:T(128)S(1)} %bitcast.21, s32[2]{0:T(128)S(1)} %copy-done.6, bf16[528,512]{1,0:T(8,128)(2,1)S(1)} %copy-done, bf16[528,512]{1,0:T(8,128)(2,1)S(1)} %collective-permute-done.one, bf16[528,512]{1,0:T(8,128)(2,1)S(1)} %right.1.right_own, ...), custom_call_target="tpu_custom_call" | custom-call | tf_op jit(solution)/shard_map/last/pallas_call | solution.py:20
  (1 shorter events, 0.0 us)
Async XLA Ops:
  0.6 34.9 %copy-start.4 = (s32[2,1]{0,1:T(1,128)S(1)}, s32[2,1]{0,1:T(1,128)}, u32[]{:S(2)}) copy-start(s32[2,1]{0,1:T(1,128)} %param.13) | copy-start | bytes 28
  0.6 40.4 %copy-start.2 = (bf16[1024,512]{1,0:T(8,128)(2,1)S(1)}, bf16[1024,512]{1,0:T(8,128)(2,1)}, u32[]{:S(2)}) copy-start(bf16[1024,512]{1,0:T(8,128)(2,1)} %density.3) | copy-start | bytes 3145732
  19.1 22.0 %copy-start.1 = (bf16[1024,512]{1,0:T(8,128)(2,1)S(1)}, bf16[1024,512]{1,0:T(8,128)(2,1)}, u32[]{:S(2)}) copy-start(bf16[1024,512]{1,0:T(8,128)(2,1)} %earlier.3) | copy-start | bytes 3145732
  19.1 25.9 %collective-permute-start = (bf16[528,512]{1,0:T(8,128)(2,1)}, bf16[528,512]{1,0:T(8,128)(2,1)S(1)}, u32[]{:S(2)}, u32[]{:S(2)}) collective-permute-start(bf16[528,512]{1,0:T(8,128)(2,1)} %get-tuple-element.6.own), channel_id=1, source_target_pairs={{0,31},{1,0},{2,1},{3,2},{4,3},{5,4},{6,5},{7,6},{8,7},{9,8},{10,9... | collective-permute-start | bytes 1622024 | tf_op jit(solution)/shard_map/ppermute | solution.py:33
  33.6 9.4 %collective-permute-start.1 = (s32[8,128]{1,0:T(8,128)}, s32[8,128]{1,0:T(8,128)S(1)}, u32[]{:S(2)}, u32[]{:S(2)}) collective-permute-start(s32[8,128]{1,0:T(8,128)} %get-tuple-element.7), channel_id=1, source_target_pairs={{32,2},{33,3},{34,4},{35,5},{36,6},{37,7},{38,8},{39,9},{40,10},{4... | collective-permute-start | bytes 12296 | tf_op jit(solution)/shard_map/ppermute | solution.py:236
  35.6 1.2 %copy-start.3 = (bf16[1024,512]{1,0:T(8,128)(2,1)S(1)}, bf16[1024,512]{1,0:T(8,128)(2,1)}, u32[]{:S(2)}) copy-start(bf16[1024,512]{1,0:T(8,128)(2,1)} %panel.3) | copy-start | bytes 3145732
  37.4 3.6 %copy-start.5 = (s32[2,1]{0,1:T(1,128)S(1)}, s32[2,1]{0,1:T(1,128)}, u32[]{:S(2)}) copy-start(s32[2,1]{0,1:T(1,128)} %param.14) | copy-start | bytes 28
  37.4 3.6 %copy-start.6 = (s32[2]{0:T(128)S(1)}, s32[2]{0:T(128)}, u32[]{:S(2)}) copy-start(s32[2]{0:T(128)} %branch.3) | copy-start | bytes 28
  37.4 15.6 %collective-permute-start.4 = (bf16[528,512]{1,0:T(8,128)(2,1)S(1)}, bf16[528,512]{1,0:T(8,128)(2,1)S(1)}, u32[]{:S(2)}, u32[]{:S(2)}) collective-permute-start(bf16[528,512]{1,0:T(8,128)(2,1)S(1)} %right.1.right_own), channel_id=1, source_target_pairs={{32,2},{33,3},{66,36},{67,37},{100,70},{101,71},{134,104},{135,105... | collective-permute-start | bytes 1622024 | tf_op jit(solution)/shard_map/ppermute | solution.py:229
  38.8 53.1 %collective-permute-start.3 = (bf16[528,512]{1,0:T(8,128)(2,1)S(1)}, bf16[528,512]{1,0:T(8,128)(2,1)S(1)}, u32[]{:S(2)}, u32[]{:S(2)}) collective-permute-start(bf16[528,512]{1,0:T(8,128)(2,1)S(1)} %right.1.right_own), channel_id=1, source_target_pairs={{0,480},{32,0},{64,32},{96,64},{128,96},{160,128},{192,160},{224,1... | collective-permute-start | bytes 1622024 | tf_op jit(solution)/shard_map/ppermute | solution.py:33
  41.1 3.9 %copy-start = (bf16[528,512]{1,0:T(8,128)(2,1)S(1)}, bf16[528,512]{1,0:T(8,128)(2,1)}, u32[]{:S(2)}) copy-start(bf16[528,512]{1,0:T(8,128)(2,1)} %get-tuple-element.6.own) | copy-start | bytes 1622020
  45.0 46.9 %collective-permute-start.2 = (bf16[528,512]{1,0:T(8,128)(2,1)S(1)}, bf16[528,512]{1,0:T(8,128)(2,1)S(1)}, u32[]{:S(2)}, u32[]{:S(2)}) collective-permute-start(bf16[528,512]{1,0:T(8,128)(2,1)S(1)} %broadcast_select_fusion.chosen), channel_id=1, source_target_pairs={{0,30},{1,31},{2,0},{3,1},{4,2},{5,3},{6,4},{7,5},{8,6},{9,7},{10,... | collective-permute-start | bytes 1622024 | tf_op jit(solution)/shard_map/ppermute | solution.py:33

commit v3 on v2

--- a/solution.py
+++ b/solution.py
@@ -9,7 +9,7 @@
 
 FLAG_ROWS = 16
 LANES = 128
-LEFT_LIMIT = 62 * 2**20
+PIECES = 4
 
 VMEM = pl.BlockSpec(memory_space=pltpu.VMEM)
 SMEM = pl.BlockSpec(memory_space=pltpu.SMEM)
@@ -33,27 +33,43 @@
     return lax.ppermute(value, axis, [(src, (src + steps) % count) for src in range(count)])
 
 
-def pack_tile(occupied, panel, packed, tail, sems):
+def write_flags(occupied, packed):
+    size = packed.shape[1]
+    lanes = lax.broadcasted_iota(jnp.int32, (FLAG_ROWS, size), 1)
+    flags = [occupied[k].astype(jnp.float32) for k in range(2)]
+    packed[size:, :] = jnp.where(lanes < size // 2, flags[0], flags[1]).astype(packed.dtype)
+
+
+def pack_tile(occupied, panel, packed, sem):
     size = panel.shape[1]
     rows = pl.ds(pl.multiple_of(occupied[1] * size, size), size)
-    tile = pltpu.make_async_copy(panel.at[rows], packed.at[:size], sems.at[0])
-    tile.start()
-    lanes = lax.broadcasted_iota(jnp.int32, tail.shape, 1)
-    flags = [occupied[k].astype(jnp.float32) for k in range(2)]
-    tail[...] = jnp.where(lanes < size // 2, flags[0], flags[1]).astype(tail.dtype)
-    below = pltpu.make_async_copy(tail, packed.at[size:], sems.at[1])
-    below.start()
-    tile.wait()
-    below.wait()
-
-
-def left_kernel(occupied, right_occupied, panel, packed, wanted, tail, sems):
+    copy = pltpu.make_async_copy(panel.at[rows], packed.at[:size], sem)
+    copy.start()
+    write_flags(occupied, packed)
+    copy.wait()
+
+
+def left_kernel(occupied, right_occupied, panel, packed, wanted, stage, in_sems, out_sems):
+    size = panel.shape[1]
+    step = size // PIECES
+    loads, stores = [], []
+    for k in range(PIECES):
+        rows = pl.ds(pl.multiple_of(occupied[1] * size, size) + k * step, step)
+        loads.append(pltpu.make_async_copy(panel.at[rows], stage.at[pl.ds(k * step, step)], in_sems.at[k]))
+        loads[k].start()
+    write_flags(occupied, stage)
     wanted[...] = jnp.full(wanted.shape, right_occupied[1], wanted.dtype)
-    pack_tile(occupied, panel, packed, tail, sems)
-
-
-def right_kernel(occupied, panel, packed, tail, sems):
-    pack_tile(occupied, panel, packed, tail, sems)
+    for k in range(PIECES):
+        loads[k].wait()
+        rows = pl.ds(k * step, step if k < PIECES - 1 else step + FLAG_ROWS)
+        stores.append(pltpu.make_async_copy(stage.at[rows], packed.at[rows], out_sems.at[k]))
+        stores[k].start()
+    for store in stores:
+        store.wait()
+
+
+def right_kernel(occupied, panel, packed, sem):
+    pack_tile(occupied, panel, packed, sem)
 
 
 def base_kernel(kept, branch, earlier, density, base, earlier_tile, density_tile, sems):
@@ -153,44 +169,30 @@
 
 
 def last_kernel(
-    right_occupied, kept, branch, own, one, right_own, two, right_next, earlier, density, out,
-    earlier_all, density_all, result, in_sems, out_sems,
+    right_occupied, kept, branch, own, one, right_own, two, right_next, earlier, density, out, result, sems
 ):
     size = own.shape[1]
     step = size // 4
-    pieces = [(start, half) for start in range(0, size, step) for half in range(2)]
-    loads = []
-    for k, (start, half) in enumerate(pieces):
-        rows = pl.ds(half * size + start, step)
-        pair = [
-            pltpu.make_async_copy(earlier.at[rows], earlier_all.at[rows], in_sems.at[2 * k]),
-            pltpu.make_async_copy(density.at[rows], density_all.at[rows], in_sems.at[2 * k + 1]),
-        ]
-        for copy in pair:
-            copy.start()
-        loads.append(pair)
     second = right_occupied[1] == 1
     occupied = (right_occupied[0] + right_occupied[1]).astype(jnp.float32)
     first_flags = [jnp.where(second, a, b) * occupied for a, b in zip(flag_pair(one), flag_pair(own))]
     right_flags = flag_pair(right_next)
     last_flags = [flag * (right_flags[0] + right_flags[1]) for flag in flag_pair(two)]
     stores = []
-    for k, (start, half) in enumerate(pieces):
-        if half == 0:
-            part = pl.ds(start, step)
-            first = dot(jnp.where(second, one[part, :], own[part, :]), right_own[:size, :])
-            last = dot(two[part, :], right_next[:size, :])
-        rows = pl.ds(half * size + start, step)
-        for copy in loads[k]:
-            copy.wait()
-        product = earlier_all[rows, :].astype(jnp.float32) + first_flags[half] * first + last_flags[half] * last
-        other = 2.0 * density_all[rows, :].astype(jnp.float32) - product
-        value = jnp.where(branch[half] == 1, product, other)
-        value = jnp.where(kept[half] == 1, value, 0.0)
-        result[rows, :] = value.astype(result.dtype)
-        store = pltpu.make_async_copy(result.at[rows], out.at[rows], out_sems.at[k])
-        store.start()
-        stores.append(store)
+    for start in range(0, size, step):
+        part = pl.ds(start, step)
+        first = dot(jnp.where(second, one[part, :], own[part, :]), right_own[:size, :])
+        last = dot(two[part, :], right_next[:size, :])
+        for half in range(2):
+            rows = pl.ds(half * size + start, step)
+            product = earlier[rows, :].astype(jnp.float32) + first_flags[half] * first + last_flags[half] * last
+            other = 2.0 * density[rows, :].astype(jnp.float32) - product
+            value = jnp.where(branch[half] == 1, product, other)
+            value = jnp.where(kept[half] == 1, value, 0.0)
+            result[rows, :] = value.astype(result.dtype)
+            store = pltpu.make_async_copy(result.at[rows], out.at[rows], sems.at[len(stores)])
+            store.start()
+            stores.append(store)
     for store in stores:
         store.wait()
 
@@ -206,7 +208,7 @@
     left_occupied, right_occupied, kept_tiles = (a.reshape(2) for a in (left_occupied, right_occupied, kept_tiles))
     kind = left_panel.dtype
     payload = jax.ShapeDtypeStruct((size + FLAG_ROWS, size), kind)
-    tail = [pltpu.VMEM((FLAG_ROWS, size), kind), pltpu.SemaphoreType.DMA((2,))]
+    pack_scratch = [pltpu.SemaphoreType.DMA]
 
     left_own, wanted = call(
         left_kernel,
@@ -214,19 +216,21 @@
         [(left_occupied, SMEM), (right_occupied, SMEM), (left_panel, HBM)],
         [payload, jax.ShapeDtypeStruct((8, LANES), jnp.int32)],
         [HBM, VMEM],
-        tail,
-        LEFT_LIMIT,
+        [pltpu.VMEM(payload.shape, kind), pltpu.SemaphoreType.DMA((PIECES,)), pltpu.SemaphoreType.DMA((PIECES,))],
+        62 * 2**20,
     )
     left_one = shift(left_own, "col", -1)
 
     right_own = call(
-        right_kernel, "right", [(right_occupied, SMEM), (right_panel, HBM)], payload, HBM, tail
+        right_kernel, "right", [(right_occupied, SMEM), (right_panel, HBM)], payload, VMEM, pack_scratch
     )
     to_trace = [
         (((j // 2 + 1) % row_count) * col_count + j, (j // 2) * col_count + (j + 2) % col_count)
         for j in range(col_count)
     ]
+    wanted, right_own = lax.optimization_barrier((wanted, right_own))
     right_trace = lax.ppermute(right_own, both, to_trace)
+    right_next = shift(right_own, "row", -1)
 
     to_wanted = [
         (((i + 1) % row_count) * col_count + j, i * col_count + (j + 2) % col_count)
@@ -234,7 +238,6 @@
         for j in range(col_count)
     ]
     wanted = lax.ppermute(wanted, both, to_wanted)
-    right_next = shift(right_own, "row", -1)
     base = call(
         base_kernel,
         "base",
@@ -274,11 +277,10 @@
         "last",
         [(right_occupied, SMEM), (kept_tiles, SMEM), (branch, SMEM)]
         + [(a, VMEM) for a in (left_own, left_one, right_own, left_two, right_next)]
-        + [(earlier, HBM), (density, HBM)],
+        + [(earlier, VMEM), (density, VMEM)],
         jax.ShapeDtypeStruct((block_rows, size), jnp.bfloat16),
         HBM,
-        [pltpu.VMEM((block_rows, size), kind)] * 3
-        + [pltpu.SemaphoreType.DMA((16,)), pltpu.SemaphoreType.DMA((8,))],
+        [pltpu.VMEM((block_rows, size), kind), pltpu.SemaphoreType.DMA((8,))],
     )
     return new_density, occupation
 

time: 98.4 us -> 79.8 us (0.81)
  Pallas kernels: 27.1 us -> 8.17 us
    pallas_call x7, Pallas kernels: 27.1 us -> 8.17 us  [call(): pl.pallas_call(kernel, out_shape=outs, in_specs=[spec for _, spec in ins]...]
    ppermute x1, waiting for transfers between devices: 1.32 us -> 3 us  [local(): wanted = lax.ppermute(wanted, both, to_wanted)]
  transfers between devices with their start and end apart: 5 -> 5, of which waited for: 2 -> 1; matrix products, arithmetic and copies ran while one was open for 1% -> 1% of each run, Pallas kernels for 3% -> 3%
where the time goes in v3:
time: 79.8 us; the launch traced here: 79.3 us
  blocking collectives  37.5 us (47%)
  starting transfers between devices  27.3 us (34%)
  Pallas kernels  8.17 us (10%)
  waiting for transfers between devices  3.01 us (4%)
  local copies, waits for them, and re-layouts  1.83 us (2%)
  between operations  1.49 us (2%)
    all_to_all x2, blocking collectives, spread_over(): return lax.all_to_all(rows, axis, 0, 0, tiled=True)  37.5 us
    ppermute x3, starting transfers between devices, shift(): lax.ppermute(value, axis, [(src, (src + steps) % count) for src in range(...  23.9 us
    pallas_call x7, Pallas kernels, call(): pl.pallas_call(kernel, out_shape=outs, in_specs=[spec for _, spec in ins]...  8.17 us
    ppermute x1, waiting for transfers between devices, local(): wanted = lax.ppermute(wanted, both, to_wanted)  3 us
    ppermute x1, starting transfers between devices, local(): wanted = lax.ppermute(wanted, both, to_wanted)  2.04 us
  transfers between devices with their start and end apart: 5, of which 1 were waited for; matrix products, arithmetic and copies ran while one was open for 1% of the time, Pallas kernels for 3%

profile of v3, /device:TPU:1, one launch (start us, length us, event | category | flops | bytes accessed | tf_op | source)
XLA Modules:
  0.0 79.3 jit_solution(16440290348595482151)
XLA Ops:
  0.6 0.0 copy-start.4
  0.6 0.0 copy-start.2
  0.7 3.2 %left.1 = (bf16[528,512]{1,0:T(8,128)(2,1)}, s32[8,128]{1,0:T(8,128)}) custom-call(s32[2]{0:T(128)} %bitcast.22, s32[2]{0:T(128)} %bitcast.16, bf16[1024,512]{1,0:T(8,128)(2,1)} %panel.2), custom_call_target="tpu_custom_call" | custom-call | tf_op jit(solution)/shard_map/left/pallas_call | solution.py:20
  3.9 0.0 copy-start.1
  3.9 14.5 %collective-permute-start = (bf16[528,512]{1,0:T(8,128)(2,1)}, bf16[528,512]{1,0:T(8,128)(2,1)S(1)}, u32[]{:S(2)}, u32[]{:S(2)}) collective-permute-start(bf16[528,512]{1,0:T(8,128)(2,1)} %get-tuple-element.8.own), channel_id=1, source_target_pairs={{0,31},{1,0},{2,1},{3,2},{4,3},{5,4},{6,5},{7,6},{8,7},{9,8},{10,9... | collective-permute-start | bytes 1622024 | tf_op jit(solution)/shard_map/ppermute | solution.py:33
  18.4 0.0 copy-done.4
  18.4 0.0 copy-start.3
  18.5 1.2 %copy-done.3 = bf16[1024,512]{1,0:T(8,128)(2,1)S(1)} copy-done((bf16[1024,512]{1,0:T(8,128)(2,1)S(1)}, bf16[1024,512]{1,0:T(8,128)(2,1)}, u32[]{:S(2)}) %copy-start.3) | copy-done | bytes 1048600
  19.7 0.0 copy-start.7
  19.7 0.6 right.1.right_own
  20.3 0.1 copy-done.7
  20.4 0.0 copy-start.5
  20.4 0.0 copy-start.6
  20.4 2.0 %collective-permute-start.1 = (s32[8,128]{1,0:T(8,128)S(1)}, s32[8,128]{1,0:T(8,128)S(1)}, u32[]{:S(2)}, u32[]{:S(2)}) collective-permute-start(s32[8,128]{1,0:T(8,128)S(1)} %copy-done.7), channel_id=1, source_target_pairs={{32,2},{33,3},{34,4},{35,5},{36,6},{37,7},{38,8},{39,9},{40,10},{4... | collective-permute-start | bytes 12296 | tf_op jit(solution)/shard_map/ppermute | solution.py:240
  22.4 1.3 %collective-permute-start.4 = (bf16[528,512]{1,0:T(8,128)(2,1)S(1)}, bf16[528,512]{1,0:T(8,128)(2,1)S(1)}, u32[]{:S(2)}, u32[]{:S(2)}) collective-permute-start(bf16[528,512]{1,0:T(8,128)(2,1)S(1)} %right.1.right_own), channel_id=1, source_target_pairs={{32,2},{33,3},{66,36},{67,37},{100,70},{101,71},{134,104},{135,105... | collective-permute-start | bytes 1622024 | tf_op jit(solution)/shard_map/ppermute | solution.py:232
  23.7 2.2 %collective-permute-start.3 = (bf16[528,512]{1,0:T(8,128)(2,1)S(1)}, bf16[528,512]{1,0:T(8,128)(2,1)S(1)}, u32[]{:S(2)}, u32[]{:S(2)}) collective-permute-start(bf16[528,512]{1,0:T(8,128)(2,1)S(1)} %right.1.right_own), channel_id=1, source_target_pairs={{0,480},{32,0},{64,32},{96,64},{128,96},{160,128},{192,160},{224,1... | collective-permute-start | bytes 1622024 | tf_op jit(solution)/shard_map/ppermute | solution.py:33
  26.0 0.0 copy-done.2
  26.0 0.0 copy-done.1
  26.0 0.0 copy-done.5
  26.0 0.0 copy-done.6
  26.0 0.0 copy-start
  26.0 0.6 base.1
  26.6 3.0 %collective-permute-done.1 = s32[8,128]{1,0:T(8,128)S(1)} collective-permute-done((s32[8,128]{1,0:T(8,128)S(1)}, s32[8,128]{1,0:T(8,128)S(1)}, u32[]{:S(2)}, u32[]{:S(2)}) %collective-permute-start.1) | collective-permute-done | bytes 4128 | tf_op jit(solution)/shard_map/ppermute | solution.py:240
  29.6 0.5 slice.3
  30.8 0.0 collective-permute-done.one
  30.8 0.0 copy-done
  30.8 0.1 broadcast_select_fusion.chosen
  30.9 7.2 %collective-permute-start.2 = (bf16[528,512]{1,0:T(8,128)(2,1)S(1)}, bf16[528,512]{1,0:T(8,128)(2,1)S(1)}, u32[]{:S(2)}, u32[]{:S(2)}) collective-permute-start(bf16[528,512]{1,0:T(8,128)(2,1)S(1)} %broadcast_select_fusion.chosen), channel_id=1, source_target_pairs={{0,30},{1,31},{2,0},{3,1},{4,2},{5,3},{6,4},{7,5},{8,6},{9,7},{10,... | collective-permute-start | bytes 1622024 | tf_op jit(solution)/shard_map/ppermute | solution.py:33
  38.0 0.0 collective-permute-done.4.right_trace
  38.0 0.6 trace.1
  38.6 14.4 %all_to_all.22 = f32[16,1,128]{2,1,0:T(1,128)S(1)} all-to-all(f32[16,1,128]{2,1,0:T(1,128)S(1)} %bitcast.14), channel_id=1, replica_groups=mesh['row'=16,'col'=32] {'row'}, dimensions={0} | all-to-all | bytes 16384 | tf_op jit(solution)/shard_map/all_to_all | solution.py:201
  53.0 23.1 %all_to_all.23 = f32[32,1,128]{2,1,0:T(1,128)S(1)} all-to-all(f32[32,1,128]{2,1,0:T(1,128)S(1)} %bitcast.12), channel_id=1, replica_groups=mesh['row'=16,'col'=32] {'col'}, dimensions={0} | all-to-all | bytes 32768 | tf_op jit(solution)/shard_map/all_to_all | solution.py:201
  76.1 0.7 total.1
  76.9 0.0 collective-permute-done.3.right_next
  76.9 0.0 collective-permute-done.2.two
  76.9 2.5 %last.1 = bf16[1024,512]{1,0:T(8,128)(2,1)} custom-call(s32[2]{0:T(128)S(1)} %bitcast.19, s32[2]{0:T(128)S(1)} %bitcast.21, s32[2]{0:T(128)S(1)} %copy-done.6, bf16[528,512]{1,0:T(8,128)(2,1)S(1)} %copy-done, bf16[528,512]{1,0:T(8,128)(2,1)S(1)} %collective-permute-done.one, bf16[528,512]{1,0:T(8,128)(2,1)S(1)} %right.1.right_own, ...), custom_call_target="tpu_custom_call" | custom-call | tf_op jit(solution)/shard_map/last/pallas_call | solution.py:20
  (1 shorter events, 0.0 us)
Async XLA Ops:
  0.6 17.8 %copy-start.4 = (s32[2,1]{0,1:T(1,128)S(1)}, s32[2,1]{0,1:T(1,128)}, u32[]{:S(2)}) copy-start(s32[2,1]{0,1:T(1,128)} %param.13) | copy-start | bytes 28
  0.6 25.3 %copy-start.2 = (bf16[1024,512]{1,0:T(8,128)(2,1)S(1)}, bf16[1024,512]{1,0:T(8,128)(2,1)}, u32[]{:S(2)}) copy-start(bf16[1024,512]{1,0:T(8,128)(2,1)} %density.3) | copy-start | bytes 3145732
  3.9 22.1 %copy-start.1 = (bf16[1024,512]{1,0:T(8,128)(2,1)S(1)}, bf16[1024,512]{1,0:T(8,128)(2,1)}, u32[]{:S(2)}) copy-start(bf16[1024,512]{1,0:T(8,128)(2,1)} %earlier.3) | copy-start | bytes 3145732
  3.9 26.9 %collective-permute-start = (bf16[528,512]{1,0:T(8,128)(2,1)}, bf16[528,512]{1,0:T(8,128)(2,1)S(1)}, u32[]{:S(2)}, u32[]{:S(2)}) collective-permute-start(bf16[528,512]{1,0:T(8,128)(2,1)} %get-tuple-element.8.own), channel_id=1, source_target_pairs={{0,31},{1,0},{2,1},{3,2},{4,3},{5,4},{6,5},{7,6},{8,7},{9,8},{10,9... | collective-permute-start | bytes 1622024 | tf_op jit(solution)/shard_map/ppermute | solution.py:33
  18.4 1.2 %copy-start.3 = (bf16[1024,512]{1,0:T(8,128)(2,1)S(1)}, bf16[1024,512]{1,0:T(8,128)(2,1)}, u32[]{:S(2)}) copy-start(bf16[1024,512]{1,0:T(8,128)(2,1)} %panel.3) | copy-start | bytes 3145732
  19.7 0.7 copy-start.7
  20.4 5.6 %copy-start.5 = (s32[2,1]{0,1:T(1,128)S(1)}, s32[2,1]{0,1:T(1,128)}, u32[]{:S(2)}) copy-start(s32[2,1]{0,1:T(1,128)} %param.14) | copy-start | bytes 28
  20.4 5.7 %copy-start.6 = (s32[2]{0:T(128)S(1)}, s32[2]{0:T(128)}, u32[]{:S(2)}) copy-start(s32[2]{0:T(128)} %branch.3) | copy-start | bytes 28
  20.4 9.3 %collective-permute-start.1 = (s32[8,128]{1,0:T(8,128)S(1)}, s32[8,128]{1,0:T(8,128)S(1)}, u32[]{:S(2)}, u32[]{:S(2)}) collective-permute-start(s32[8,128]{1,0:T(8,128)S(1)} %copy-done.7), channel_id=1, source_target_pairs={{32,2},{33,3},{34,4},{35,5},{36,6},{37,7},{38,8},{39,9},{40,10},{4... | collective-permute-start | bytes 12296 | tf_op jit(solution)/shard_map/ppermute | solution.py:240
  22.4 15.6 %collective-permute-start.4 = (bf16[528,512]{1,0:T(8,128)(2,1)S(1)}, bf16[528,512]{1,0:T(8,128)(2,1)S(1)}, u32[]{:S(2)}, u32[]{:S(2)}) collective-permute-start(bf16[528,512]{1,0:T(8,128)(2,1)S(1)} %right.1.right_own), channel_id=1, source_target_pairs={{32,2},{33,3},{66,36},{67,37},{100,70},{101,71},{134,104},{135,105... | collective-permute-start | bytes 1622024 | tf_op jit(solution)/shard_map/ppermute | solution.py:232
  23.7 53.1 %collective-permute-start.3 = (bf16[528,512]{1,0:T(8,128)(2,1)S(1)}, bf16[528,512]{1,0:T(8,128)(2,1)S(1)}, u32[]{:S(2)}, u32[]{:S(2)}) collective-permute-start(bf16[528,512]{1,0:T(8,128)(2,1)S(1)} %right.1.right_own), channel_id=1, source_target_pairs={{0,480},{32,0},{64,32},{96,64},{128,96},{160,128},{192,160},{224,1... | collective-permute-start | bytes 1622024 | tf_op jit(solution)/shard_map/ppermute | solution.py:33
  26.0 4.8 %copy-start = (bf16[528,512]{1,0:T(8,128)(2,1)S(1)}, bf16[528,512]{1,0:T(8,128)(2,1)}, u32[]{:S(2)}) copy-start(bf16[528,512]{1,0:T(8,128)(2,1)} %get-tuple-element.8.own) | copy-start | bytes 1622020
  30.9 46.0 %collective-permute-start.2 = (bf16[528,512]{1,0:T(8,128)(2,1)S(1)}, bf16[528,512]{1,0:T(8,128)(2,1)S(1)}, u32[]{:S(2)}, u32[]{:S(2)}) collective-permute-start(bf16[528,512]{1,0:T(8,128)(2,1)S(1)} %broadcast_select_fusion.chosen), channel_id=1, source_target_pairs={{0,30},{1,31},{2,0},{3,1},{4,2},{5,3},{6,4},{7,5},{8,6},{9,7},{10,... | collective-permute-start | bytes 1622024 | tf_op jit(solution)/shard_map/ppermute | solution.py:33

commit v4 on v3

v4 whole, which is shorter than its diff:
```python
import functools

import jax
import jax.numpy as jnp
from jax import lax
from jax.experimental import pallas as pl
from jax.experimental.pallas import tpu as pltpu
from jax.sharding import PartitionSpec as P

FLAG_ROWS = 16
LANES = 128

VMEM = pl.BlockSpec(memory_space=pltpu.VMEM)
SMEM = pl.BlockSpec(memory_space=pltpu.SMEM)
HBM = pl.BlockSpec(memory_space=pltpu.HBM)


def call(kernel, name, ins, outs, out_specs, scratch=(), limit=12 * 2**20):
    return pl.pallas_call(
        kernel,
        out_shape=outs,
        in_specs=[spec for _, spec in ins],
        out_specs=out_specs,
        scratch_shapes=list(scratch),
        compiler_params=pltpu.CompilerParams(vmem_limit_bytes=limit),
        name=name,
    )(*[array for array, _ in ins])


def shift(value, axis, steps):
    count = lax.axis_size(axis)
    return lax.ppermute(value, axis, [(src, (src + steps) % count) for src in range(count)])


def pack_kernel(*refs):
    occupied, panels, packed, (stage, in_sems, out_sems) = refs[:2], refs[2:4], refs[4:6], refs[6:]
    size = stage.shape[2]
    loads, stores = [], []
    for side in range(2):
        rows = pl.ds(pl.multiple_of(occupied[side][1] * size, size), size)
        loads.append(pltpu.make_async_copy(panels[side].at[rows], stage.at[side, :size], in_sems.at[side]))
        loads[side].start()
    for side in range(2):
        lanes = lax.broadcasted_iota(jnp.int32, (FLAG_ROWS, size), 1)
        flags = [occupied[side][k].astype(jnp.float32) for k in range(2)]
        stage[side, size:, :] = jnp.where(lanes < size // 2, flags[0], flags[1]).astype(stage.dtype)
    for side in range(2):
        loads[side].wait()
        stores.append(pltpu.make_async_copy(stage.at[side], packed[side], out_sems.at[side]))
        stores[side].start()
    for store in stores:
        store.wait()


def base_kernel(right_occupied, kept, branch, right_own, earlier, density, base, wanted, right_here, earlier_tile, density_tile, sems):
    size = earlier_tile.shape[0]
    row, col = lax.axis_index(ROW), lax.axis_index(COL)
    half = lax.rem(col, 2)
    base[...] = jnp.zeros_like(base)
    wanted[...] = jnp.full(wanted.shape, right_occupied[1], wanted.dtype)
    right_here[...] = right_own[...]

    @pl.when(lax.div(col, 2) == row)
    def _mine():
        rows = pl.ds(pl.multiple_of(half * size, size), size)
        copies = [
            pltpu.make_async_copy(earlier.at[rows], earlier_tile, sems.at[0]),
            pltpu.make_async_copy(density.at[rows], density_tile, sems.at[1]),
        ]
        for copy in copies:
            copy.start()
        for copy in copies:
            copy.wait()
        once = jnp.zeros((1, 1), jnp.float32)
        twice = jnp.zeros((1, 1), jnp.float32)
        for start in range(0, size, LANES):
            part = pl.ds(start, LANES)
            once = once + diagonal(earlier_tile[part, part].astype(jnp.float32))
            twice = twice + diagonal(2.0 * density_tile[part, part].astype(jnp.float32))
        squared = branch[half] == 1
        keep = (kept[half] == 1).astype(jnp.float32)
        lanes = lax.broadcasted_iota(jnp.int32, base.shape, 1)
        value = keep * jnp.where(squared, once, twice - once)
        weight = jnp.where(squared, keep, -keep)
        high = lax.axis_index("x_hi")
        base[...] = jnp.where(lanes == 0, value, 0.0) + jnp.where(lanes == 3 + high, weight, 0.0)


def flag_pair(payload):
    size = payload.shape[1]
    tail = payload[size:, :].astype(jnp.float32)
    return tail[0:1, 0:1], tail[0:1, size // 2 : size // 2 + 1]


def dot(a, b):
    return jnp.dot(a, b, preferred_element_type=jnp.float32)


def diagonal(block):
    rows = lax.broadcasted_iota(jnp.int32, block.shape, 0)
    cols = lax.broadcasted_iota(jnp.int32, block.shape, 1)
    return jnp.sum(jnp.where(rows == cols, block, 0.0), axis=(0, 1), keepdims=True)


def product_trace(left, right, size):
    total = jnp.zeros((1, 1), jnp.float32)
    for start in range(0, size, LANES):
        part = pl.ds(start, LANES)
        total = total + diagonal(dot(left(part), right[:size, part]))
    return total


def far_here():
    row, col = lax.axis_index(ROW), lax.axis_index(COL)
    count = lax.axis_size(COL)
    return lax.div(lax.rem(col + count - 2, count), 2) == row


def decide_kernel(wanted, right_trace, second):
    second[...] = wanted[...]

    @pl.when(far_here())
    def _far():
        flag = flag_pair(right_trace)[1].astype(second.dtype)
        second[...] = jnp.broadcast_to(flag, second.shape)


def choose_kernel(second, own, one, chosen):
    use_one = jnp.max(second[...]) == 1

    @pl.when(use_one)
    def _one():
        chosen[...] = one[...]

    @pl.when(jnp.logical_not(use_one))
    def _own():
        chosen[...] = own[...]


def trace_kernel(right_occupied, own, one, chosen, right_own, right_trace, base, parts):
    size = own.shape[1]
    row, col = lax.axis_index(ROW), lax.axis_index(COL)
    half = lax.rem(col, 2)
    lanes = lax.broadcasted_iota(jnp.int32, (1, LANES), 1)
    parts[...] = jnp.zeros_like(parts)

    @pl.when(lax.div(col, 2) == row)
    def _near():
        second = right_occupied[1] == 1
        value = product_trace(lambda part: jnp.where(second, one[part, :], own[part, :]), right_own, size)
        flags = [jnp.where(second, a, b) for a, b in zip(flag_pair(one), flag_pair(own))]
        occupied = (right_occupied[0] + right_occupied[1]).astype(jnp.float32)
        value = value * jnp.where(half == 1, flags[1], flags[0]) * occupied
        known = base[0:1, :]
        weight = jnp.sum(jnp.where(lanes == 3 + lax.axis_index("x_hi"), known, 0.0), axis=1, keepdims=True)
        parts[...] += known + jnp.where(lanes == 0, value * weight, 0.0)

    @pl.when(far_here())
    def _far():
        value = product_trace(lambda part: chosen[part, :], right_trace, size)
        flags, right_flags = flag_pair(chosen), flag_pair(right_trace)
        value = value * jnp.where(half == 1, flags[1], flags[0]) * (right_flags[0] + right_flags[1])
        parts[...] += jnp.where(lanes == 1 + lax.axis_index("x_hi"), value, 0.0)


def middle_kernel(parts, spread):
    spread[...] = jnp.broadcast_to(jnp.sum(parts[...], axis=0, keepdims=True), spread.shape)


def total_kernel(order, parts, occupation):
    values = parts[...]
    lanes = lax.broadcasted_iota(jnp.int32, values.shape, 1)
    planes = lax.broadcasted_iota(jnp.int32, (values.shape[0], 1), 0)
    moved = jnp.concatenate([values[-2:], values[:-2]], axis=0)

    def lane(array, index):
        return jnp.sum(jnp.where(lanes == index, array, 0.0), axis=1, keepdims=True)

    low, high = lane(moved, 3), lane(moved, 4)
    low, high = jnp.where(planes < 2, high, low), jnp.where(planes < 2, low, high)
    occupation[0] = jnp.sum(lane(values, 0) + lane(values, 1) * low + lane(values, 2) * high) / order


def last_kernel(
    right_occupied, kept, branch, own, one, right_own, two, right_next, earlier, density, out, result, sems
):
    size = own.shape[1]
    step = size // 4
    second = right_occupied[1] == 1
    occupied = (right_occupied[0] + right_occupied[1]).astype(jnp.float32)
    first_flags = [jnp.where(second, a, b) * occupied for a, b in zip(flag_pair(one), flag_pair(own))]
    right_flags = flag_pair(right_next)
    last_flags = [flag * (right_flags[0] + right_flags[1]) for flag in flag_pair(two)]
    signs = [jnp.where(branch[half] == 1, 1.0, -1.0) for half in range(2)]
    stores = []
    for start in range(0, size, step):
        part = pl.ds(start, step)
        first = dot(jnp.where(second, one[part, :], own[part, :]), right_own[:size, :])
        last = dot(two[part, :], right_next[:size, :])
        for half in range(2):
            rows = pl.ds(half * size + start, step)
            product = earlier[rows, :].astype(jnp.float32) + first_flags[half] * first + last_flags[half] * last
            value = signs[half] * product + (1.0 - signs[half]) * density[rows, :].astype(jnp.float32)
            value = jnp.where(kept[half] == 1, value, 0.0)
            result[rows, :] = value.astype(result.dtype)
            store = pltpu.make_async_copy(result.at[rows], out.at[rows], sems.at[len(stores)])
            store.start()
            stores.append(store)
    for store in stores:
        store.wait()


def spread_over(rows, axis):
    return lax.all_to_all(rows, axis, 0, 0, tiled=True)


AXES = ("y", "x_lo", "core", "x_hi", "z")
SIZES = (4, 2, 2, 2, 16)
ROW, COL, PLANE = AXES[:3], AXES[3:], AXES[:4]


def local(left_panel, right_panel, earlier, density, left_occupied, right_occupied, kept_tiles, branch):
    block_rows, size = left_panel.shape
    row_count, col_count = lax.axis_size(ROW), lax.axis_size(COL)
    both = AXES
    left_occupied, right_occupied, kept_tiles = (a.reshape(2) for a in (left_occupied, right_occupied, kept_tiles))
    kind = left_panel.dtype
    payload = jax.ShapeDtypeStruct((size + FLAG_ROWS, size), kind)

    left_own, right_own = call(
        pack_kernel,
        "pack",
        [(left_occupied, SMEM), (right_occupied, SMEM), (left_panel, HBM), (right_panel, HBM)],
        [payload, payload],
        [HBM, HBM],
        [pltpu.VMEM((2,) + payload.shape, kind), pltpu.SemaphoreType.DMA((2,)), pltpu.SemaphoreType.DMA((2,))],
        62 * 2**20,
    )
    left_one = shift(left_own, COL, -1)

    to_trace = [
        (((j // 2 + 1) % row_count) * col_count + j, (j // 2) * col_count + (j + 2) % col_count)
        for j in range(col_count)
    ]
    right_trace = lax.ppermute(right_own, both, to_trace)

    base, wanted, right_here = call(
        base_kernel,
        "base",
        [(right_occupied, SMEM), (kept_tiles, SMEM), (branch, SMEM), (right_own, VMEM), (earlier, HBM), (density, HBM)],
        [jax.ShapeDtypeStruct((8, LANES), jnp.float32), jax.ShapeDtypeStruct((8, LANES), jnp.int32), payload],
        [VMEM, VMEM, VMEM],
        [pltpu.VMEM((size, size), kind), pltpu.VMEM((size, size), kind), pltpu.SemaphoreType.DMA((2,))],
    )

    to_wanted = [
        (((i + 1) % row_count) * col_count + j, i * col_count + (j + 2) % col_count)
        for i in range(row_count)
        for j in range(col_count)
        if j // 2 != i
    ]
    wanted = lax.ppermute(wanted, both, to_wanted)
    right_next = shift(right_here, ROW, -1)

    second = call(
        decide_kernel,
        "decide",
        [(wanted, VMEM), (right_trace, VMEM)],
        jax.ShapeDtypeStruct((8, LANES), jnp.int32),
        VMEM,
    )
    chosen = call(choose_kernel, "choose", [(a, VMEM) for a in (second, left_own, left_one)], payload, VMEM)
    left_two = shift(chosen, COL, -2)

    parts = call(
        trace_kernel,
        "trace",
        [(right_occupied, SMEM)] + [(a, VMEM) for a in (left_own, left_one, chosen, right_here, right_trace, base)],
        jax.ShapeDtypeStruct((lax.axis_size(PLANE), LANES), jnp.float32),
        VMEM,
    )
    parts = spread_over(parts, PLANE)
    parts = call(
        middle_kernel, "middle", [(parts, VMEM)], jax.ShapeDtypeStruct((lax.axis_size("z"), LANES), jnp.float32), VMEM
    )
    parts = spread_over(parts, "z")
    occupation = call(
        functools.partial(total_kernel, row_count * block_rows),
        "total",
        [(parts, VMEM)],
        jax.ShapeDtypeStruct((1,), jnp.float32),
        SMEM,
    )

    new_density = call(
        last_kernel,
        "last",
        [(right_occupied, SMEM), (kept_tiles, SMEM), (branch, SMEM)]
        + [(a, VMEM) for a in (left_own, left_one, right_here, left_two, right_next, earlier, density)],
        jax.ShapeDtypeStruct((block_rows, size), jnp.bfloat16),
        HBM,
        [pltpu.VMEM((block_rows, size), kind), pltpu.SemaphoreType.DMA((8,))],
    )
    return new_density, occupation


def solution(mesh):
    mesh = jax.sharding.Mesh(mesh.devices.reshape(SIZES), AXES)
    whole = P(ROW, COL)
    in_specs = (whole,) * 7 + (P(ROW),)
    return jax.shard_map(local, mesh=mesh, in_specs=in_specs, out_specs=(whole, P()), check_vma=False)
```

time: 79.8 us -> 73 us (0.915)
  blocking collectives: 37.5 us -> 33.1 us
  starting transfers between devices: 27.3 us -> 25.4 us
    ppermute x3, starting transfers between devices: 23.9 us -> 17.7 us  [shift(): lax.ppermute(value, axis, [(src, (src + steps) % count) for src in range(...]
    ppermute x1, starting transfers between devices: 1.32 us -> 6.32 us  [local(): right_trace = lax.ppermute(right_own, both, to_trace)]
    all_to_all x2, blocking collectives: 37.5 us -> 33.1 us  [spread_over(): return lax.all_to_all(rows, axis, 0, 0, tiled=True)]
    unnamed x16, local copies, waits for them, and re-layouts: 1.32 us -> 2.3 us
    pallas_call x7 -> x8, Pallas kernels: 8.17 us -> 7.46 us  [call(): pl.pallas_call(kernel, out_shape=outs, in_specs=[spec for _, spec in ins]...]
  transfers between devices with their start and end apart: 5 -> 5, of which waited for: 1 -> 1; matrix products, arithmetic and copies ran while one was open for 1% -> 0% of each run, Pallas kernels for 3% -> 3%
where the time goes in v4:
time: 73 us; the launch traced here: 72.6 us
  blocking collectives  33.1 us (45%)
  starting transfers between devices  25.4 us (35%)
  Pallas kernels  7.46 us (10%)
  waiting for transfers between devices  3.45 us (5%)
  local copies, waits for them, and re-layouts  2.3 us (3%)
  between operations  0.84 us (1%)
    all_to_all x2, blocking collectives, spread_over(): return lax.all_to_all(rows, axis, 0, 0, tiled=True)  33.1 us
    ppermute x3, starting transfers between devices, shift(): lax.ppermute(value, axis, [(src, (src + steps) % count) for src in range(...  17.7 us
    pallas_call x8, Pallas kernels, call(): pl.pallas_call(kernel, out_shape=outs, in_specs=[spec for _, spec in ins]...  7.46 us
    ppermute x1, starting transfers between devices, local(): right_trace = lax.ppermute(right_own, both, to_trace)  6.32 us
    ppermute x1, waiting for transfers between devices, local(): wanted = lax.ppermute(wanted, both, to_wanted)  3.44 us
    unnamed x16, local copies, waits for them, and re-layouts  2.3 us
  transfers between devices with their start and end apart: 5, of which 1 were waited for; matrix products, arithmetic and copies ran while one was open for 0% of the time, Pallas kernels for 3%

profile of v4, /device:TPU:1, one launch (start us, length us, event | category | flops | bytes accessed | tf_op | source)
XLA Modules:
  0.0 72.6 jit_solution(13314957279668752044)
XLA Ops:
  0.6 0.0 copy-start.1
  0.6 2.9 %pack.1 = (bf16[528,512]{1,0:T(8,128)(2,1)}, bf16[528,512]{1,0:T(8,128)(2,1)}) custom-call(s32[2]{0:T(128)} %bitcast.21, s32[2]{0:T(128)} %bitcast.15, bf16[1024,512]{1,0:T(8,128)(2,1)} %refs_2_.1, bf16[1024,512]{1,0:T(8,128)(2,1)} %refs_3_.1), custom_call_target="tpu_custom_call" | custom-call | tf_op jit(solution)/shard_map/pack/pallas_call | solution.py:19
  3.5 6.3 %collective-permute-start.2 = (bf16[528,512]{1,0:T(8,128)(2,1)}, bf16[528,512]{1,0:T(8,128)(2,1)S(1)}, u32[]{:S(2)}, u32[]{:S(2)}) collective-permute-start(bf16[528,512]{1,0:T(8,128)(2,1)} %get-tuple-element.8.right_own), channel_id=1, source_target_pairs={{32,2},{33,3},{66,36},{67,37},{100,70},{101,71},{134,104},{135,105... | collective-permute-start | bytes 1622024 | tf_op jit(solution)/shard_map/ppermute | solution.py:245
  9.8 0.0 copy-start.5
  9.8 0.0 copy-start.6
  9.8 0.0 copy-start.7
  9.9 8.9 %collective-permute-start = (bf16[528,512]{1,0:T(8,128)(2,1)}, bf16[528,512]{1,0:T(8,128)(2,1)S(1)}, u32[]{:S(2)}, u32[]{:S(2)}) collective-permute-start(bf16[528,512]{1,0:T(8,128)(2,1)} %get-tuple-element.7.own), channel_id=1, source_target_pairs={{0,31},{1,0},{2,1},{3,2},{4,3},{5,4},{6,5},{7,6},{8,7},{9,8},{10,9... | collective-permute-start | bytes 1622024 | tf_op jit(solution)/shard_map/ppermute | solution.py:32
  18.8 0.0 copy-done.1
  18.8 0.0 copy-done.5
  18.8 0.0 copy-done.6
  18.8 0.0 copy-done.7
  18.8 0.0 copy-start.2
  18.8 1.2 %copy-done.2 = bf16[1024,512]{1,0:T(8,128)(2,1)S(1)} copy-done((bf16[1024,512]{1,0:T(8,128)(2,1)S(1)}, bf16[1024,512]{1,0:T(8,128)(2,1)}, u32[]{:S(2)}) %copy-start.2) | copy-done | bytes 1048600
  20.1 0.0 copy-start.4
  20.1 1.0 %copy-done.4 = bf16[528,512]{1,0:T(8,128)(2,1)S(1)} copy-done((bf16[528,512]{1,0:T(8,128)(2,1)S(1)}, bf16[528,512]{1,0:T(8,128)(2,1)}, u32[]{:S(2)}) %copy-start.4) | copy-done | bytes 540696
  21.1 0.6 base.1
  21.7 0.0 copy-start
  21.7 1.4 %collective-permute-start.1 = (s32[8,128]{1,0:T(8,128)S(1)}, s32[8,128]{1,0:T(8,128)S(1)}, u32[]{:S(2)}, u32[]{:S(2)}) collective-permute-start(s32[8,128]{1,0:T(8,128)S(1)} %get-tuple-element.10), channel_id=1, source_target_pairs={{34,4},{35,5},{36,6},{37,7},{38,8},{39,9},{40,10},{41,11},{42,12},... | collective-permute-start | bytes 12296 | tf_op jit(solution)/shard_map/ppermute | solution.py:262
  23.2 4.4 %collective-permute-start.4 = (bf16[528,512]{1,0:T(8,128)(2,1)S(1)}, bf16[528,512]{1,0:T(8,128)(2,1)S(1)}, u32[]{:S(2)}, u32[]{:S(2)}) collective-permute-start(bf16[528,512]{1,0:T(8,128)(2,1)S(1)} %get-tuple-element.9.right_own), channel_id=1, source_target_pairs={{0,480},{32,0},{64,32},{96,64},{128,96},{160,128},{192,160},{224,1... | collective-permute-start | bytes 1622024 | tf_op jit(solution)/shard_map/ppermute | solution.py:32
  27.6 3.4 %collective-permute-done.1.wanted = s32[8,128]{1,0:T(8,128)S(1)} collective-permute-done((s32[8,128]{1,0:T(8,128)S(1)}, s32[8,128]{1,0:T(8,128)S(1)}, u32[]{:S(2)}, u32[]{:S(2)}) %collective-permute-start.1) | collective-permute-done | bytes 4128 | tf_op jit(solution)/shard_map/ppermute | solution.py:262
  31.0 0.0 collective-permute-done.2.right_trace
  31.0 0.0 collective-permute-done.one
  31.0 0.0 copy-done
  31.0 0.2 choose.1.chosen
  31.3 4.4 %collective-permute-start.3 = (bf16[528,512]{1,0:T(8,128)(2,1)S(1)}, bf16[528,512]{1,0:T(8,128)(2,1)S(1)}, u32[]{:S(2)}, u32[]{:S(2)}) collective-permute-start(bf16[528,512]{1,0:T(8,128)(2,1)S(1)} %choose.1.chosen), channel_id=1, source_target_pairs={{0,30},{1,31},{2,0},{3,1},{4,2},{5,3},{6,4},{7,5},{8,6},{9,7},{10,... | collective-permute-start | bytes 1622024 | tf_op jit(solution)/shard_map/ppermute | solution.py:32
  35.7 0.0 copy-start.3
  35.7 0.6 trace.1
  36.3 13.8 %all_to_all.22 = f32[32,1,128]{2,1,0:T(1,128)S(1)} all-to-all(f32[32,1,128]{2,1,0:T(1,128)S(1)} %bitcast.11), channel_id=1, replica_groups=mesh['y'=4,'x_lo'=2,'core'=2,'x_hi'=2,'z'=16] {'y','x_lo','core','x_hi'}, dimensions={0} | all-to-all | bytes 32768 | tf_op jit(solution)/shard_map/all_to_all | solution.py:214
  50.1 19.3 %all_to_all.23 = f32[16,1,128]{2,1,0:T(1,128)S(1)} all-to-all(f32[16,1,128]{2,1,0:T(1,128)S(1)} %bitcast.13), channel_id=1, replica_groups=mesh['y'=4,'x_lo'=2,'core'=2,'x_hi'=2,'z'=16] {'z'}, dimensions={0} | all-to-all | bytes 16384 | tf_op jit(solution)/shard_map/all_to_all | solution.py:214
  69.4 0.7 total.1
  70.1 0.0 collective-permute-done.4.right_next
  70.1 0.0 collective-permute-done.3.two
  70.1 0.0 copy-done.3
  70.1 2.4 %last.1 = bf16[1024,512]{1,0:T(8,128)(2,1)} custom-call(s32[2]{0:T(128)S(1)} %bitcast.18, s32[2]{0:T(128)S(1)} %bitcast.20, s32[2]{0:T(128)S(1)} %copy-done.7, bf16[528,512]{1,0:T(8,128)(2,1)S(1)} %copy-done, bf16[528,512]{1,0:T(8,128)(2,1)S(1)} %collective-permute-done.one, bf16[528,512]{1,0:T(8,128)(2,1)S(1)} %get-tuple-element.9.right_own, ...), custom_call_target="tpu_custom_call" | custom-call | tf_op jit(solution)/shard_map/last/pallas_call | solution.py:19
  (2 shorter events, 0.0 us)
Async XLA Ops:
  0.6 18.2 %copy-start.1 = (bf16[1024,512]{1,0:T(8,128)(2,1)S(1)}, bf16[1024,512]{1,0:T(8,128)(2,1)}, u32[]{:S(2)}) copy-start(bf16[1024,512]{1,0:T(8,128)(2,1)} %earlier.3) | copy-start | bytes 3145732
  3.5 27.5 %collective-permute-start.2 = (bf16[528,512]{1,0:T(8,128)(2,1)}, bf16[528,512]{1,0:T(8,128)(2,1)S(1)}, u32[]{:S(2)}, u32[]{:S(2)}) collective-permute-start(bf16[528,512]{1,0:T(8,128)(2,1)} %get-tuple-element.8.right_own), channel_id=1, source_target_pairs={{32,2},{33,3},{66,36},{67,37},{100,70},{101,71},{134,104},{135,105... | collective-permute-start | bytes 1622024 | tf_op jit(solution)/shard_map/ppermute | solution.py:245
  9.8 9.0 %copy-start.5 = (s32[2,1]{0,1:T(1,128)S(1)}, s32[2,1]{0,1:T(1,128)}, u32[]{:S(2)}) copy-start(s32[2,1]{0,1:T(1,128)} %param.13) | copy-start | bytes 28
  9.8 9.0 %copy-start.6 = (s32[2,1]{0,1:T(1,128)S(1)}, s32[2,1]{0,1:T(1,128)}, u32[]{:S(2)}) copy-start(s32[2,1]{0,1:T(1,128)} %param.14) | copy-start | bytes 28
  9.8 9.0 %copy-start.7 = (s32[2]{0:T(128)S(1)}, s32[2]{0:T(128)}, u32[]{:S(2)}) copy-start(s32[2]{0:T(128)} %branch.3) | copy-start | bytes 28
  9.9 21.2 %collective-permute-start = (bf16[528,512]{1,0:T(8,128)(2,1)}, bf16[528,512]{1,0:T(8,128)(2,1)S(1)}, u32[]{:S(2)}, u32[]{:S(2)}) collective-permute-start(bf16[528,512]{1,0:T(8,128)(2,1)} %get-tuple-element.7.own), channel_id=1, source_target_pairs={{0,31},{1,0},{2,1},{3,2},{4,3},{5,4},{6,5},{7,6},{8,7},{9,8},{10,9... | collective-permute-start | bytes 1622024 | tf_op jit(solution)/shard_map/ppermute | solution.py:32
  18.8 1.2 %copy-start.2 = (bf16[1024,512]{1,0:T(8,128)(2,1)S(1)}, bf16[1024,512]{1,0:T(8,128)(2,1)}, u32[]{:S(2)}) copy-start(bf16[1024,512]{1,0:T(8,128)(2,1)} %density.3) | copy-start | bytes 3145732
  20.1 1.0 %copy-start.4 = (bf16[528,512]{1,0:T(8,128)(2,1)S(1)}, bf16[528,512]{1,0:T(8,128)(2,1)}, u32[]{:S(2)}) copy-start(bf16[528,512]{1,0:T(8,128)(2,1)} %get-tuple-element.8.right_own) | copy-start | bytes 1622020
  21.7 9.3 %copy-start = (bf16[528,512]{1,0:T(8,128)(2,1)S(1)}, bf16[528,512]{1,0:T(8,128)(2,1)}, u32[]{:S(2)}) copy-start(bf16[528,512]{1,0:T(8,128)(2,1)} %get-tuple-element.7.own) | copy-start | bytes 1622020
  21.7 9.3 %collective-permute-start.1 = (s32[8,128]{1,0:T(8,128)S(1)}, s32[8,128]{1,0:T(8,128)S(1)}, u32[]{:S(2)}, u32[]{:S(2)}) collective-permute-start(s32[8,128]{1,0:T(8,128)S(1)} %get-tuple-element.10), channel_id=1, source_target_pairs={{34,4},{35,5},{36,6},{37,7},{38,8},{39,9},{40,10},{41,11},{42,12},... | collective-permute-start | bytes 12296 | tf_op jit(solution)/shard_map/ppermute | solution.py:262
  23.2 46.9 %collective-permute-start.4 = (bf16[528,512]{1,0:T(8,128)(2,1)S(1)}, bf16[528,512]{1,0:T(8,128)(2,1)S(1)}, u32[]{:S(2)}, u32[]{:S(2)}) collective-permute-start(bf16[528,512]{1,0:T(8,128)(2,1)S(1)} %get-tuple-element.9.right_own), channel_id=1, source_target_pairs={{0,480},{32,0},{64,32},{96,64},{128,96},{160,128},{192,160},{224,1... | collective-permute-start | bytes 1622024 | tf_op jit(solution)/shard_map/ppermute | solution.py:32
  31.3 38.8 %collective-permute-start.3 = (bf16[528,512]{1,0:T(8,128)(2,1)S(1)}, bf16[528,512]{1,0:T(8,128)(2,1)S(1)}, u32[]{:S(2)}, u32[]{:S(2)}) collective-permute-start(bf16[528,512]{1,0:T(8,128)(2,1)S(1)} %choose.1.chosen), channel_id=1, source_target_pairs={{0,30},{1,31},{2,0},{3,1},{4,2},{5,3},{6,4},{7,5},{8,6},{9,7},{10,... | collective-permute-start | bytes 1622024 | tf_op jit(solution)/shard_map/ppermute | solution.py:32
  35.7 34.4 %copy-start.3 = (bf16[1024,512]{1,0:T(8,128)(2,1)S(1)}, bf16[1024,512]{1,0:T(8,128)(2,1)}, u32[]{:S(2)}) copy-start(bf16[1024,512]{1,0:T(8,128)(2,1)} %density.3) | copy-start | bytes 3145732

commit v5 on v4

--- a/solution.py
+++ b/solution.py
@@ -33,21 +33,30 @@
 
 
 def pack_kernel(*refs):
-    occupied, panels, packed, (stage, in_sems, out_sems) = refs[:2], refs[2:4], refs[4:6], refs[6:]
-    size = stage.shape[2]
-    loads, stores = [], []
+    occupied, panels, packed, (stage, flags, in_sems, out_sems, flag_sems) = refs[:2], refs[2:4], refs[4:6], refs[6:]
+    size = stage.shape[3]
+    asked = [pltpu.make_async_copy(occupied[side], flags.at[side], flag_sems.at[side]) for side in range(2)]
+    loads = [
+        pltpu.make_async_copy(panels[side].at[pl.ds(half * size, size)], stage.at[side, half, :size], in_sems.at[side, half])
+        for side in range(2)
+        for half in range(2)
+    ]
+    for copy in asked + loads:
+        copy.start()
     for side in range(2):
-        rows = pl.ds(pl.multiple_of(occupied[side][1] * size, size), size)
-        loads.append(pltpu.make_async_copy(panels[side].at[rows], stage.at[side, :size], in_sems.at[side]))
-        loads[side].start()
-    for side in range(2):
+        asked[side].wait()
         lanes = lax.broadcasted_iota(jnp.int32, (FLAG_ROWS, size), 1)
-        flags = [occupied[side][k].astype(jnp.float32) for k in range(2)]
-        stage[side, size:, :] = jnp.where(lanes < size // 2, flags[0], flags[1]).astype(stage.dtype)
-    for side in range(2):
-        loads[side].wait()
-        stores.append(pltpu.make_async_copy(stage.at[side], packed[side], out_sems.at[side]))
-        stores[side].start()
+        values = [flags[side, k].astype(jnp.float32) for k in range(2)]
+        rows = jnp.where(lanes < size // 2, values[0], values[1]).astype(stage.dtype)
+        for half in range(2):
+            stage[side, half, size:, :] = rows
+    for copy in loads:
+        copy.wait()
+    stores = [
+        pltpu.make_async_copy(stage.at[side, flags[side, 1]], packed[side], out_sems.at[side]) for side in range(2)
+    ]
+    for store in stores:
+        store.start()
     for store in stores:
         store.wait()
 
@@ -167,7 +176,7 @@
     spread[...] = jnp.broadcast_to(jnp.sum(parts[...], axis=0, keepdims=True), spread.shape)
 
 
-def total_kernel(order, parts, occupation):
+def total_kernel(order, parts, stored, occupation):
     values = parts[...]
     lanes = lax.broadcasted_iota(jnp.int32, values.shape, 1)
     planes = lax.broadcasted_iota(jnp.int32, (values.shape[0], 1), 0)
@@ -182,10 +191,11 @@
 
 
 def last_kernel(
-    right_occupied, kept, branch, own, one, right_own, two, right_next, earlier, density, out, result, sems
+    right_occupied, kept, branch, own, one, right_own, two, right_next, earlier, density, out, stored, result, sems
 ):
     size = own.shape[1]
     step = size // 4
+    stored[...] = jnp.zeros_like(stored)
     second = right_occupied[1] == 1
     occupied = (right_occupied[0] + right_occupied[1]).astype(jnp.float32)
     first_flags = [jnp.where(second, a, b) * occupied for a, b in zip(flag_pair(one), flag_pair(own))]
@@ -230,10 +240,16 @@
     left_own, right_own = call(
         pack_kernel,
         "pack",
-        [(left_occupied, SMEM), (right_occupied, SMEM), (left_panel, HBM), (right_panel, HBM)],
+        [(left_occupied, HBM), (right_occupied, HBM), (left_panel, HBM), (right_panel, HBM)],
         [payload, payload],
         [HBM, HBM],
-        [pltpu.VMEM((2,) + payload.shape, kind), pltpu.SemaphoreType.DMA((2,)), pltpu.SemaphoreType.DMA((2,))],
+        [
+            pltpu.VMEM((2, 2) + payload.shape, kind),
+            pltpu.SMEM((2, 2), jnp.int32),
+            pltpu.SemaphoreType.DMA((2, 2)),
+            pltpu.SemaphoreType.DMA((2,)),
+            pltpu.SemaphoreType.DMA((2,)),
+        ],
         62 * 2**20,
     )
     left_one = shift(left_own, COL, -1)
@@ -260,7 +276,7 @@
         if j // 2 != i
     ]
     wanted = lax.ppermute(wanted, both, to_wanted)
-    right_next = shift(right_here, ROW, -1)
+    right_next = shift(right_own, ROW, -1)
 
     second = call(
         decide_kernel,
@@ -284,22 +300,22 @@
         middle_kernel, "middle", [(parts, VMEM)], jax.ShapeDtypeStruct((lax.axis_size("z"), LANES), jnp.float32), VMEM
     )
     parts = spread_over(parts, "z")
+    new_density, stored = call(
+        last_kernel,
+        "last",
+        [(right_occupied, SMEM), (kept_tiles, SMEM), (branch, SMEM)]
+        + [(a, VMEM) for a in (left_own, left_one, right_own, left_two, right_next, earlier, density)],
+        [jax.ShapeDtypeStruct((block_rows, size), jnp.bfloat16), jax.ShapeDtypeStruct((8, LANES), jnp.float32)],
+        [HBM, VMEM],
+        [pltpu.VMEM((block_rows, size), kind), pltpu.SemaphoreType.DMA((8,))],
+    )
+
     occupation = call(
         functools.partial(total_kernel, row_count * block_rows),
         "total",
-        [(parts, VMEM)],
+        [(parts, VMEM), (stored, VMEM)],
         jax.ShapeDtypeStruct((1,), jnp.float32),
         SMEM,
-    )
-
-    new_density = call(
-        last_kernel,
-        "last",
-        [(right_occupied, SMEM), (kept_tiles, SMEM), (branch, SMEM)]
-        + [(a, VMEM) for a in (left_own, left_one, right_here, left_two, right_next, earlier, density)],
-        jax.ShapeDtypeStruct((block_rows, size), jnp.bfloat16),
-        HBM,
-        [pltpu.VMEM((block_rows, size), kind), pltpu.SemaphoreType.DMA((8,))],
     )
     return new_density, occupation
 

time: 73 us -> 71.1 us (0.974)
  blocking collectives: 33.1 us -> 13.8 us
  starting transfers between devices: 25.4 us -> 34.1 us
  waiting for transfers between devices: 3.45 us -> 10.2 us
  Pallas kernels: 7.46 us -> 9.16 us
    all_to_all x2 -> x1, blocking collectives: 33.1 us -> 13.8 us  [spread_over(): return lax.all_to_all(rows, axis, 0, 0, tiled=True)]
    all_to_all x0 -> x1, starting transfers between devices: none -> 8.7 us  [spread_over(): return lax.all_to_all(rows, axis, 0, 0, tiled=True)]
    all_to_all x0 -> x1, waiting for transfers between devices: none -> 6.73 us  [spread_over(): return lax.all_to_all(rows, axis, 0, 0, tiled=True)]
    pallas_call x8, Pallas kernels: 7.46 us -> 9.16 us  [call(): pl.pallas_call(kernel, out_shape=outs, in_specs=[spec for _, spec in ins]...]
    unnamed x16 -> x14, local copies, waits for them, and re-layouts: 2.3 us -> 2.47 us
  transfers between devices with their start and end apart: 5 -> 6, of which waited for: 1 -> 2; matrix products, arithmetic and copies ran while one was open for 0% -> 0% of each run, Pallas kernels for 3% -> 8%
where the time goes in v5:
time: 71.1 us; the launch traced here: 70.6 us
  starting transfers between devices  34.1 us (48%)
  blocking collectives  13.8 us (19%)
  waiting for transfers between devices  10.2 us (14%)
  Pallas kernels  9.16 us (13%)
  local copies, waits for them, and re-layouts  2.47 us (3%)
  between operations  0.84 us (1%)
    ppermute x3, starting transfers between devices, shift(): lax.ppermute(value, axis, [(src, (src + steps) % count) for src in range(...  17.7 us
    all_to_all x1, blocking collectives, spread_over(): return lax.all_to_all(rows, axis, 0, 0, tiled=True)  13.8 us
    pallas_call x8, Pallas kernels, call(): pl.pallas_call(kernel, out_shape=outs, in_specs=[spec for _, spec in ins]...  9.16 us
    all_to_all x1, starting transfers between devices, spread_over(): return lax.all_to_all(rows, axis, 0, 0, tiled=True)  8.7 us
    all_to_all x1, waiting for transfers between devices, spread_over(): return lax.all_to_all(rows, axis, 0, 0, tiled=True)  6.73 us
    ppermute x1, starting transfers between devices, local(): right_trace = lax.ppermute(right_own, both, to_trace)  6.32 us
    ppermute x1, waiting for transfers between devices, local(): wanted = lax.ppermute(wanted, both, to_wanted)  3.44 us
    unnamed x14, local copies, waits for them, and re-layouts  2.47 us
  transfers between devices with their start and end apart: 6, of which 2 were waited for; matrix products, arithmetic and copies ran while one was open for 0% of the time, Pallas kernels for 8%

profile of v5, /device:TPU:1, one launch (start us, length us, event | category | flops | bytes accessed | tf_op | source)
XLA Modules:
  0.0 70.6 jit_solution(8972390699007097740)
XLA Ops:
  0.6 0.0 copy-start.1
  0.6 2.6 %pack.1 = (bf16[528,512]{1,0:T(8,128)(2,1)}, bf16[528,512]{1,0:T(8,128)(2,1)}) custom-call(s32[2]{0:T(128)} %bitcast.20, s32[2]{0:T(128)} %bitcast.14, bf16[1024,512]{1,0:T(8,128)(2,1)} %refs_2_.1, bf16[1024,512]{1,0:T(8,128)(2,1)} %refs_3_.1), custom_call_target="tpu_custom_call" | custom-call | tf_op jit(solution)/shard_map/pack/pallas_call | solution.py:19
  3.3 6.3 %collective-permute-start.2 = (bf16[528,512]{1,0:T(8,128)(2,1)}, bf16[528,512]{1,0:T(8,128)(2,1)S(1)}, u32[]{:S(2)}, u32[]{:S(2)}) collective-permute-start(bf16[528,512]{1,0:T(8,128)(2,1)} %get-tuple-element.10.right_own), channel_id=1, source_target_pairs={{32,2},{33,3},{66,36},{67,37},{100,70},{101,71},{134,104},{135,105... | collective-permute-start | bytes 1622024 | tf_op jit(solution)/shard_map/ppermute | solution.py:261
  9.6 0.0 copy-start.4
  9.6 0.0 copy-start.5
  9.6 0.0 copy-start.6
  9.7 8.9 %collective-permute-start = (bf16[528,512]{1,0:T(8,128)(2,1)}, bf16[528,512]{1,0:T(8,128)(2,1)S(1)}, u32[]{:S(2)}, u32[]{:S(2)}) collective-permute-start(bf16[528,512]{1,0:T(8,128)(2,1)} %get-tuple-element.9.own), channel_id=1, source_target_pairs={{0,31},{1,0},{2,1},{3,2},{4,3},{5,4},{6,5},{7,6},{8,7},{9,8},{10,9... | collective-permute-start | bytes 1622024 | tf_op jit(solution)/shard_map/ppermute | solution.py:32
  18.6 0.0 copy-done.1
  18.6 0.0 copy-done.4
  18.6 0.0 copy-done.5
  18.6 0.0 copy-done.6
  18.6 0.0 copy-start.2
  18.6 1.2 %copy-done.2 = bf16[1024,512]{1,0:T(8,128)(2,1)S(1)} copy-done((bf16[1024,512]{1,0:T(8,128)(2,1)S(1)}, bf16[1024,512]{1,0:T(8,128)(2,1)}, u32[]{:S(2)}) %copy-start.2) | copy-done | bytes 1048600
  19.9 1.1 %base.1 = (f32[8,128]{1,0:T(8,128)S(1)}, s32[8,128]{1,0:T(8,128)S(1)}, bf16[528,512]{1,0:T(8,128)(2,1)S(1)}) custom-call(s32[2]{0:T(128)S(1)} %bitcast.15, s32[2]{0:T(128)S(1)} %bitcast.18, s32[2]{0:T(128)S(1)} %copy-done.6, bf16[528,512]{1,0:T(8,128)(2,1)} %get-tuple-element.10.right_own, bf16[1024,512]{1,0:T(8,128)(2,1)S(1)} %copy-done.1, ...), custom_call_target="tpu_custom_call" | custom-call | tf_op jit(solution)/shard_map/base/pallas_call | solution.py:19
  21.0 0.0 copy-start
  21.0 1.4 %collective-permute-start.1 = (s32[8,128]{1,0:T(8,128)S(1)}, s32[8,128]{1,0:T(8,128)S(1)}, u32[]{:S(2)}, u32[]{:S(2)}) collective-permute-start(s32[8,128]{1,0:T(8,128)S(1)} %get-tuple-element.11), channel_id=1, source_target_pairs={{34,4},{35,5},{36,6},{37,7},{38,8},{39,9},{40,10},{41,11},{42,12},... | collective-permute-start | bytes 12296 | tf_op jit(solution)/shard_map/ppermute | solution.py:278
  22.4 4.4 %collective-permute-start.4 = (bf16[528,512]{1,0:T(8,128)(2,1)}, bf16[528,512]{1,0:T(8,128)(2,1)}, u32[]{:S(2)}, u32[]{:S(2)}) collective-permute-start(bf16[528,512]{1,0:T(8,128)(2,1)} %get-tuple-element.10.right_own), channel_id=1, source_target_pairs={{0,480},{32,0},{64,32},{96,64},{128,96},{160,128},{192,160},{224,1... | collective-permute-start | bytes 1622024 | tf_op jit(solution)/shard_map/ppermute | solution.py:32
  26.8 3.4 %collective-permute-done.1.wanted = s32[8,128]{1,0:T(8,128)S(1)} collective-permute-done((s32[8,128]{1,0:T(8,128)S(1)}, s32[8,128]{1,0:T(8,128)S(1)}, u32[]{:S(2)}, u32[]{:S(2)}) %collective-permute-start.1) | collective-permute-done | bytes 4128 | tf_op jit(solution)/shard_map/ppermute | solution.py:278
  30.3 0.0 collective-permute-done.2.right_trace
  30.3 0.0 collective-permute-done.one
  30.3 0.0 copy-done
  30.3 0.2 choose.1.chosen
  30.5 4.4 %collective-permute-start.3 = (bf16[528,512]{1,0:T(8,128)(2,1)S(1)}, bf16[528,512]{1,0:T(8,128)(2,1)}, u32[]{:S(2)}, u32[]{:S(2)}) collective-permute-start(bf16[528,512]{1,0:T(8,128)(2,1)S(1)} %choose.1.chosen), channel_id=1, source_target_pairs={{0,30},{1,31},{2,0},{3,1},{4,2},{5,3},{6,4},{7,5},{8,6},{9,7},{10,... | collective-permute-start | bytes 1622024 | tf_op jit(solution)/shard_map/ppermute | solution.py:32
  34.9 0.6 trace.1
  35.5 13.8 %all_to_all.22 = f32[32,1,128]{2,1,0:T(1,128)S(1)} all-to-all(f32[32,1,128]{2,1,0:T(1,128)S(1)} %bitcast.11), channel_id=1, replica_groups=mesh['y'=4,'x_lo'=2,'core'=2,'x_hi'=2,'z'=16] {'y','x_lo','core','x_hi'}, dimensions={0} | all-to-all | bytes 32768 | tf_op jit(solution)/shard_map/all_to_all | solution.py:224
  49.3 0.6 middle.1
  49.9 8.7 %all-to-all-start.1 = ((f32[16,1,128]{2,1,0:T(1,128)}), f32[16,1,128]{2,1,0:T(1,128)S(1)}, u32[]{:S(2)}, u32[]{:S(2)}) async-start(f32[16,1,128]{2,1,0:T(1,128)} %bitcast.7), calls=%async_computation.1 | async-start | bytes 16384 | tf_op jit(solution)/shard_map/all_to_all | solution.py:224
  58.6 0.0 collective-permute-done.4.right_next
  58.6 0.0 collective-permute-done.3.two
  58.7 0.0 copy-start.3
  58.7 1.2 %copy-done.3 = bf16[1024,512]{1,0:T(8,128)(2,1)S(1)} copy-done((bf16[1024,512]{1,0:T(8,128)(2,1)S(1)}, bf16[1024,512]{1,0:T(8,128)(2,1)}, u32[]{:S(2)}) %copy-start.3) | copy-done | bytes 1048600
  59.9 3.3 %last.1 = (bf16[1024,512]{1,0:T(8,128)(2,1)}, f32[8,128]{1,0:T(8,128)S(1)}) custom-call(s32[2]{0:T(128)S(1)} %bitcast.17, s32[2]{0:T(128)S(1)} %bitcast.19, s32[2]{0:T(128)S(1)} %copy-done.6, bf16[528,512]{1,0:T(8,128)(2,1)S(1)} %copy-done, bf16[528,512]{1,0:T(8,128)(2,1)S(1)} %collective-permute-done.one, bf16[528,512]{1,0:T(8,128)(2,1)} %get-tuple-element.10.right_own, ...), custom_call_target="tpu_custom_call" | custom-call | tf_op jit(solution)/shard_map/last/pallas_call | solution.py:19
  63.1 6.7 %all-to-all-done.1 = f32[16,1,128]{2,1,0:T(1,128)S(1)} async-done(((f32[16,1,128]{2,1,0:T(1,128)}), f32[16,1,128]{2,1,0:T(1,128)S(1)}, u32[]{:S(2)}, u32[]{:S(2)}) %all-to-all-start.1) | async-done | bytes 8224 | tf_op jit(solution)/shard_map/all_to_all | solution.py:224
  69.9 0.7 %total.1 = f32[1]{0:T(128)} custom-call(f32[16,128]{1,0:T(8,128)S(1)} %bitcast.13, f32[8,128]{1,0:T(8,128)S(1)} %get-tuple-element.15.stored), custom_call_target="tpu_custom_call" | custom-call | tf_op jit(solution)/shard_map/total/pallas_call | solution.py:19
  (1 shorter events, 0.0 us)
Async XLA Ops:
  0.6 18.0 %copy-start.1 = (bf16[1024,512]{1,0:T(8,128)(2,1)S(1)}, bf16[1024,512]{1,0:T(8,128)(2,1)}, u32[]{:S(2)}) copy-start(bf16[1024,512]{1,0:T(8,128)(2,1)} %earlier.3) | copy-start | bytes 3145732
  3.3 27.0 %collective-permute-start.2 = (bf16[528,512]{1,0:T(8,128)(2,1)}, bf16[528,512]{1,0:T(8,128)(2,1)S(1)}, u32[]{:S(2)}, u32[]{:S(2)}) collective-permute-start(bf16[528,512]{1,0:T(8,128)(2,1)} %get-tuple-element.10.right_own), channel_id=1, source_target_pairs={{32,2},{33,3},{66,36},{67,37},{100,70},{101,71},{134,104},{135,105... | collective-permute-start | bytes 1622024 | tf_op jit(solution)/shard_map/ppermute | solution.py:261
  9.6 9.0 %copy-start.4 = (s32[2,1]{0,1:T(1,128)S(1)}, s32[2,1]{0,1:T(1,128)}, u32[]{:S(2)}) copy-start(s32[2,1]{0,1:T(1,128)} %param.13) | copy-start | bytes 28
  9.6 9.0 %copy-start.5 = (s32[2,1]{0,1:T(1,128)S(1)}, s32[2,1]{0,1:T(1,128)}, u32[]{:S(2)}) copy-start(s32[2,1]{0,1:T(1,128)} %param.14) | copy-start | bytes 28
  9.6 9.0 %copy-start.6 = (s32[2]{0:T(128)S(1)}, s32[2]{0:T(128)}, u32[]{:S(2)}) copy-start(s32[2]{0:T(128)} %branch.3) | copy-start | bytes 28
  9.7 20.6 %collective-permute-start = (bf16[528,512]{1,0:T(8,128)(2,1)}, bf16[528,512]{1,0:T(8,128)(2,1)S(1)}, u32[]{:S(2)}, u32[]{:S(2)}) collective-permute-start(bf16[528,512]{1,0:T(8,128)(2,1)} %get-tuple-element.9.own), channel_id=1, source_target_pairs={{0,31},{1,0},{2,1},{3,2},{4,3},{5,4},{6,5},{7,6},{8,7},{9,8},{10,9... | collective-permute-start | bytes 1622024 | tf_op jit(solution)/shard_map/ppermute | solution.py:32
  18.6 1.2 %copy-start.2 = (bf16[1024,512]{1,0:T(8,128)(2,1)S(1)}, bf16[1024,512]{1,0:T(8,128)(2,1)}, u32[]{:S(2)}) copy-start(bf16[1024,512]{1,0:T(8,128)(2,1)} %density.3) | copy-start | bytes 3145732
  21.0 9.3 %copy-start = (bf16[528,512]{1,0:T(8,128)(2,1)S(1)}, bf16[528,512]{1,0:T(8,128)(2,1)}, u32[]{:S(2)}) copy-start(bf16[528,512]{1,0:T(8,128)(2,1)} %get-tuple-element.9.own) | copy-start | bytes 1622020
  21.0 9.3 %collective-permute-start.1 = (s32[8,128]{1,0:T(8,128)S(1)}, s32[8,128]{1,0:T(8,128)S(1)}, u32[]{:S(2)}, u32[]{:S(2)}) collective-permute-start(s32[8,128]{1,0:T(8,128)S(1)} %get-tuple-element.11), channel_id=1, source_target_pairs={{34,4},{35,5},{36,6},{37,7},{38,8},{39,9},{40,10},{41,11},{42,12},... | collective-permute-start | bytes 12296 | tf_op jit(solution)/shard_map/ppermute | solution.py:278
  22.4 36.2 %collective-permute-start.4 = (bf16[528,512]{1,0:T(8,128)(2,1)}, bf16[528,512]{1,0:T(8,128)(2,1)}, u32[]{:S(2)}, u32[]{:S(2)}) collective-permute-start(bf16[528,512]{1,0:T(8,128)(2,1)} %get-tuple-element.10.right_own), channel_id=1, source_target_pairs={{0,480},{32,0},{64,32},{96,64},{128,96},{160,128},{192,160},{224,1... | collective-permute-start | bytes 1622024 | tf_op jit(solution)/shard_map/ppermute | solution.py:32
  30.5 28.1 %collective-permute-start.3 = (bf16[528,512]{1,0:T(8,128)(2,1)S(1)}, bf16[528,512]{1,0:T(8,128)(2,1)}, u32[]{:S(2)}, u32[]{:S(2)}) collective-permute-start(bf16[528,512]{1,0:T(8,128)(2,1)S(1)} %choose.1.chosen), channel_id=1, source_target_pairs={{0,30},{1,31},{2,0},{3,1},{4,2},{5,3},{6,4},{7,5},{8,6},{9,7},{10,... | collective-permute-start | bytes 1622024 | tf_op jit(solution)/shard_map/ppermute | solution.py:32
  49.9 19.9 %all-to-all-start.1 = ((f32[16,1,128]{2,1,0:T(1,128)}), f32[16,1,128]{2,1,0:T(1,128)S(1)}, u32[]{:S(2)}, u32[]{:S(2)}) async-start(f32[16,1,128]{2,1,0:T(1,128)} %bitcast.7), calls=%async_computation.1 | async-start | bytes 16384 | tf_op jit(solution)/shard_map/all_to_all | solution.py:224
  58.7 1.2 %copy-start.3 = (bf16[1024,512]{1,0:T(8,128)(2,1)S(1)}, bf16[1024,512]{1,0:T(8,128)(2,1)}, u32[]{:S(2)}) copy-start(bf16[1024,512]{1,0:T(8,128)(2,1)} %density.3) | copy-start | bytes 3145732

commit v6 on v5

--- a/solution.py
+++ b/solution.py
@@ -134,7 +134,7 @@
         second[...] = jnp.broadcast_to(flag, second.shape)
 
 
-def choose_kernel(second, own, one, chosen):
+def choose_kernel(second, own, one, parts, chosen):
     use_one = jnp.max(second[...]) == 1
 
     @pl.when(use_one)
@@ -146,7 +146,7 @@
         chosen[...] = own[...]
 
 
-def trace_kernel(right_occupied, own, one, chosen, right_own, right_trace, base, parts):
+def trace_kernel(right_occupied, own, one, right_own, right_trace, base, parts):
     size = own.shape[1]
     row, col = lax.axis_index(ROW), lax.axis_index(COL)
     half = lax.rem(col, 2)
@@ -166,8 +166,10 @@
 
     @pl.when(far_here())
     def _far():
-        value = product_trace(lambda part: chosen[part, :], right_trace, size)
-        flags, right_flags = flag_pair(chosen), flag_pair(right_trace)
+        right_flags = flag_pair(right_trace)
+        second = jnp.max(right_flags[1]) == 1.0
+        value = product_trace(lambda part: jnp.where(second, one[part, :], own[part, :]), right_trace, size)
+        flags = [jnp.where(second, a, b) for a, b in zip(flag_pair(one), flag_pair(own))]
         value = value * jnp.where(half == 1, flags[1], flags[0]) * (right_flags[0] + right_flags[1])
         parts[...] += jnp.where(lanes == 1 + lax.axis_index("x_hi"), value, 0.0)
 
@@ -285,16 +287,16 @@
         jax.ShapeDtypeStruct((8, LANES), jnp.int32),
         VMEM,
     )
-    chosen = call(choose_kernel, "choose", [(a, VMEM) for a in (second, left_own, left_one)], payload, VMEM)
-    left_two = shift(chosen, COL, -2)
-
     parts = call(
         trace_kernel,
         "trace",
-        [(right_occupied, SMEM)] + [(a, VMEM) for a in (left_own, left_one, chosen, right_here, right_trace, base)],
+        [(right_occupied, SMEM)] + [(a, VMEM) for a in (left_own, left_one, right_here, right_trace, base)],
         jax.ShapeDtypeStruct((lax.axis_size(PLANE), LANES), jnp.float32),
         VMEM,
     )
+
+    chosen = call(choose_kernel, "choose", [(a, VMEM) for a in (second, left_own, left_one, parts)], payload, VMEM)
+    left_two = shift(chosen, COL, -2)
     parts = spread_over(parts, PLANE)
     parts = call(
         middle_kernel, "middle", [(parts, VMEM)], jax.ShapeDtypeStruct((lax.axis_size("z"), LANES), jnp.float32), VMEM

time: 71.1 us -> 70.6 us (level)
  no operation moved by 1% of the time
where the time goes in v6:
time: 70.6 us; the launch traced here: 70.1 us
  starting transfers between devices  34.1 us (48%)
  blocking collectives  13.4 us (19%)
  waiting for transfers between devices  10.2 us (14%)
  Pallas kernels  9.17 us (13%)
  local copies, waits for them, and re-layouts  2.47 us (3%)
  between operations  0.84 us (1%)
    ppermute x3, starting transfers between devices, shift(): lax.ppermute(value, axis, [(src, (src + steps) % count) for src in range(...  17.7 us
    all_to_all x1, blocking collectives, spread_over(): return lax.all_to_all(rows, axis, 0, 0, tiled=True)  13.4 us
    pallas_call x8, Pallas kernels, call(): pl.pallas_call(kernel, out_shape=outs, in_specs=[spec for _, spec in ins]...  9.17 us
    all_to_all x1, starting transfers between devices, spread_over(): return lax.all_to_all(rows, axis, 0, 0, tiled=True)  8.61 us
    all_to_all x1, waiting for transfers between devices, spread_over(): return lax.all_to_all(rows, axis, 0, 0, tiled=True)  6.72 us
    ppermute x1, starting transfers between devices, local(): right_trace = lax.ppermute(right_own, both, to_trace)  6.32 us
    ppermute x1, waiting for transfers between devices, local(): wanted = lax.ppermute(wanted, both, to_wanted)  3.44 us
    unnamed x14, local copies, waits for them, and re-layouts  2.47 us
  transfers between devices with their start and end apart: 6, of which 2 were waited for; matrix products, arithmetic and copies ran while one was open for 0% of the time, Pallas kernels for 8%

profile of v6, /device:TPU:1, one launch (start us, length us, event | category | flops | bytes accessed | tf_op | source)
XLA Modules:
  0.0 70.1 jit_solution(15665770713504446705)
XLA Ops:
  0.6 0.0 copy-start.1
  0.6 2.6 %pack.1 = (bf16[528,512]{1,0:T(8,128)(2,1)}, bf16[528,512]{1,0:T(8,128)(2,1)}) custom-call(s32[2]{0:T(128)} %bitcast.20, s32[2]{0:T(128)} %bitcast.14, bf16[1024,512]{1,0:T(8,128)(2,1)} %refs_2_.1, bf16[1024,512]{1,0:T(8,128)(2,1)} %refs_3_.1), custom_call_target="tpu_custom_call" | custom-call | tf_op jit(solution)/shard_map/pack/pallas_call | solution.py:19
  3.3 6.3 %collective-permute-start.2 = (bf16[528,512]{1,0:T(8,128)(2,1)}, bf16[528,512]{1,0:T(8,128)(2,1)S(1)}, u32[]{:S(2)}, u32[]{:S(2)}) collective-permute-start(bf16[528,512]{1,0:T(8,128)(2,1)} %get-tuple-element.10.right_own), channel_id=1, source_target_pairs={{32,2},{33,3},{66,36},{67,37},{100,70},{101,71},{134,104},{135,105... | collective-permute-start | bytes 1622024 | tf_op jit(solution)/shard_map/ppermute | solution.py:263
  9.6 0.0 copy-start.4
  9.6 0.0 copy-start.5
  9.6 0.0 copy-start.6
  9.7 8.9 %collective-permute-start = (bf16[528,512]{1,0:T(8,128)(2,1)}, bf16[528,512]{1,0:T(8,128)(2,1)S(1)}, u32[]{:S(2)}, u32[]{:S(2)}) collective-permute-start(bf16[528,512]{1,0:T(8,128)(2,1)} %get-tuple-element.9.own), channel_id=1, source_target_pairs={{0,31},{1,0},{2,1},{3,2},{4,3},{5,4},{6,5},{7,6},{8,7},{9,8},{10,9... | collective-permute-start | bytes 1622024 | tf_op jit(solution)/shard_map/ppermute | solution.py:32
  18.6 0.0 copy-done.1
  18.6 0.0 copy-done.4
  18.6 0.0 copy-done.5
  18.6 0.0 copy-done.6
  18.6 0.0 copy-start.2
  18.6 1.2 %copy-done.2 = bf16[1024,512]{1,0:T(8,128)(2,1)S(1)} copy-done((bf16[1024,512]{1,0:T(8,128)(2,1)S(1)}, bf16[1024,512]{1,0:T(8,128)(2,1)}, u32[]{:S(2)}) %copy-start.2) | copy-done | bytes 1048600
  19.9 1.1 %base.1 = (f32[8,128]{1,0:T(8,128)S(1)}, s32[8,128]{1,0:T(8,128)S(1)}, bf16[528,512]{1,0:T(8,128)(2,1)S(1)}) custom-call(s32[2]{0:T(128)S(1)} %bitcast.15, s32[2]{0:T(128)S(1)} %bitcast.18, s32[2]{0:T(128)S(1)} %copy-done.6, bf16[528,512]{1,0:T(8,128)(2,1)} %get-tuple-element.10.right_own, bf16[1024,512]{1,0:T(8,128)(2,1)S(1)} %copy-done.1, ...), custom_call_target="tpu_custom_call" | custom-call | tf_op jit(solution)/shard_map/base/pallas_call | solution.py:19
  21.0 0.0 copy-start
  21.0 1.4 %collective-permute-start.1 = (s32[8,128]{1,0:T(8,128)S(1)}, s32[8,128]{1,0:T(8,128)S(1)}, u32[]{:S(2)}, u32[]{:S(2)}) collective-permute-start(s32[8,128]{1,0:T(8,128)S(1)} %get-tuple-element.11), channel_id=1, source_target_pairs={{34,4},{35,5},{36,6},{37,7},{38,8},{39,9},{40,10},{41,11},{42,12},... | collective-permute-start | bytes 12296 | tf_op jit(solution)/shard_map/ppermute | solution.py:280
  22.4 4.4 %collective-permute-start.4 = (bf16[528,512]{1,0:T(8,128)(2,1)}, bf16[528,512]{1,0:T(8,128)(2,1)}, u32[]{:S(2)}, u32[]{:S(2)}) collective-permute-start(bf16[528,512]{1,0:T(8,128)(2,1)} %get-tuple-element.10.right_own), channel_id=1, source_target_pairs={{0,480},{32,0},{64,32},{96,64},{128,96},{160,128},{192,160},{224,1... | collective-permute-start | bytes 1622024 | tf_op jit(solution)/shard_map/ppermute | solution.py:32
  26.8 3.4 %collective-permute-done.1.wanted = s32[8,128]{1,0:T(8,128)S(1)} collective-permute-done((s32[8,128]{1,0:T(8,128)S(1)}, s32[8,128]{1,0:T(8,128)S(1)}, u32[]{:S(2)}, u32[]{:S(2)}) %collective-permute-start.1) | collective-permute-done | bytes 4128 | tf_op jit(solution)/shard_map/ppermute | solution.py:280
  30.3 0.0 collective-permute-done.2.right_trace
  30.3 0.0 collective-permute-done.one
  30.3 0.0 copy-done
  30.3 0.6 trace.1.parts
  30.9 0.2 choose.1
  31.1 4.4 %collective-permute-start.3 = (bf16[528,512]{1,0:T(8,128)(2,1)S(1)}, bf16[528,512]{1,0:T(8,128)(2,1)}, u32[]{:S(2)}, u32[]{:S(2)}) collective-permute-start(bf16[528,512]{1,0:T(8,128)(2,1)S(1)} %choose.1), channel_id=1, source_target_pairs={{0,30},{1,31},{2,0},{3,1},{4,2},{5,3},{6,4},{7,5},{8,6},{9,7},{10,... | collective-permute-start | bytes 1622024 | tf_op jit(solution)/shard_map/ppermute | solution.py:32
  35.5 13.4 %all_to_all.22 = f32[32,1,128]{2,1,0:T(1,128)S(1)} all-to-all(f32[32,1,128]{2,1,0:T(1,128)S(1)} %bitcast.11), channel_id=1, replica_groups=mesh['y'=4,'x_lo'=2,'core'=2,'x_hi'=2,'z'=16] {'y','x_lo','core','x_hi'}, dimensions={0} | all-to-all | bytes 32768 | tf_op jit(solution)/shard_map/all_to_all | solution.py:226
  48.9 0.6 middle.1
  49.5 8.6 %all-to-all-start.1 = ((f32[16,1,128]{2,1,0:T(1,128)}), f32[16,1,128]{2,1,0:T(1,128)S(1)}, u32[]{:S(2)}, u32[]{:S(2)}) async-start(f32[16,1,128]{2,1,0:T(1,128)} %bitcast.7), calls=%async_computation.1 | async-start | bytes 16384 | tf_op jit(solution)/shard_map/all_to_all | solution.py:226
  58.2 0.0 collective-permute-done.4.right_next
  58.2 0.0 collective-permute-done.3.two
  58.2 0.0 copy-start.3
  58.2 1.2 %copy-done.3 = bf16[1024,512]{1,0:T(8,128)(2,1)S(1)} copy-done((bf16[1024,512]{1,0:T(8,128)(2,1)S(1)}, bf16[1024,512]{1,0:T(8,128)(2,1)}, u32[]{:S(2)}) %copy-start.3) | copy-done | bytes 1048600
  59.4 3.3 %last.1 = (bf16[1024,512]{1,0:T(8,128)(2,1)}, f32[8,128]{1,0:T(8,128)S(1)}) custom-call(s32[2]{0:T(128)S(1)} %bitcast.17, s32[2]{0:T(128)S(1)} %bitcast.19, s32[2]{0:T(128)S(1)} %copy-done.6, bf16[528,512]{1,0:T(8,128)(2,1)S(1)} %copy-done, bf16[528,512]{1,0:T(8,128)(2,1)S(1)} %collective-permute-done.one, bf16[528,512]{1,0:T(8,128)(2,1)} %get-tuple-element.10.right_own, ...), custom_call_target="tpu_custom_call" | custom-call | tf_op jit(solution)/shard_map/last/pallas_call | solution.py:19
  62.7 6.7 %all-to-all-done.1 = f32[16,1,128]{2,1,0:T(1,128)S(1)} async-done(((f32[16,1,128]{2,1,0:T(1,128)}), f32[16,1,128]{2,1,0:T(1,128)S(1)}, u32[]{:S(2)}, u32[]{:S(2)}) %all-to-all-start.1) | async-done | bytes 8224 | tf_op jit(solution)/shard_map/all_to_all | solution.py:226
  69.4 0.7 %total.1 = f32[1]{0:T(128)} custom-call(f32[16,128]{1,0:T(8,128)S(1)} %bitcast.13, f32[8,128]{1,0:T(8,128)S(1)} %get-tuple-element.15.stored), custom_call_target="tpu_custom_call" | custom-call | tf_op jit(solution)/shard_map/total/pallas_call | solution.py:19
  (1 shorter events, 0.0 us)
Async XLA Ops:
  0.6 18.0 %copy-start.1 = (bf16[1024,512]{1,0:T(8,128)(2,1)S(1)}, bf16[1024,512]{1,0:T(8,128)(2,1)}, u32[]{:S(2)}) copy-start(bf16[1024,512]{1,0:T(8,128)(2,1)} %earlier.3) | copy-start | bytes 3145732
  3.3 27.0 %collective-permute-start.2 = (bf16[528,512]{1,0:T(8,128)(2,1)}, bf16[528,512]{1,0:T(8,128)(2,1)S(1)}, u32[]{:S(2)}, u32[]{:S(2)}) collective-permute-start(bf16[528,512]{1,0:T(8,128)(2,1)} %get-tuple-element.10.right_own), channel_id=1, source_target_pairs={{32,2},{33,3},{66,36},{67,37},{100,70},{101,71},{134,104},{135,105... | collective-permute-start | bytes 1622024 | tf_op jit(solution)/shard_map/ppermute | solution.py:263
  9.6 9.0 %copy-start.4 = (s32[2,1]{0,1:T(1,128)S(1)}, s32[2,1]{0,1:T(1,128)}, u32[]{:S(2)}) copy-start(s32[2,1]{0,1:T(1,128)} %param.13) | copy-start | bytes 28
  9.6 9.0 %copy-start.5 = (s32[2,1]{0,1:T(1,128)S(1)}, s32[2,1]{0,1:T(1,128)}, u32[]{:S(2)}) copy-start(s32[2,1]{0,1:T(1,128)} %param.14) | copy-start | bytes 28
  9.6 9.0 %copy-start.6 = (s32[2]{0:T(128)S(1)}, s32[2]{0:T(128)}, u32[]{:S(2)}) copy-start(s32[2]{0:T(128)} %branch.3) | copy-start | bytes 28
  9.7 20.6 %collective-permute-start = (bf16[528,512]{1,0:T(8,128)(2,1)}, bf16[528,512]{1,0:T(8,128)(2,1)S(1)}, u32[]{:S(2)}, u32[]{:S(2)}) collective-permute-start(bf16[528,512]{1,0:T(8,128)(2,1)} %get-tuple-element.9.own), channel_id=1, source_target_pairs={{0,31},{1,0},{2,1},{3,2},{4,3},{5,4},{6,5},{7,6},{8,7},{9,8},{10,9... | collective-permute-start | bytes 1622024 | tf_op jit(solution)/shard_map/ppermute | solution.py:32
  18.6 1.2 %copy-start.2 = (bf16[1024,512]{1,0:T(8,128)(2,1)S(1)}, bf16[1024,512]{1,0:T(8,128)(2,1)}, u32[]{:S(2)}) copy-start(bf16[1024,512]{1,0:T(8,128)(2,1)} %density.3) | copy-start | bytes 3145732
  21.0 9.3 %copy-start = (bf16[528,512]{1,0:T(8,128)(2,1)S(1)}, bf16[528,512]{1,0:T(8,128)(2,1)}, u32[]{:S(2)}) copy-start(bf16[528,512]{1,0:T(8,128)(2,1)} %get-tuple-element.9.own) | copy-start | bytes 1622020
  21.0 9.3 %collective-permute-start.1 = (s32[8,128]{1,0:T(8,128)S(1)}, s32[8,128]{1,0:T(8,128)S(1)}, u32[]{:S(2)}, u32[]{:S(2)}) collective-permute-start(s32[8,128]{1,0:T(8,128)S(1)} %get-tuple-element.11), channel_id=1, source_target_pairs={{34,4},{35,5},{36,6},{37,7},{38,8},{39,9},{40,10},{41,11},{42,12},... | collective-permute-start | bytes 12296 | tf_op jit(solution)/shard_map/ppermute | solution.py:280
  22.4 35.8 %collective-permute-start.4 = (bf16[528,512]{1,0:T(8,128)(2,1)}, bf16[528,512]{1,0:T(8,128)(2,1)}, u32[]{:S(2)}, u32[]{:S(2)}) collective-permute-start(bf16[528,512]{1,0:T(8,128)(2,1)} %get-tuple-element.10.right_own), channel_id=1, source_target_pairs={{0,480},{32,0},{64,32},{96,64},{128,96},{160,128},{192,160},{224,1... | collective-permute-start | bytes 1622024 | tf_op jit(solution)/shard_map/ppermute | solution.py:32
  31.1 27.1 %collective-permute-start.3 = (bf16[528,512]{1,0:T(8,128)(2,1)S(1)}, bf16[528,512]{1,0:T(8,128)(2,1)}, u32[]{:S(2)}, u32[]{:S(2)}) collective-permute-start(bf16[528,512]{1,0:T(8,128)(2,1)S(1)} %choose.1), channel_id=1, source_target_pairs={{0,30},{1,31},{2,0},{3,1},{4,2},{5,3},{6,4},{7,5},{8,6},{9,7},{10,... | collective-permute-start | bytes 1622024 | tf_op jit(solution)/shard_map/ppermute | solution.py:32
  49.5 19.9 %all-to-all-start.1 = ((f32[16,1,128]{2,1,0:T(1,128)}), f32[16,1,128]{2,1,0:T(1,128)S(1)}, u32[]{:S(2)}, u32[]{:S(2)}) async-start(f32[16,1,128]{2,1,0:T(1,128)} %bitcast.7), calls=%async_computation.1 | async-start | bytes 16384 | tf_op jit(solution)/shard_map/all_to_all | solution.py:226
  58.2 1.2 %copy-start.3 = (bf16[1024,512]{1,0:T(8,128)(2,1)S(1)}, bf16[1024,512]{1,0:T(8,128)(2,1)}, u32[]{:S(2)}) copy-start(bf16[1024,512]{1,0:T(8,128)(2,1)} %density.3) | copy-start | bytes 3145732

commit v7 on v6

--- a/solution.py
+++ b/solution.py
@@ -146,7 +146,7 @@
         chosen[...] = own[...]
 
 
-def trace_kernel(right_occupied, own, one, right_own, right_trace, base, parts):
+def trace_kernel(own, one, right_own, right_trace, base, parts):
     size = own.shape[1]
     row, col = lax.axis_index(ROW), lax.axis_index(COL)
     half = lax.rem(col, 2)
@@ -155,11 +155,11 @@
 
     @pl.when(lax.div(col, 2) == row)
     def _near():
-        second = right_occupied[1] == 1
+        right_flags = flag_pair(right_own)
+        second = jnp.max(right_flags[1]) == 1.0
         value = product_trace(lambda part: jnp.where(second, one[part, :], own[part, :]), right_own, size)
         flags = [jnp.where(second, a, b) for a, b in zip(flag_pair(one), flag_pair(own))]
-        occupied = (right_occupied[0] + right_occupied[1]).astype(jnp.float32)
-        value = value * jnp.where(half == 1, flags[1], flags[0]) * occupied
+        value = value * jnp.where(half == 1, flags[1], flags[0]) * (right_flags[0] + right_flags[1])
         known = base[0:1, :]
         weight = jnp.sum(jnp.where(lanes == 3 + lax.axis_index("x_hi"), known, 0.0), axis=1, keepdims=True)
         parts[...] += known + jnp.where(lanes == 0, value * weight, 0.0)
@@ -290,7 +290,7 @@
     parts = call(
         trace_kernel,
         "trace",
-        [(right_occupied, SMEM)] + [(a, VMEM) for a in (left_own, left_one, right_here, right_trace, base)],
+        [(a, VMEM) for a in (left_own, left_one, right_here, right_trace, base)],
         jax.ShapeDtypeStruct((lax.axis_size(PLANE), LANES), jnp.float32),
         VMEM,
     )

time: 70.6 us -> 70 us (level)
  no operation moved by 1% of the time
where the time goes in v7:
time: 70 us; the launch traced here: 69.5 us
  starting transfers between devices  34 us (49%)
  blocking collectives  13.4 us (19%)
  waiting for transfers between devices  10.2 us (15%)
  Pallas kernels  8.62 us (12%)
  local copies, waits for them, and re-layouts  2.47 us (4%)
  between operations  0.84 us (1%)
    ppermute x3, starting transfers between devices, shift(): lax.ppermute(value, axis, [(src, (src + steps) % count) for src in range(...  17.7 us
    all_to_all x1, blocking collectives, spread_over(): return lax.all_to_all(rows, axis, 0, 0, tiled=True)  13.4 us
    pallas_call x8, Pallas kernels, call(): pl.pallas_call(kernel, out_shape=outs, in_specs=[spec for _, spec in ins]...  8.62 us
    all_to_all x1, starting transfers between devices, spread_over(): return lax.all_to_all(rows, axis, 0, 0, tiled=True)  8.55 us
    all_to_all x1, waiting for transfers between devices, spread_over(): return lax.all_to_all(rows, axis, 0, 0, tiled=True)  6.72 us
    ppermute x1, starting transfers between devices, local(): right_trace = lax.ppermute(right_own, both, to_trace)  6.32 us
    ppermute x1, waiting for transfers between devices, local(): wanted = lax.ppermute(wanted, both, to_wanted)  3.44 us
    unnamed x14, local copies, waits for them, and re-layouts  2.47 us
  transfers between devices with their start and end apart: 6, of which 2 were waited for; matrix products, arithmetic and copies ran while one was open for 0% of the time, Pallas kernels for 8%

profile of v7, /device:TPU:1, one launch (start us, length us, event | category | flops | bytes accessed | tf_op | source)
XLA Modules:
  0.0 69.5 jit_solution(17272191638887572816)
XLA Ops:
  0.6 0.0 copy-start.1
  0.6 2.6 %pack.1 = (bf16[528,512]{1,0:T(8,128)(2,1)}, bf16[528,512]{1,0:T(8,128)(2,1)}) custom-call(s32[2]{0:T(128)} %bitcast.19, s32[2]{0:T(128)} %bitcast.14, bf16[1024,512]{1,0:T(8,128)(2,1)} %refs_2_.1, bf16[1024,512]{1,0:T(8,128)(2,1)} %refs_3_.1), custom_call_target="tpu_custom_call" | custom-call | tf_op jit(solution)/shard_map/pack/pallas_call | solution.py:19
  3.3 6.3 %collective-permute-start.2 = (bf16[528,512]{1,0:T(8,128)(2,1)}, bf16[528,512]{1,0:T(8,128)(2,1)S(1)}, u32[]{:S(2)}, u32[]{:S(2)}) collective-permute-start(bf16[528,512]{1,0:T(8,128)(2,1)} %get-tuple-element.10.right_own), channel_id=1, source_target_pairs={{32,2},{33,3},{66,36},{67,37},{100,70},{101,71},{134,104},{135,105... | collective-permute-start | bytes 1622024 | tf_op jit(solution)/shard_map/ppermute | solution.py:263
  9.6 0.0 copy-start.4
  9.6 0.0 copy-start.5
  9.6 0.0 copy-start.6
  9.7 8.9 %collective-permute-start = (bf16[528,512]{1,0:T(8,128)(2,1)}, bf16[528,512]{1,0:T(8,128)(2,1)S(1)}, u32[]{:S(2)}, u32[]{:S(2)}) collective-permute-start(bf16[528,512]{1,0:T(8,128)(2,1)} %get-tuple-element.9.own), channel_id=1, source_target_pairs={{0,31},{1,0},{2,1},{3,2},{4,3},{5,4},{6,5},{7,6},{8,7},{9,8},{10,9... | collective-permute-start | bytes 1622024 | tf_op jit(solution)/shard_map/ppermute | solution.py:32
  18.6 0.0 copy-done.1
  18.6 0.0 copy-done.4
  18.6 0.0 copy-done.5
  18.6 0.0 copy-done.6
  18.6 0.0 copy-start.2
  18.6 1.2 %copy-done.2 = bf16[1024,512]{1,0:T(8,128)(2,1)S(1)} copy-done((bf16[1024,512]{1,0:T(8,128)(2,1)S(1)}, bf16[1024,512]{1,0:T(8,128)(2,1)}, u32[]{:S(2)}) %copy-start.2) | copy-done | bytes 1048600
  19.9 1.1 %base.1 = (f32[8,128]{1,0:T(8,128)S(1)}, s32[8,128]{1,0:T(8,128)S(1)}, bf16[528,512]{1,0:T(8,128)(2,1)S(1)}) custom-call(s32[2]{0:T(128)S(1)} %bitcast.15, s32[2]{0:T(128)S(1)} %bitcast.17, s32[2]{0:T(128)S(1)} %copy-done.6, bf16[528,512]{1,0:T(8,128)(2,1)} %get-tuple-element.10.right_own, bf16[1024,512]{1,0:T(8,128)(2,1)S(1)} %copy-done.1, ...), custom_call_target="tpu_custom_call" | custom-call | tf_op jit(solution)/shard_map/base/pallas_call | solution.py:19
  21.0 0.0 copy-start
  21.0 1.4 %collective-permute-start.1 = (s32[8,128]{1,0:T(8,128)S(1)}, s32[8,128]{1,0:T(8,128)S(1)}, u32[]{:S(2)}, u32[]{:S(2)}) collective-permute-start(s32[8,128]{1,0:T(8,128)S(1)} %get-tuple-element.11), channel_id=1, source_target_pairs={{34,4},{35,5},{36,6},{37,7},{38,8},{39,9},{40,10},{41,11},{42,12},... | collective-permute-start | bytes 12296 | tf_op jit(solution)/shard_map/ppermute | solution.py:280
  22.4 4.4 %collective-permute-start.4 = (bf16[528,512]{1,0:T(8,128)(2,1)}, bf16[528,512]{1,0:T(8,128)(2,1)}, u32[]{:S(2)}, u32[]{:S(2)}) collective-permute-start(bf16[528,512]{1,0:T(8,128)(2,1)} %get-tuple-element.10.right_own), channel_id=1, source_target_pairs={{0,480},{32,0},{64,32},{96,64},{128,96},{160,128},{192,160},{224,1... | collective-permute-start | bytes 1622024 | tf_op jit(solution)/shard_map/ppermute | solution.py:32
  26.8 3.4 %collective-permute-done.1.wanted = s32[8,128]{1,0:T(8,128)S(1)} collective-permute-done((s32[8,128]{1,0:T(8,128)S(1)}, s32[8,128]{1,0:T(8,128)S(1)}, u32[]{:S(2)}, u32[]{:S(2)}) %collective-permute-start.1) | collective-permute-done | bytes 4128 | tf_op jit(solution)/shard_map/ppermute | solution.py:280
  30.3 0.0 collective-permute-done.2.right_trace
  30.3 0.0 collective-permute-done.one
  30.3 0.0 copy-done
  30.3 0.2 choose.1
  30.6 4.4 %collective-permute-start.3 = (bf16[528,512]{1,0:T(8,128)(2,1)S(1)}, bf16[528,512]{1,0:T(8,128)(2,1)}, u32[]{:S(2)}, u32[]{:S(2)}) collective-permute-start(bf16[528,512]{1,0:T(8,128)(2,1)S(1)} %choose.1), channel_id=1, source_target_pairs={{0,30},{1,31},{2,0},{3,1},{4,2},{5,3},{6,4},{7,5},{8,6},{9,7},{10,... | collective-permute-start | bytes 1622024 | tf_op jit(solution)/shard_map/ppermute | solution.py:32
  35.0 13.4 %all_to_all.22 = f32[32,1,128]{2,1,0:T(1,128)S(1)} all-to-all(f32[32,1,128]{2,1,0:T(1,128)S(1)} %bitcast.11), channel_id=1, replica_groups=mesh['y'=4,'x_lo'=2,'core'=2,'x_hi'=2,'z'=16] {'y','x_lo','core','x_hi'}, dimensions={0} | all-to-all | bytes 32768 | tf_op jit(solution)/shard_map/all_to_all | solution.py:226
  48.4 0.6 middle.1
  49.0 8.6 %all-to-all-start.1 = ((f32[16,1,128]{2,1,0:T(1,128)}), f32[16,1,128]{2,1,0:T(1,128)S(1)}, u32[]{:S(2)}, u32[]{:S(2)}) async-start(f32[16,1,128]{2,1,0:T(1,128)} %bitcast.7), calls=%async_computation.1 | async-start | bytes 16384 | tf_op jit(solution)/shard_map/all_to_all | solution.py:226
  57.6 0.0 collective-permute-done.4.right_next
  57.6 0.0 collective-permute-done.3.two
  57.6 0.0 copy-start.3
  57.6 1.2 %copy-done.3 = bf16[1024,512]{1,0:T(8,128)(2,1)S(1)} copy-done((bf16[1024,512]{1,0:T(8,128)(2,1)S(1)}, bf16[1024,512]{1,0:T(8,128)(2,1)}, u32[]{:S(2)}) %copy-start.3) | copy-done | bytes 1048600
  58.8 3.3 %last.1 = (bf16[1024,512]{1,0:T(8,128)(2,1)}, f32[8,128]{1,0:T(8,128)S(1)}) custom-call(s32[2]{0:T(128)S(1)} %bitcast.16, s32[2]{0:T(128)S(1)} %bitcast.18, s32[2]{0:T(128)S(1)} %copy-done.6, bf16[528,512]{1,0:T(8,128)(2,1)S(1)} %copy-done, bf16[528,512]{1,0:T(8,128)(2,1)S(1)} %collective-permute-done.one, bf16[528,512]{1,0:T(8,128)(2,1)} %get-tuple-element.10.right_own, ...), custom_call_target="tpu_custom_call" | custom-call | tf_op jit(solution)/shard_map/last/pallas_call | solution.py:19
  62.1 6.7 %all-to-all-done.1 = f32[16,1,128]{2,1,0:T(1,128)S(1)} async-done(((f32[16,1,128]{2,1,0:T(1,128)}), f32[16,1,128]{2,1,0:T(1,128)S(1)}, u32[]{:S(2)}, u32[]{:S(2)}) %all-to-all-start.1) | async-done | bytes 8224 | tf_op jit(solution)/shard_map/all_to_all | solution.py:226
  68.8 0.7 %total.1 = f32[1]{0:T(128)} custom-call(f32[16,128]{1,0:T(8,128)S(1)} %bitcast.13, f32[8,128]{1,0:T(8,128)S(1)} %get-tuple-element.15.stored), custom_call_target="tpu_custom_call" | custom-call | tf_op jit(solution)/shard_map/total/pallas_call | solution.py:19
  (2 shorter events, 0.0 us)
Async XLA Ops:
  0.6 18.0 %copy-start.1 = (bf16[1024,512]{1,0:T(8,128)(2,1)S(1)}, bf16[1024,512]{1,0:T(8,128)(2,1)}, u32[]{:S(2)}) copy-start(bf16[1024,512]{1,0:T(8,128)(2,1)} %earlier.3) | copy-start | bytes 3145732
  3.3 27.0 %collective-permute-start.2 = (bf16[528,512]{1,0:T(8,128)(2,1)}, bf16[528,512]{1,0:T(8,128)(2,1)S(1)}, u32[]{:S(2)}, u32[]{:S(2)}) collective-permute-start(bf16[528,512]{1,0:T(8,128)(2,1)} %get-tuple-element.10.right_own), channel_id=1, source_target_pairs={{32,2},{33,3},{66,36},{67,37},{100,70},{101,71},{134,104},{135,105... | collective-permute-start | bytes 1622024 | tf_op jit(solution)/shard_map/ppermute | solution.py:263
  9.6 9.0 %copy-start.4 = (s32[2,1]{0,1:T(1,128)S(1)}, s32[2,1]{0,1:T(1,128)}, u32[]{:S(2)}) copy-start(s32[2,1]{0,1:T(1,128)} %param.13) | copy-start | bytes 28
  9.6 9.0 %copy-start.5 = (s32[2,1]{0,1:T(1,128)S(1)}, s32[2,1]{0,1:T(1,128)}, u32[]{:S(2)}) copy-start(s32[2,1]{0,1:T(1,128)} %param.14) | copy-start | bytes 28
  9.6 9.0 %copy-start.6 = (s32[2]{0:T(128)S(1)}, s32[2]{0:T(128)}, u32[]{:S(2)}) copy-start(s32[2]{0:T(128)} %branch.3) | copy-start | bytes 28
  9.7 20.6 %collective-permute-start = (bf16[528,512]{1,0:T(8,128)(2,1)}, bf16[528,512]{1,0:T(8,128)(2,1)S(1)}, u32[]{:S(2)}, u32[]{:S(2)}) collective-permute-start(bf16[528,512]{1,0:T(8,128)(2,1)} %get-tuple-element.9.own), channel_id=1, source_target_pairs={{0,31},{1,0},{2,1},{3,2},{4,3},{5,4},{6,5},{7,6},{8,7},{9,8},{10,9... | collective-permute-start | bytes 1622024 | tf_op jit(solution)/shard_map/ppermute | solution.py:32
  18.6 1.2 %copy-start.2 = (bf16[1024,512]{1,0:T(8,128)(2,1)S(1)}, bf16[1024,512]{1,0:T(8,128)(2,1)}, u32[]{:S(2)}) copy-start(bf16[1024,512]{1,0:T(8,128)(2,1)} %density.3) | copy-start | bytes 3145732
  21.0 9.3 %copy-start = (bf16[528,512]{1,0:T(8,128)(2,1)S(1)}, bf16[528,512]{1,0:T(8,128)(2,1)}, u32[]{:S(2)}) copy-start(bf16[528,512]{1,0:T(8,128)(2,1)} %get-tuple-element.9.own) | copy-start | bytes 1622020
  21.0 9.3 %collective-permute-start.1 = (s32[8,128]{1,0:T(8,128)S(1)}, s32[8,128]{1,0:T(8,128)S(1)}, u32[]{:S(2)}, u32[]{:S(2)}) collective-permute-start(s32[8,128]{1,0:T(8,128)S(1)} %get-tuple-element.11), channel_id=1, source_target_pairs={{34,4},{35,5},{36,6},{37,7},{38,8},{39,9},{40,10},{41,11},{42,12},... | collective-permute-start | bytes 12296 | tf_op jit(solution)/shard_map/ppermute | solution.py:280
  22.4 35.2 %collective-permute-start.4 = (bf16[528,512]{1,0:T(8,128)(2,1)}, bf16[528,512]{1,0:T(8,128)(2,1)}, u32[]{:S(2)}, u32[]{:S(2)}) collective-permute-start(bf16[528,512]{1,0:T(8,128)(2,1)} %get-tuple-element.10.right_own), channel_id=1, source_target_pairs={{0,480},{32,0},{64,32},{96,64},{128,96},{160,128},{192,160},{224,1... | collective-permute-start | bytes 1622024 | tf_op jit(solution)/shard_map/ppermute | solution.py:32
  30.6 27.0 %collective-permute-start.3 = (bf16[528,512]{1,0:T(8,128)(2,1)S(1)}, bf16[528,512]{1,0:T(8,128)(2,1)}, u32[]{:S(2)}, u32[]{:S(2)}) collective-permute-start(bf16[528,512]{1,0:T(8,128)(2,1)S(1)} %choose.1), channel_id=1, source_target_pairs={{0,30},{1,31},{2,0},{3,1},{4,2},{5,3},{6,4},{7,5},{8,6},{9,7},{10,... | collective-permute-start | bytes 1622024 | tf_op jit(solution)/shard_map/ppermute | solution.py:32
  49.0 19.8 %all-to-all-start.1 = ((f32[16,1,128]{2,1,0:T(1,128)}), f32[16,1,128]{2,1,0:T(1,128)S(1)}, u32[]{:S(2)}, u32[]{:S(2)}) async-start(f32[16,1,128]{2,1,0:T(1,128)} %bitcast.7), calls=%async_computation.1 | async-start | bytes 16384 | tf_op jit(solution)/shard_map/all_to_all | solution.py:226
  57.6 1.2 %copy-start.3 = (bf16[1024,512]{1,0:T(8,128)(2,1)S(1)}, bf16[1024,512]{1,0:T(8,128)(2,1)}, u32[]{:S(2)}) copy-start(bf16[1024,512]{1,0:T(8,128)(2,1)} %density.3) | copy-start | bytes 3145732

commit v8 on v7

--- a/solution.py
+++ b/solution.py
@@ -61,12 +61,19 @@
         store.wait()
 
 
-def base_kernel(right_occupied, kept, branch, right_own, earlier, density, base, wanted, right_here, earlier_tile, density_tile, sems):
+def wanted_kernel(right_occupied, wanted):
+    wanted[...] = jnp.full(wanted.shape, right_occupied[1], wanted.dtype)
+
+
+def copy_kernel(after, source, copied):
+    copied[...] = source[...]
+
+
+def base_kernel(kept, branch, right_own, earlier, density, base, right_here, earlier_tile, density_tile, sems):
     size = earlier_tile.shape[0]
     row, col = lax.axis_index(ROW), lax.axis_index(COL)
     half = lax.rem(col, 2)
     base[...] = jnp.zeros_like(base)
-    wanted[...] = jnp.full(wanted.shape, right_occupied[1], wanted.dtype)
     right_here[...] = right_own[...]
 
     @pl.when(lax.div(col, 2) == row)
@@ -262,12 +269,12 @@
     ]
     right_trace = lax.ppermute(right_own, both, to_trace)
 
-    base, wanted, right_here = call(
+    base, right_here = call(
         base_kernel,
         "base",
-        [(right_occupied, SMEM), (kept_tiles, SMEM), (branch, SMEM), (right_own, VMEM), (earlier, HBM), (density, HBM)],
-        [jax.ShapeDtypeStruct((8, LANES), jnp.float32), jax.ShapeDtypeStruct((8, LANES), jnp.int32), payload],
-        [VMEM, VMEM, VMEM],
+        [(kept_tiles, SMEM), (branch, SMEM), (right_own, VMEM), (earlier, HBM), (density, HBM)],
+        [jax.ShapeDtypeStruct((8, LANES), jnp.float32), payload],
+        [VMEM, VMEM],
         [pltpu.VMEM((size, size), kind), pltpu.VMEM((size, size), kind), pltpu.SemaphoreType.DMA((2,))],
     )
 
@@ -277,9 +284,13 @@
         for j in range(col_count)
         if j // 2 != i
     ]
+    wanted = call(
+        wanted_kernel, "wanted", [(right_occupied, SMEM)], jax.ShapeDtypeStruct((8, LANES), jnp.int32), VMEM
+    )
     wanted = lax.ppermute(wanted, both, to_wanted)
-    right_next = shift(right_own, ROW, -1)
-
+
+    right_sent = call(copy_kernel, "sent", [(wanted, VMEM), (right_own, VMEM)], payload, VMEM)
+    right_next = shift(right_sent, ROW, -1)
     second = call(
         decide_kernel,
         "decide",

time: 70 us -> 69.9 us (level)
  starting transfers between devices: 34 us -> 29.4 us
  waiting for transfers between devices: 10.2 us -> 11.8 us
  local copies, waits for them, and re-layouts: 2.47 us -> 3.52 us
  blocking collectives: 13.4 us -> 14.4 us
  Pallas kernels: 8.62 us -> 9.39 us
    ppermute x3, waiting for transfers between devices: 0.01 us -> 3.61 us  [shift(): lax.ppermute(value, axis, [(src, (src + steps) % count) for src in range(...]
    all_to_all x1, waiting for transfers between devices: 6.72 us -> 3.29 us  [spread_over(): return lax.all_to_all(rows, axis, 0, 0, tiled=True)]
    all_to_all x1, starting transfers between devices: 8.55 us -> 5.96 us  [spread_over(): return lax.all_to_all(rows, axis, 0, 0, tiled=True)]
    ppermute x3, starting transfers between devices: 17.7 us -> 15.9 us  [shift(): lax.ppermute(value, axis, [(src, (src + steps) % count) for src in range(...]
    ppermute x1, waiting for transfers between devices: 3.44 us -> 4.94 us  [local(): wanted = lax.ppermute(wanted, both, to_wanted)]
    unnamed x14 -> x18, local copies, waits for them, and re-layouts: 2.47 us -> 3.52 us
    all_to_all x1, blocking collectives: 13.4 us -> 14.4 us  [spread_over(): return lax.all_to_all(rows, axis, 0, 0, tiled=True)]
    pallas_call x8 -> x10, Pallas kernels: 8.62 us -> 9.39 us  [call(): pl.pallas_call(kernel, out_shape=outs, in_specs=[spec for _, spec in ins]...]
  transfers between devices with their start and end apart: 6 -> 6, of which waited for: 2 -> 3; matrix products, arithmetic and copies ran while one was open for 0% -> 0% of each run, Pallas kernels for 8% -> 9%
where the time goes in v8:
time: 69.9 us; the launch traced here: 69.4 us
  starting transfers between devices  29.4 us (42%)
  blocking collectives  14.4 us (21%)
  waiting for transfers between devices  11.8 us (17%)
  Pallas kernels  9.39 us (13%)
  local copies, waits for them, and re-layouts  3.52 us (5%)
  between operations  0.85 us (1%)
    ppermute x3, starting transfers between devices, shift(): lax.ppermute(value, axis, [(src, (src + steps) % count) for src in range(...  15.9 us
    all_to_all x1, blocking collectives, spread_over(): return lax.all_to_all(rows, axis, 0, 0, tiled=True)  14.4 us
    pallas_call x10, Pallas kernels, call(): pl.pallas_call(kernel, out_shape=outs, in_specs=[spec for _, spec in ins]...  9.39 us
    ppermute x1, starting transfers between devices, local(): right_trace = lax.ppermute(right_own, both, to_trace)  6.32 us
    all_to_all x1, starting transfers between devices, spread_over(): return lax.all_to_all(rows, axis, 0, 0, tiled=True)  5.96 us
    ppermute x1, waiting for transfers between devices, local(): wanted = lax.ppermute(wanted, both, to_wanted)  4.94 us
    ppermute x3, waiting for transfers between devices, shift(): lax.ppermute(value, axis, [(src, (src + steps) % count) for src in range(...  3.61 us
    unnamed x18, local copies, waits for them, and re-layouts  3.52 us
  transfers between devices with their start and end apart: 6, of which 3 were waited for; matrix products, arithmetic and copies ran while one was open for 0% of the time, Pallas kernels for 9%

profile of v8, /device:TPU:1, one launch (start us, length us, event | category | flops | bytes accessed | tf_op | source)
XLA Modules:
  0.0 69.4 jit_solution(8137006165948195880)
XLA Ops:
  0.6 0.0 copy-start.3
  0.6 2.7 %pack.1 = (bf16[528,512]{1,0:T(8,128)(2,1)}, bf16[528,512]{1,0:T(8,128)(2,1)}) custom-call(s32[2]{0:T(128)} %bitcast.19, s32[2]{0:T(128)} %bitcast.14, bf16[1024,512]{1,0:T(8,128)(2,1)} %refs_2_.1, bf16[1024,512]{1,0:T(8,128)(2,1)} %refs_3_.1), custom_call_target="tpu_custom_call" | custom-call | tf_op jit(solution)/shard_map/pack/pallas_call | solution.py:19
  3.3 0.0 copy-start.6
  3.3 6.3 %collective-permute-start.2 = (bf16[528,512]{1,0:T(8,128)(2,1)}, bf16[528,512]{1,0:T(8,128)(2,1)S(1)}, u32[]{:S(2)}, u32[]{:S(2)}) collective-permute-start(bf16[528,512]{1,0:T(8,128)(2,1)} %get-tuple-element.9.right_own.source), channel_id=1, source_target_pairs={{32,2},{33,3},{66,36},{67,37},{100,70},{101,71},{134,104},{135,105... | collective-permute-start | bytes 1622024 | tf_op jit(solution)/shard_map/ppermute | solution.py:270
  9.6 8.8 %collective-permute-start = (bf16[528,512]{1,0:T(8,128)(2,1)}, bf16[528,512]{1,0:T(8,128)(2,1)S(1)}, u32[]{:S(2)}, u32[]{:S(2)}) collective-permute-start(bf16[528,512]{1,0:T(8,128)(2,1)} %get-tuple-element.8.own), channel_id=1, source_target_pairs={{0,31},{1,0},{2,1},{3,2},{4,3},{5,4},{6,5},{7,6},{8,7},{9,8},{10,9... | collective-permute-start | bytes 1622024 | tf_op jit(solution)/shard_map/ppermute | solution.py:32
  18.4 0.0 copy-done.6
  18.4 0.5 wanted.1
  19.0 0.0 copy-start.7
  19.0 0.0 copy-start.8
  19.0 1.3 %collective-permute-start.1 = (s32[8,128]{1,0:T(8,128)S(1)}, s32[8,128]{1,0:T(8,128)S(1)}, u32[]{:S(2)}, u32[]{:S(2)}) collective-permute-start(s32[8,128]{1,0:T(8,128)S(1)} %wanted.1), channel_id=1, source_target_pairs={{34,4},{35,5},{36,6},{37,7},{38,8},{39,9},{40,10},{41,11},{42,12},... | collective-permute-start | bytes 12296 | tf_op jit(solution)/shard_map/ppermute | solution.py:290
  20.3 0.0 copy-done.3
  20.3 0.0 copy-done.7
  20.3 0.0 copy-done.8
  20.4 0.0 copy-start
  20.4 1.0 %copy-done = bf16[528,512]{1,0:T(8,128)(2,1)S(1)} copy-done((bf16[528,512]{1,0:T(8,128)(2,1)S(1)}, bf16[528,512]{1,0:T(8,128)(2,1)}, u32[]{:S(2)}) %copy-start) | copy-done | bytes 540696
  21.4 0.0 copy-start.4
  21.4 1.2 %copy-done.4 = bf16[1024,512]{1,0:T(8,128)(2,1)S(1)} copy-done((bf16[1024,512]{1,0:T(8,128)(2,1)S(1)}, bf16[1024,512]{1,0:T(8,128)(2,1)}, u32[]{:S(2)}) %copy-start.4) | copy-done | bytes 1048600
  22.6 0.6 base.1
  23.2 4.9 %collective-permute-done.1.wanted.after = s32[8,128]{1,0:T(8,128)S(1)} collective-permute-done((s32[8,128]{1,0:T(8,128)S(1)}, s32[8,128]{1,0:T(8,128)S(1)}, u32[]{:S(2)}, u32[]{:S(2)}) %collective-permute-start.1) | collective-permute-done | bytes 4128 | tf_op jit(solution)/shard_map/ppermute | solution.py:290
  28.2 0.9 %sent.1 = bf16[528,512]{1,0:T(8,128)(2,1)} custom-call(s32[8,128]{1,0:T(8,128)S(1)} %collective-permute-done.1.wanted.after, bf16[528,512]{1,0:T(8,128)(2,1)S(1)} %copy-done), custom_call_target="tpu_custom_call" | custom-call | tf_op jit(solution)/shard_map/sent/pallas_call | solution.py:19
  29.0 0.0 copy-start.2
  29.0 4.0 %collective-permute-start.4 = (bf16[528,512]{1,0:T(8,128)(2,1)}, bf16[528,512]{1,0:T(8,128)(2,1)}, u32[]{:S(2)}, u32[]{:S(2)}) collective-permute-start(bf16[528,512]{1,0:T(8,128)(2,1)} %sent.1), channel_id=1, source_target_pairs={{0,480},{32,0},{64,32},{96,64},{128,96},{160,128},{192,160},{224,1... | collective-permute-start | bytes 1622024 | tf_op jit(solution)/shard_map/ppermute | solution.py:32
  33.0 0.0 collective-permute-done.2.right_trace
  33.1 0.0 collective-permute-done.one
  33.1 0.0 copy-done.2
  33.2 0.0 copy-start.1
  33.2 0.2 choose.1
  33.4 3.1 %collective-permute-start.3 = (bf16[528,512]{1,0:T(8,128)(2,1)S(1)}, bf16[528,512]{1,0:T(8,128)(2,1)}, u32[]{:S(2)}, u32[]{:S(2)}) collective-permute-start(bf16[528,512]{1,0:T(8,128)(2,1)S(1)} %choose.1), channel_id=1, source_target_pairs={{0,30},{1,31},{2,0},{3,1},{4,2},{5,3},{6,4},{7,5},{8,6},{9,7},{10,... | collective-permute-start | bytes 1622024 | tf_op jit(solution)/shard_map/ppermute | solution.py:32
  36.5 14.4 %all_to_all.22 = f32[32,1,128]{2,1,0:T(1,128)S(1)} all-to-all(f32[32,1,128]{2,1,0:T(1,128)S(1)} %bitcast.11), channel_id=1, replica_groups=mesh['y'=4,'x_lo'=2,'core'=2,'x_hi'=2,'z'=16] {'y','x_lo','core','x_hi'}, dimensions={0} | all-to-all | bytes 32768 | tf_op jit(solution)/shard_map/all_to_all | solution.py:233
  50.9 0.6 middle.1
  51.5 6.0 %all-to-all-start.1 = ((f32[16,1,128]{2,1,0:T(1,128)}), f32[16,1,128]{2,1,0:T(1,128)S(1)}, u32[]{:S(2)}, u32[]{:S(2)}) async-start(f32[16,1,128]{2,1,0:T(1,128)} %bitcast.7), calls=%async_computation.1 | async-start | bytes 16384 | tf_op jit(solution)/shard_map/all_to_all | solution.py:233
  57.4 0.0 collective-permute-done.4.right_next
  57.5 3.6 %collective-permute-done.3.two = bf16[528,512]{1,0:T(8,128)(2,1)} collective-permute-done((bf16[528,512]{1,0:T(8,128)(2,1)S(1)}, bf16[528,512]{1,0:T(8,128)(2,1)}, u32[]{:S(2)}, u32[]{:S(2)}) %collective-permute-start.3) | collective-permute-done | bytes 540704 | tf_op jit(solution)/shard_map/ppermute | solution.py:32
  61.1 0.0 copy-done.1
  61.1 0.0 copy-start.5
  61.1 1.2 %copy-done.5 = bf16[1024,512]{1,0:T(8,128)(2,1)S(1)} copy-done((bf16[1024,512]{1,0:T(8,128)(2,1)S(1)}, bf16[1024,512]{1,0:T(8,128)(2,1)}, u32[]{:S(2)}) %copy-start.5) | copy-done | bytes 1048600
  62.3 3.1 %last.1 = (bf16[1024,512]{1,0:T(8,128)(2,1)}, f32[8,128]{1,0:T(8,128)S(1)}) custom-call(s32[2]{0:T(128)S(1)} %bitcast.16, s32[2]{0:T(128)S(1)} %bitcast.18, s32[2]{0:T(128)S(1)} %copy-done.8, bf16[528,512]{1,0:T(8,128)(2,1)S(1)} %copy-done.2, bf16[528,512]{1,0:T(8,128)(2,1)S(1)} %collective-permute-done.one, bf16[528,512]{1,0:T(8,128)(2,1)S(1)} %copy-done.1, ...), custom_call_target="tpu_custom_call" | custom-call | tf_op jit(solution)/shard_map/last/pallas_call | solution.py:19
  65.4 3.3 %all-to-all-done.1 = f32[16,1,128]{2,1,0:T(1,128)S(1)} async-done(((f32[16,1,128]{2,1,0:T(1,128)}), f32[16,1,128]{2,1,0:T(1,128)S(1)}, u32[]{:S(2)}, u32[]{:S(2)}) %all-to-all-start.1) | async-done | bytes 8224 | tf_op jit(solution)/shard_map/all_to_all | solution.py:233
  68.7 0.7 %total.1 = f32[1]{0:T(128)} custom-call(f32[16,128]{1,0:T(8,128)S(1)} %bitcast.13, f32[8,128]{1,0:T(8,128)S(1)} %get-tuple-element.13.stored), custom_call_target="tpu_custom_call" | custom-call | tf_op jit(solution)/shard_map/total/pallas_call | solution.py:19
  (2 shorter events, 0.1 us)
Async XLA Ops:
  0.6 19.7 %copy-start.3 = (bf16[1024,512]{1,0:T(8,128)(2,1)S(1)}, bf16[1024,512]{1,0:T(8,128)(2,1)}, u32[]{:S(2)}) copy-start(bf16[1024,512]{1,0:T(8,128)(2,1)} %earlier.3) | copy-start | bytes 3145732
  3.3 15.1 %copy-start.6 = (s32[2,1]{0,1:T(1,128)S(1)}, s32[2,1]{0,1:T(1,128)}, u32[]{:S(2)}) copy-start(s32[2,1]{0,1:T(1,128)} %param.13) | copy-start | bytes 28
  3.3 29.7 %collective-permute-start.2 = (bf16[528,512]{1,0:T(8,128)(2,1)}, bf16[528,512]{1,0:T(8,128)(2,1)S(1)}, u32[]{:S(2)}, u32[]{:S(2)}) collective-permute-start(bf16[528,512]{1,0:T(8,128)(2,1)} %get-tuple-element.9.right_own.source), channel_id=1, source_target_pairs={{32,2},{33,3},{66,36},{67,37},{100,70},{101,71},{134,104},{135,105... | collective-permute-start | bytes 1622024 | tf_op jit(solution)/shard_map/ppermute | solution.py:270
  9.6 23.5 %collective-permute-start = (bf16[528,512]{1,0:T(8,128)(2,1)}, bf16[528,512]{1,0:T(8,128)(2,1)S(1)}, u32[]{:S(2)}, u32[]{:S(2)}) collective-permute-start(bf16[528,512]{1,0:T(8,128)(2,1)} %get-tuple-element.8.own), channel_id=1, source_target_pairs={{0,31},{1,0},{2,1},{3,2},{4,3},{5,4},{6,5},{7,6},{8,7},{9,8},{10,9... | collective-permute-start | bytes 1622024 | tf_op jit(solution)/shard_map/ppermute | solution.py:32
  19.0 1.3 %copy-start.7 = (s32[2,1]{0,1:T(1,128)S(1)}, s32[2,1]{0,1:T(1,128)}, u32[]{:S(2)}) copy-start(s32[2,1]{0,1:T(1,128)} %param.14) | copy-start | bytes 28
  19.0 1.3 %copy-start.8 = (s32[2]{0:T(128)S(1)}, s32[2]{0:T(128)}, u32[]{:S(2)}) copy-start(s32[2]{0:T(128)} %branch.3) | copy-start | bytes 28
  19.0 9.1 %collective-permute-start.1 = (s32[8,128]{1,0:T(8,128)S(1)}, s32[8,128]{1,0:T(8,128)S(1)}, u32[]{:S(2)}, u32[]{:S(2)}) collective-permute-start(s32[8,128]{1,0:T(8,128)S(1)} %wanted.1), channel_id=1, source_target_pairs={{34,4},{35,5},{36,6},{37,7},{38,8},{39,9},{40,10},{41,11},{42,12},... | collective-permute-start | bytes 12296 | tf_op jit(solution)/shard_map/ppermute | solution.py:290
  20.4 1.0 %copy-start = (bf16[528,512]{1,0:T(8,128)(2,1)S(1)}, bf16[528,512]{1,0:T(8,128)(2,1)}, u32[]{:S(2)}) copy-start(bf16[528,512]{1,0:T(8,128)(2,1)} %get-tuple-element.9.right_own.source) | copy-start | bytes 1622020
  21.4 1.2 %copy-start.4 = (bf16[1024,512]{1,0:T(8,128)(2,1)S(1)}, bf16[1024,512]{1,0:T(8,128)(2,1)}, u32[]{:S(2)}) copy-start(bf16[1024,512]{1,0:T(8,128)(2,1)} %density.3) | copy-start | bytes 3145732
  29.0 4.1 %copy-start.2 = (bf16[528,512]{1,0:T(8,128)(2,1)S(1)}, bf16[528,512]{1,0:T(8,128)(2,1)}, u32[]{:S(2)}) copy-start(bf16[528,512]{1,0:T(8,128)(2,1)} %get-tuple-element.8.own) | copy-start | bytes 1622020
  29.0 28.4 %collective-permute-start.4 = (bf16[528,512]{1,0:T(8,128)(2,1)}, bf16[528,512]{1,0:T(8,128)(2,1)}, u32[]{:S(2)}, u32[]{:S(2)}) collective-permute-start(bf16[528,512]{1,0:T(8,128)(2,1)} %sent.1), channel_id=1, source_target_pairs={{0,480},{32,0},{64,32},{96,64},{128,96},{160,128},{192,160},{224,1... | collective-permute-start | bytes 1622024 | tf_op jit(solution)/shard_map/ppermute | solution.py:32
  33.2 27.9 %copy-start.1 = (bf16[528,512]{1,0:T(8,128)(2,1)S(1)}, bf16[528,512]{1,0:T(8,128)(2,1)}, u32[]{:S(2)}) copy-start(bf16[528,512]{1,0:T(8,128)(2,1)} %get-tuple-element.9.right_own.source) | copy-start | bytes 1622020
  33.4 27.6 %collective-permute-start.3 = (bf16[528,512]{1,0:T(8,128)(2,1)S(1)}, bf16[528,512]{1,0:T(8,128)(2,1)}, u32[]{:S(2)}, u32[]{:S(2)}) collective-permute-start(bf16[528,512]{1,0:T(8,128)(2,1)S(1)} %choose.1), channel_id=1, source_target_pairs={{0,30},{1,31},{2,0},{3,1},{4,2},{5,3},{6,4},{7,5},{8,6},{9,7},{10,... | collective-permute-start | bytes 1622024 | tf_op jit(solution)/shard_map/ppermute | solution.py:32
  51.5 17.2 %all-to-all-start.1 = ((f32[16,1,128]{2,1,0:T(1,128)}), f32[16,1,128]{2,1,0:T(1,128)S(1)}, u32[]{:S(2)}, u32[]{:S(2)}) async-start(f32[16,1,128]{2,1,0:T(1,128)} %bitcast.7), calls=%async_computation.1 | async-start | bytes 16384 | tf_op jit(solution)/shard_map/all_to_all | solution.py:233
  61.1 1.2 %copy-start.5 = (bf16[1024,512]{1,0:T(8,128)(2,1)S(1)}, bf16[1024,512]{1,0:T(8,128)(2,1)}, u32[]{:S(2)}) copy-start(bf16[1024,512]{1,0:T(8,128)(2,1)} %density.3) | copy-start | bytes 3145732
